TPU v7x, 256 devices: a whole 4x4x8 slice. The times are simulated.
256 devices in a mesh: row: 16 (over y, x), col: 16 (over z, core).
Axes of the slice: x: 4, y: 4, z: 8, core: 2. Of those that a mesh axis runs over, the one named last changes fastest.
Arguments:
- hist_corr: float32 [16384, 16384], P('row', 'col'), may hold values from -1 to 1
- hist_resp: float32 [16384, 16384], P('row', 'col'), may hold values from -1 to 1, as said below
- row_corr: float32 [128, 16384], P(None, 'col'), may hold values from -1 to 1
- row_resp: float32 [128, 16384], P(None, 'col'), may hold values from -1 to 1
Outputs:
- final_corr: float32 [128, 16384], P(None, 'col')
- final_resp: float32 [128, 16384], P(None, 'col')
Inputs may be any that keep to these rules, and one draw needn't show every extreme that they name: hist_resp[s, u] is 0 where u > s and 1 where u == s.
All inputs are finite; a program needn't handle non-finite values.
Results may differ from a plain program's by a relative error of at most 0.00015.
Values sent between devices are 32-bit elements; how exact they have to be, the bound alone decides.
No kernel may reach another device: no remote copies, remote signals or barrier semaphores. Data moves between devices by JAX's collectives and lax.ppermute only.
A program may use at most 64 MiB of HBM per device.

v0:
```python
import math

import jax
import jax.numpy as jnp
from jax import lax
from jax.sharding import PartitionSpec as P

HIST = 16384
BLOCKS = 4


step_size = 0.2
heat_reservoir_warmth = 0.6


def from_root(block, axis, source):
    block = jnp.where(lax.axis_index(axis) == source, block, jnp.zeros_like(block))
    return lax.psum(block, axis)


def to_rows(values):
    row_count = lax.axis_size("row")
    col_count = lax.axis_size("col")
    my_row = lax.axis_index("row")
    factor = max(col_count // row_count, 1)
    shrink = max(row_count // col_count, 1)
    source = my_row // shrink * factor + 0
    pieces = from_root(values, "col", source)
    return pieces


def to_cols(values):
    row_count = lax.axis_size("row")
    col_count = lax.axis_size("col")
    my_col = lax.axis_index("col")
    factor = max(row_count // col_count, 1)
    shrink = max(col_count // row_count, 1)
    source = my_col // shrink * factor + 0
    pieces = from_root(values, "row", source)
    return pieces


def energy_layout(values):
    return to_rows(values)


def cross_layout(values):
    return to_cols(values)


def advance(
    autocovariance_curve,
    perturbation_reaction,
    memory_corr,
    memory_resp,
    cross_term,
    norm_enforcing_scalar,
    integration_coefficient,
):
    next_corr = autocovariance_curve + step_size * (
        integration_coefficient * (memory_corr + cross_term)
        - norm_enforcing_scalar * autocovariance_curve
    )
    next_resp = perturbation_reaction + step_size * (
        integration_coefficient * memory_resp - norm_enforcing_scalar * perturbation_reaction
    )
    return (next_corr, next_resp)


def body(hist_corr, hist_resp, row_corr, row_resp):
    highest = lax.Precision.HIGHEST
    integration_coefficient = 1.0 / math.sqrt(HIST)
    autocovariance_curve = row_corr
    perturbation_reaction = row_resp
    for block_index in range(BLOCKS):
        history_integrand = 3.0 * autocovariance_curve * perturbation_reaction
        slope_contribution = 1.5 * autocovariance_curve * autocovariance_curve
        multiplier_terms = jnp.sum(
            history_integrand * autocovariance_curve + slope_contribution * perturbation_reaction,
            axis=1,
        )
        part_cross = lax.dot_general(
            slope_contribution,
            hist_resp,
            (((1,), (1,)), ((), ())),
            precision=highest,
            preferred_element_type=jnp.float32,
        )
        enforcing_scalar_sum = lax.psum(multiplier_terms, "col")
        energy_rows = energy_layout(history_integrand)
        cross_total = lax.psum(part_cross, "col")
        cross_term = cross_layout(cross_total)
        norm_enforcing_scalar = (
            heat_reservoir_warmth + integration_coefficient * enforcing_scalar_sum[:, None]
        )
        part_corr = jnp.dot(
            energy_rows, hist_corr, precision=highest, preferred_element_type=jnp.float32
        )
        part_resp = jnp.dot(
            energy_rows, hist_resp, precision=highest, preferred_element_type=jnp.float32
        )
        memory_corr, memory_resp = lax.psum((part_corr, part_resp), "row")
        autocovariance_curve, perturbation_reaction = advance(
            autocovariance_curve,
            perturbation_reaction,
            memory_corr,
            memory_resp,
            cross_term,
            norm_enforcing_scalar,
            integration_coefficient,
        )
    return (autocovariance_curve, perturbation_reaction)


def solution(mesh):
    in_specs = (P("row", "col"), P("row", "col"), P(None, "col"), P(None, "col"))
    out_specs = (P(None, "col"), P(None, "col"))
    return jax.shard_map(body, mesh=mesh, in_specs=in_specs, out_specs=out_specs, check_vma=False)
```

profile of v0, /device:TPU:1, one launch (start us, length us, event | category | flops | bytes accessed | tf_op | source)
XLA Modules:
  0.0 927.8 jit_solution(6894575853050435657)
XLA Ops:
  7.2 0.0 copy-start.4
  7.2 0.0 copy-start.9
  7.2 0.0 all-reduce.23.cloned.1.call-start
  7.2 7.5 fusion.4
  14.7 0.0 copy-done.4
  14.7 0.0 copy-done.9
  14.7 0.9 fusion.3
  15.6 0.0 all-reduce.23.cloned.1.call-update
  15.7 0.0 all-reduce.31.cloned.1.call-start
  15.7 115.4 %all-reduce.23.cloned.1.call-done = (f32[128,1024]{1,0:T(8,128)}, f32[128,1024]{1,0:T(8,128)}) async-done(((f32[128,1024]{1,0:T(8,128)}, f32[128,1024]{1,0:T(8,128)}), (f32[128,1024]{1,0:T(8,128)}, f32[128,1024]{1,0:T(8,128)})) %all-reduce.23.cloned.1.call-update) | async-done | bytes 1048592 | tf_op jit(solution)/shard_map/psum | solution.py:18
  131.1 5.7 fusion.16
  136.8 0.0 copy-done
  136.8 0.0 copy-done.5
  136.8 0.0 copy-done.10
  136.8 3.2 convolution_add_fusion.3
  140.0 0.0 all-reduce.31.cloned.1.call-update
  140.1 0.0 all-reduce.21.cloned.1.call-start
  140.1 24.0 %psum.172 = f32[128]{0:T(128)S(1)} all-reduce(f32[128]{0:T(128)S(1)} %get-tuple-element.28), channel_id=1, replica_groups=mesh['row'=16,'col'=16] {'col'}, use_global_device_ids=true, to_apply=%region_5.6 | all-reduce | flops 128 | bytes 1024 | tf_op jit(solution)/shard_map/psum | solution.py:89
  164.1 72.2 %all-reduce.31.cloned.1.call-done = (f32[128,1024]{1,0:T(8,128)}, f32[128,1024]{1,0:T(8,128)}) async-done(((f32[128,1024]{1,0:T(8,128)}, f32[128,1024]{1,0:T(8,128)}), (f32[128,1024]{1,0:T(8,128)}, f32[128,1024]{1,0:T(8,128)})) %all-reduce.31.cloned.1.call-update) | async-done | bytes 1048592 | tf_op jit(solution)/shard_map/psum | solution.py:102
  236.3 1.6 add_reduce_fusion.2
  238.0 7.2 fusion.5
  245.2 0.9 fusion.2
  246.1 0.0 all-reduce.21.cloned.1.call-update
  246.1 0.0 all-reduce.29.cloned.1.call-start
  246.1 112.4 %all-reduce.21.cloned.1.call-done = (f32[128,1024]{1,0:T(8,128)}, f32[128,1024]{1,0:T(8,128)}) async-done(((f32[128,1024]{1,0:T(8,128)}, f32[128,1024]{1,0:T(8,128)}), (f32[128,1024]{1,0:T(8,128)}, f32[128,1024]{1,0:T(8,128)})) %all-reduce.21.cloned.1.call-update) | async-done | bytes 1048592 | tf_op jit(solution)/shard_map/psum | solution.py:18
  358.5 5.7 fusion.17
  364.2 0.0 copy-done.1
  364.2 0.0 copy-done.7
  364.2 0.0 copy-done.12
  364.2 3.2 convolution_add_fusion.2
  367.4 0.0 all-reduce.29.cloned.1.call-update
  367.4 0.0 all-reduce.19.cloned.1.call-start
  367.5 24.0 %psum.178 = f32[128]{0:T(128)S(1)} all-reduce(f32[128]{0:T(128)S(1)} %get-tuple-element.24), channel_id=1, replica_groups=mesh['row'=16,'col'=16] {'col'}, use_global_device_ids=true, to_apply=%region_12.13 | all-reduce | flops 128 | bytes 1024 | tf_op jit(solution)/shard_map/psum | solution.py:89
  391.5 72.2 %all-reduce.29.cloned.1.call-done = (f32[128,1024]{1,0:T(8,128)}, f32[128,1024]{1,0:T(8,128)}) async-done(((f32[128,1024]{1,0:T(8,128)}, f32[128,1024]{1,0:T(8,128)}), (f32[128,1024]{1,0:T(8,128)}, f32[128,1024]{1,0:T(8,128)})) %all-reduce.29.cloned.1.call-update) | async-done | bytes 1048592 | tf_op jit(solution)/shard_map/psum | solution.py:102
  463.7 1.6 add_reduce_fusion.1
  465.4 7.2 fusion.6
  472.6 0.9 fusion.1
  473.5 0.0 all-reduce.19.cloned.1.call-update
  473.5 0.0 all-reduce.27.cloned.1.call-start
  473.5 112.4 %all-reduce.19.cloned.1.call-done = (f32[128,1024]{1,0:T(8,128)}, f32[128,1024]{1,0:T(8,128)}) async-done(((f32[128,1024]{1,0:T(8,128)}, f32[128,1024]{1,0:T(8,128)}), (f32[128,1024]{1,0:T(8,128)}, f32[128,1024]{1,0:T(8,128)})) %all-reduce.19.cloned.1.call-update) | async-done | bytes 1048592 | tf_op jit(solution)/shard_map/psum | solution.py:18
  585.9 5.7 fusion.18
  591.6 0.0 copy-done.2
  591.6 0.0 copy-done.8
  591.6 0.0 copy-done.13
  591.6 3.2 convolution_add_fusion.1
  594.8 0.0 all-reduce.27.cloned.1.call-update
  594.9 0.0 all-reduce.17.cloned.1.call-start
  594.9 24.0 %psum.184 = f32[128]{0:T(128)S(1)} all-reduce(f32[128]{0:T(128)S(1)} %get-tuple-element.21), channel_id=1, replica_groups=mesh['row'=16,'col'=16] {'col'}, use_global_device_ids=true, to_apply=%region_19.20 | all-reduce | flops 128 | bytes 1024 | tf_op jit(solution)/shard_map/psum | solution.py:89
  619.0 72.2 %all-reduce.27.cloned.1.call-done = (f32[128,1024]{1,0:T(8,128)}, f32[128,1024]{1,0:T(8,128)}) async-done(((f32[128,1024]{1,0:T(8,128)}, f32[128,1024]{1,0:T(8,128)}), (f32[128,1024]{1,0:T(8,128)}, f32[128,1024]{1,0:T(8,128)})) %all-reduce.27.cloned.1.call-update) | async-done | bytes 1048592 | tf_op jit(solution)/shard_map/psum | solution.py:102
  691.1 1.6 add_reduce_fusion
  692.8 7.2 fusion.7
  700.0 0.9 fusion
  700.9 0.0 all-reduce.17.cloned.1.call-update
  700.9 0.0 all-reduce.25.cloned.1.call-start
  700.9 112.4 %all-reduce.17.cloned.1.call-done = (f32[128,1024]{1,0:T(8,128)}, f32[128,1024]{1,0:T(8,128)}) async-done(((f32[128,1024]{1,0:T(8,128)}, f32[128,1024]{1,0:T(8,128)}), (f32[128,1024]{1,0:T(8,128)}, f32[128,1024]{1,0:T(8,128)})) %all-reduce.17.cloned.1.call-update) | async-done | bytes 1048592 | tf_op jit(solution)/shard_map/psum | solution.py:18
  813.3 5.7 fusion.19
  819.0 0.0 copy-done.3
  819.0 0.0 copy-done.6
  819.0 0.0 copy-done.11
  819.0 3.2 convolution_add_fusion
  822.2 0.0 all-reduce.25.cloned.1.call-update
  822.2 23.8 %psum.190 = f32[128]{0:T(128)S(1)} all-reduce(f32[128]{0:T(128)S(1)} %get-tuple-element.18), channel_id=1, replica_groups=mesh['row'=16,'col'=16] {'col'}, use_global_device_ids=true, to_apply=%region_26.27 | all-reduce | flops 128 | bytes 1024 | tf_op jit(solution)/shard_map/psum | solution.py:89
  846.0 72.5 %all-reduce.25.cloned.1.call-done = (f32[128,1024]{1,0:T(8,128)}, f32[128,1024]{1,0:T(8,128)}) async-done(((f32[128,1024]{1,0:T(8,128)}, f32[128,1024]{1,0:T(8,128)}), (f32[128,1024]{1,0:T(8,128)}, f32[128,1024]{1,0:T(8,128)})) %all-reduce.25.cloned.1.call-update) | async-done | bytes 1048592 | tf_op jit(solution)/shard_map/psum | solution.py:102
  918.5 2.4 multiply_add_fusion
  (16 shorter events, 0.0 us)
Async XLA Ops:
  7.2 7.5 copy-start.4
  7.2 7.5 copy-start.9
  7.2 124.0 %all-reduce.23.cloned.1.call-start = ((), (), s32[]{:S(2)}) async-start(), calls=%async_computation.3 | async-start | bytes 2097152 | tf_op jit(solution)/shard_map/psum | solution.py:18
  15.7 220.7 %all-reduce.31.cloned.1.call-start = ((), (), s32[]{:S(2)}) async-start(), calls=%async_computation.7 | async-start | bytes 2097152 | tf_op jit(solution)/shard_map/psum | solution.py:102
  131.1 5.7 copy-start
  131.1 5.7 copy-start.5
  131.1 5.7 copy-start.10
  140.1 218.4 %all-reduce.21.cloned.1.call-start = ((), (), s32[]{:S(2)}) async-start(), calls=%async_computation.2 | async-start | bytes 2097152 | tf_op jit(solution)/shard_map/psum | solution.py:18
  246.1 217.7 %all-reduce.29.cloned.1.call-start = ((), (), s32[]{:S(2)}) async-start(), calls=%async_computation.6 | async-start | bytes 2097152 | tf_op jit(solution)/shard_map/psum | solution.py:102
  358.5 5.7 copy-start.1
  358.5 5.7 copy-start.7
  358.5 5.7 copy-start.12
  367.4 218.5 %all-reduce.19.cloned.1.call-start = ((), (), s32[]{:S(2)}) async-start(), calls=%async_computation.1 | async-start | bytes 2097152 | tf_op jit(solution)/shard_map/psum | solution.py:18
  473.5 217.6 %all-reduce.27.cloned.1.call-start = ((), (), s32[]{:S(2)}) async-start(), calls=%async_computation.5 | async-start | bytes 2097152 | tf_op jit(solution)/shard_map/psum | solution.py:102
  585.9 5.7 copy-start.2
  585.9 5.7 copy-start.8
  585.9 5.7 copy-start.13
  594.9 218.4 %all-reduce.17.cloned.1.call-start = ((), (), s32[]{:S(2)}) async-start(), calls=%async_computation | async-start | bytes 2097152 | tf_op jit(solution)/shard_map/psum | solution.py:18
  700.9 217.6 %all-reduce.25.cloned.1.call-start = ((), (), s32[]{:S(2)}) async-start(), calls=%async_computation.4 | async-start | bytes 2097152 | tf_op jit(solution)/shard_map/psum | solution.py:102
  813.3 5.7 copy-start.3
  813.3 5.7 copy-start.6
  813.3 5.7 copy-start.11
Sparse Core Ops, SparseCore 0:
  15.8 115.3 all-reduce.22
  140.2 96.0 all-reduce.30
  246.2 112.2 all-reduce.20
  367.6 96.1 all-reduce.28
  473.6 112.2 all-reduce.18
  595.0 96.0 all-reduce.26
  701.0 112.2 all-reduce.16
  822.4 96.1 all-reduce.24
where the time goes:
time: 928 us
  waiting for transfers between devices  742 us (80%)
  blocking collectives  95.8 us (10%)
  matrix products  64.7 us (7%)
  between operations  14.2 us (2%)
  other arithmetic  10.9 us (1%)
    psum x4, waiting for transfers between devices, from_root(): return lax.psum(block, axis)  453 us
    psum x4, waiting for transfers between devices, body(): memory_corr, memory_resp = lax.psum((part_corr, part_resp), 'row')  289 us
    psum x4, blocking collectives, body(): enforcing_scalar_sum = lax.psum(multiplier_terms, 'col')  95.8 us
    dot_general x4, matrix products, body(): lax.dot_general(slope_contribution, hist_resp, (((1,), (1,)), ((), ())),...  29.1 us
    dot_general x4, matrix products, body(): jnp.dot(energy_rows, hist_resp, precision=highest, preferred_element_type...  22.7 us
  transfers between devices with their start and end apart: 8, of which 8 were waited for; matrix products, arithmetic and copies ran while one was open for 0% of the time, Pallas kernels for 0%

commit v1 on v0

v1 whole, which is shorter than its diff:
```python
import functools
import math

import jax
import jax.numpy as jnp
from jax import lax
from jax.experimental import pallas as pl
from jax.experimental.pallas import tpu as pltpu
from jax.sharding import Mesh
from jax.sharding import PartitionSpec as P

HIST = 16384
BLOCKS = 4
SIDE = 16
SLICE = 8
ROWS = SIDE * SLICE
WIDTH = 1024
LANES = 128
TILE = 256
COEFFICIENT = 1.0 / math.sqrt(HIST)

step_size = 0.2
heat_reservoir_warmth = 0.6

ROW = ("y", "x")
ALL = ("y", "x", "z", "core")
TRANSPOSE = [(r * SIDE + c, c * SIDE + r) for r in range(SIDE) for c in range(SIDE)]

f32, bf16 = jnp.float32, jnp.bfloat16


def kernel_call(body, outs, args, scratch=(), flops=0, prefetch=0):
    vmem = pl.BlockSpec(memory_space=pltpu.VMEM)
    smem = pl.BlockSpec(memory_space=pltpu.SMEM)
    size = sum(a.size * a.dtype.itemsize for a in args)
    return pl.pallas_call(
        body,
        out_shape=outs,
        in_specs=[smem] * prefetch + [vmem] * (len(args) - prefetch),
        out_specs=jax.tree.map(lambda _: vmem, outs),
        scratch_shapes=list(scratch),
        compiler_params=pltpu.CompilerParams(vmem_limit_bytes=40 * 1024 * 1024),
        cost_estimate=pl.CostEstimate(flops=flops, bytes_accessed=size, transcendentals=0),
    )(*args)


def shape(*dims, dtype=f32):
    return jax.ShapeDtypeStruct(dims, dtype)


def split(values):
    high = values.astype(bf16)
    low = (values - high.astype(f32)).astype(bf16)
    return high, low


def split_kernel(corr_ref, resp_ref, ch_ref, cl_ref, rh_ref, rl_ref):
    @pl.loop(0, WIDTH // LANES)
    def _(i):
        rows = pl.ds(pl.multiple_of(i * LANES, LANES), LANES)
        ch_ref[rows, :], cl_ref[rows, :] = split(corr_ref[rows, :])
        rh_ref[rows, :], rl_ref[rows, :] = split(resp_ref[rows, :])


def split_history(hist_corr, hist_resp):
    out = shape(WIDTH, WIDTH, dtype=bf16)
    return kernel_call(split_kernel, (out,) * 4, (hist_corr, hist_resp), flops=WIDTH * WIDTH)


def cross_kernel(col_ref, full_ref, rh_ref, rl_ref, keep_ref, give_ref, lhs_ref):
    col = col_ref[0]
    full = full_ref[...].reshape(ROWS, WIDTH)
    lhs_ref[:ROWS], lhs_ref[ROWS:] = split(1.5 * full * full)
    dims = (((1,), (1,)), ((), ()))

    @pl.loop(0, WIDTH // TILE)
    def _(n):
        at = pl.ds(pl.multiple_of(n * TILE, TILE), TILE)
        both = lax.dot_general(lhs_ref[...], rh_ref[at, :], dims, preferred_element_type=f32)
        low = lax.dot_general(lhs_ref[:ROWS], rl_ref[at, :], dims, preferred_element_type=f32)
        total = (both[:ROWS] + (both[ROWS:] + low)).reshape(SIDE, SLICE, TILE)
        for j in range(SIDE):
            slot = j ^ col
            half = slot // 2

            @pl.when(slot % 2 == 0)
            def _():
                keep_ref[half, :, at] = total[j]

            @pl.when(slot % 2 == 1)
            def _():
                give_ref[half, :, at] = total[j]


def cross_parts(col, full, resp_high, resp_low):
    out = shape(SIDE // 2, SLICE, WIDTH)
    return kernel_call(
        cross_kernel,
        (out, out),
        (col, full, resp_high, resp_low),
        scratch=(pltpu.VMEM((2 * ROWS, WIDTH), bf16),),
        flops=6 * ROWS * WIDTH * WIDTH,
        prefetch=1,
    )


def memory_kernel(
    core_ref, mine_ref, other_ref, ch_ref, cl_ref, rh_ref, rl_ref, out_ref, lhs_ref
):
    core = core_ref[0]
    half = ROWS // 2
    for k, ref in enumerate((mine_ref, other_ref)):
        values = ref[:, :, :WIDTH].reshape(half, WIDTH)
        at = pl.ds(k * half, half)
        high, low = split(values)
        lhs_ref[k * half : (k + 1) * half] = high
        lhs_ref[ROWS + k * half : ROWS + (k + 1) * half] = low
        for z in range(SIDE // 2):
            out_ref[2 * z + (core + k) % 2, :, 2 * WIDTH :] = ref[z, :, WIDTH:]
    for first, high_ref, low_ref in ((0, ch_ref, cl_ref), (WIDTH, rh_ref, rl_ref)):

        @pl.loop(0, WIDTH // TILE)
        def _(n):
            at = pl.ds(pl.multiple_of(n * TILE, TILE), TILE)
            to = pl.ds(pl.multiple_of(first + n * TILE, TILE), TILE)
            both = jnp.dot(lhs_ref[...], high_ref[:, at], preferred_element_type=f32)
            low = jnp.dot(lhs_ref[:ROWS], low_ref[:, at], preferred_element_type=f32)
            total = (both[:ROWS] + (both[ROWS:] + low)).reshape(2, SIDE // 2, SLICE, TILE)
            for k in range(2):
                for z in range(SIDE // 2):
                    out_ref[2 * z + (core + k) % 2, :, to] = total[k, z]


def memory_parts(core, mine, other, corr_high, corr_low, resp_high, resp_low):
    return kernel_call(
        memory_kernel,
        shape(SIDE, SLICE, 2 * WIDTH + LANES),
        (core, mine, other, corr_high, corr_low, resp_high, resp_low),
        scratch=(pltpu.VMEM((2 * ROWS, WIDTH), bf16),),
        flops=12 * ROWS * WIDTH * WIDTH,
        prefetch=1,
    )


def energy_message(corr, resp):
    energy = 3.0 * corr * resp
    slope = 1.5 * corr * corr
    terms = jnp.sum(energy * corr + slope * resp, axis=1, keepdims=True)
    return jnp.concatenate([energy, jnp.broadcast_to(terms, (SLICE, LANES))], axis=1)


def advance(pieces, cross, corr, resp):
    sums = jnp.sum(pieces, axis=0)
    memory_corr = sums[:, :WIDTH]
    memory_resp = sums[:, WIDTH : 2 * WIDTH]
    multiplier = heat_reservoir_warmth + COEFFICIENT * sums[:, 2 * WIDTH : 2 * WIDTH + 1]
    return (
        corr + step_size * (COEFFICIENT * (memory_corr + cross) - multiplier * corr),
        resp + step_size * (COEFFICIENT * memory_resp - multiplier * resp),
    )


def advance_kernel(pieces_ref, cross_ref, corr_ref, resp_ref, c_ref, r_ref, m_ref, copies_ref):
    corr, resp = advance(pieces_ref[...], cross_ref[...], corr_ref[...], resp_ref[...])
    c_ref[...] = corr
    r_ref[...] = resp
    m_ref[...] = energy_message(corr, resp)
    for j in range(SIDE):
        copies_ref[j] = corr


def last_kernel(pieces_ref, cross_ref, corr_ref, resp_ref, copies_ref):
    corr, resp = advance(pieces_ref[...], cross_ref[...], corr_ref[...], resp_ref[...])
    for j in range(SIDE):
        copies_ref[j, :, :WIDTH] = corr
        copies_ref[j, :, WIDTH:] = resp


def swap(values, axis, size, bit):
    return lax.ppermute(values, axis, [(i, i ^ bit) for i in range(size)])


def sum_over_col(keep, give):
    total = keep + swap(give, "core", 2, 1)
    for bit in (1, 2, 4):
        pairs = total.reshape(-1, 2, SLICE, WIDTH)
        total = pairs[:, 0] + swap(pairs[:, 1], "z", 8, bit)
    return total[0]


def transpose(piece):
    return lax.ppermute(piece, ALL, TRANSPOSE)


def body(hist_corr, hist_resp, row_corr, row_resp):
    my_row = lax.axis_index(ROW)
    core = lax.axis_index("core")
    col = (2 * lax.axis_index("z") + core).reshape(1)
    core = core.reshape(1)
    corr = lax.dynamic_slice_in_dim(row_corr, my_row * SLICE, SLICE, 0)
    resp = lax.dynamic_slice_in_dim(row_resp, my_row * SLICE, SLICE, 0)
    message = energy_message(corr, resp)
    full = row_corr.reshape(SIDE, SLICE, WIDTH)
    corr_high, corr_low, resp_high, resp_low = split_history(hist_corr, hist_resp)
    for block_index in range(BLOCKS):
        if block_index:
            full = lax.all_to_all(copies, ROW, 0, 0, tiled=True)
        message = transpose(message)
        mine = lax.all_to_all(
            jnp.broadcast_to(message[None], (SIDE // 2,) + message.shape), "z", 0, 0, tiled=True
        )
        other = swap(mine, "core", 2, 1)
        keep, give = cross_parts(col, full, resp_high, resp_low)
        cross = transpose(sum_over_col(keep, give))
        parts = memory_parts(core, mine, other, corr_high, corr_low, resp_high, resp_low)
        pieces = lax.all_to_all(parts, ROW, 0, 0, tiled=True)
        piece = shape(SLICE, WIDTH)
        if block_index < BLOCKS - 1:
            corr, resp, message, copies = kernel_call(
                advance_kernel,
                (piece, piece, shape(SLICE, WIDTH + LANES), shape(SIDE, SLICE, WIDTH)),
                (pieces, cross, corr, resp),
            )
        else:
            copies = kernel_call(
                last_kernel, shape(SIDE, SLICE, 2 * WIDTH), (pieces, cross, corr, resp)
            )
    final = lax.all_to_all(copies, ROW, 0, 0, tiled=True).reshape(ROWS, 2 * WIDTH)
    return (final[:, :WIDTH], final[:, WIDTH:])


def solution(mesh):
    split_mesh = Mesh(mesh.devices.reshape(4, 4, 8, 2), ALL)
    times = ("z", "core")
    in_specs = (P(ROW, times), P(ROW, times), P(None, times), P(None, times))
    out_specs = (P(None, times), P(None, times))
    return jax.shard_map(
        body, mesh=split_mesh, in_specs=in_specs, out_specs=out_specs, check_vma=False
    )
```

time: 928 us -> 352 us (0.38)
  waiting for transfers between devices: 742 us -> 83.9 us
  starting transfers between devices: 0.33 us -> 164 us
  blocking collectives: 95.8 us -> 25.1 us
  matrix products: 64.7 us -> 0 us
  local copies, waits for them, and re-layouts: 0.05 us -> 35.3 us
  Pallas kernels: 0 us -> 34.4 us
  between operations: 14.2 us -> 1.09 us
    psum x8 -> x0, waiting for transfers between devices: 742 us -> none  [the longest x4 453 us: from_root(): return lax.psum(block, axis)]
    psum x4 -> x0, blocking collectives: 95.8 us -> none  [body(): enforcing_scalar_sum = lax.psum(multiplier_terms, 'col')]
    all_to_all x0 -> x11, starting transfers between devices: none -> 94.6 us  [the longest x3 35.6 us: body(): full = lax.all_to_all(copies, ROW, 0, 0, tiled=True)]
    ppermute x0 -> x28, waiting for transfers between devices: none -> 70.1 us  [the longest x20 47.1 us: swap(): return lax.ppermute(values, axis, [(i, i ^ bit) for i in range(size)])]
    ppermute x0 -> x28, starting transfers between devices: none -> 69.9 us  [the longest x8 46.5 us: transpose(): return lax.ppermute(piece, ALL, TRANSPOSE)]
    dot_general x12 -> x0, matrix products: 64.7 us -> none  [the longest x4 29.1 us: body(): lax.dot_general(slope_contribution, hist_resp, (((1,), (1,)), ((), ())),...]
    pallas_call x0 -> x13, Pallas kernels: none -> 34.4 us  [kernel_call(): pl.pallas_call(body, out_shape=outs, in_specs=[smem] * prefetch + [vmem]...]
    unnamed x28 -> x50, local copies, waits for them, and re-layouts: 0.05 us -> 29.7 us
  transfers between devices with their start and end apart: 8 -> 39, of which waited for: 8 -> 22; matrix products, arithmetic and copies ran while one was open for 0% -> 1% of each run, Pallas kernels for 0% -> 10%
where the time goes in v1:
time: 352 us; the launch traced here: 348 us
  starting transfers between devices  164 us (47%)
  waiting for transfers between devices  83.9 us (24%)
  local copies, waits for them, and re-layouts  35.3 us (10%)
  Pallas kernels  34.4 us (10%)
  blocking collectives  25.1 us (7%)
  other arithmetic  3.88 us (1%)
    ppermute x20, waiting for transfers between devices, swap(): return lax.ppermute(values, axis, [(i, i ^ bit) for i in range(size)])  47.1 us
    ppermute x8, starting transfers between devices, transpose(): return lax.ppermute(piece, ALL, TRANSPOSE)  46.5 us
    all_to_all x3, starting transfers between devices, body(): full = lax.all_to_all(copies, ROW, 0, 0, tiled=True)  35.6 us
    pallas_call x13, Pallas kernels, kernel_call(): pl.pallas_call(body, out_shape=outs, in_specs=[smem] * prefetch + [vmem]...  34.4 us
    all_to_all x4, starting transfers between devices, body(): lax.all_to_all(jnp.broadcast_to(message[None], (SIDE // 2,) + message.sha...  34 us
    unnamed x50, local copies, waits for them, and re-layouts  29.7 us
    all_to_all x1, blocking collectives, body(): lax.all_to_all(copies, ROW, 0, 0, tiled=True).reshape(ROWS, 2 * WIDTH)  25.1 us
    all_to_all x4, starting transfers between devices, body(): pieces = lax.all_to_all(parts, ROW, 0, 0, tiled=True)  25 us
  transfers between devices with their start and end apart: 39, of which 22 were waited for; matrix products, arithmetic and copies ran while one was open for 1% of the time, Pallas kernels for 10%

profile of v1, /device:TPU:1, one launch (start us, length us, event | category | flops | bytes accessed | tf_op | source)
XLA Modules:
  0.0 348.1 jit_solution(8313057363774174384)
XLA Ops:
  1.6 4.5 %collective-permute-start = (f32[8,1152]{1,0:T(8,128)S(1)}, f32[8,1152]{1,0:T(8,128)S(1)}, u32[]{:S(2)}, u32[]{:S(2)}) collective-permute-start(f32[8,1152]{1,0:T(8,128)S(1)} %pad_maximum_fusion), channel_id=1, source_target_pairs={{0,0},{1,16},{2,32},{3,48},{4,64},{5,80},{6,96},{7,112},{8,128},{9... | collective-permute-start | bytes 110600 | tf_op jit(solution)/shard_map/ppermute | solution.py:192
  6.1 1.6 collective-permute-done
  8.5 16.0 %all-to-all-start = ((f32[8,8,1152]{2,1,0:T(8,128)}), f32[8,8,1152]{2,1,0:T(8,128)S(1)}, u32[]{:S(2)}, u32[]{:S(2)}) async-start(f32[8,8,1152]{2,1,0:T(8,128)} %broadcast_in_dim.11), calls=%async_computation | async-start | bytes 589824 | tf_op jit(solution)/shard_map/all_to_all | solution.py:209
  24.5 2.2 copy-done.18
  26.7 3.7 %shard_map.59 = (bf16[1024,1024]{1,0:T(8,128)(2,1)S(1)}, bf16[1024,1024]{1,0:T(8,128)(2,1)S(1)}, bf16[1024,1024]{1,0:T(8,128)(2,1)S(1)}, bf16[1024,1024]{1,0:T(8,128)(2,1)S(1)}) custom-call(f32[1024,1024]{1,0:T(8,128)S(1)} %copy-done.18, f32[1024,1024]{1,0:T(8,128)} %resp_ref.1), custom_call_target="tpu_custom_call" | custom-call | flops 1048576 | bytes 8388608 | tf_op jit(solution)/shard_map/pallas_call | solution.py:36
  31.8 2.8 shard_map.61
  36.1 2.0 collective-permute-start.1
  39.7 1.6 copy-done.1
  41.3 1.6 copy-done.9
  42.9 1.6 copy-done.14
  44.5 4.3 %shard_map.60 = f32[16,8,2176]{2,1,0:T(8,128)} custom-call(s32[1]{0:T(128)} %bitcast.core_ref, f32[8,8,1152]{2,1,0:T(8,128)S(1)} %all-to-all-done.mine_ref, f32[8,8,1152]{2,1,0:T(8,128)S(1)} %collective-permute-done.1.other_ref, bf16[1024,1024]{1,0:T(8,128)(2,1)S(1)} %copy-done.9, bf16[1024,1024]{1,0:T(8,128)(2,1)S(1)} %copy-done.14, ...), custom_call_target="tpu_custom_call" | custom-call | flops 1610612736 | bytes 8978436 | tf_op jit(solution)/shard_map/pallas_call | solution.py:36
  48.8 4.5 %all-to-all-start.1 = ((f32[16,8,2176]{2,1,0:T(8,128)}), f32[16,8,2176]{2,1,0:T(8,128)S(1)}, u32[]{:S(2)}, u32[]{:S(2)}) async-start(f32[16,8,2176]{2,1,0:T(8,128)} %shard_map.60), calls=%async_computation.1 | async-start | bytes 2228224 | tf_op jit(solution)/shard_map/all_to_all | solution.py:216
  54.3 2.2 collective-permute-start.4
  56.5 4.0 %collective-permute-done.4 = f32[2,8,1024]{2,1,0:T(8,128)S(1)} collective-permute-done((f32[2,8,1024]{2,1,0:T(8,128)S(1)}, f32[2,8,1024]{2,1,0:T(8,128)S(1)}, u32[]{:S(2)}, u32[]{:S(2)}) %collective-permute-start.4) | collective-permute-done | bytes 65568 | tf_op jit(solution)/shard_map/ppermute | solution.py:180
  60.5 2.2 collective-permute-start.5
  62.7 5.0 %collective-permute-done.5 = f32[1,8,1024]{2,1,0:T(8,128)S(1)} collective-permute-done((f32[1,8,1024]{2,1,0:T(8,128)S(1)}, f32[1,8,1024]{2,1,0:T(8,128)S(1)}, u32[]{:S(2)}, u32[]{:S(2)}) %collective-permute-start.5) | collective-permute-done | bytes 32800 | tf_op jit(solution)/shard_map/ppermute | solution.py:180
  67.7 4.6 %collective-permute-start.6 = (f32[8,1024]{1,0:T(8,128)S(1)}, f32[8,1024]{1,0:T(8,128)S(1)}, u32[]{:S(2)}, u32[]{:S(2)}) collective-permute-start(f32[8,1024]{1,0:T(8,128)S(1)} %fusion.22), channel_id=1, source_target_pairs={{0,0},{1,16},{2,32},{3,48},{4,64},{5,80},{6,96},{7,112},{8,128},{9... | collective-permute-start | bytes 98312 | tf_op jit(solution)/shard_map/ppermute | solution.py:192
  72.3 1.6 collective-permute-done.6.cross_ref
  74.9 11.8 %all-to-all-start.4 = ((f32[16,8,1024]{2,1,0:T(8,128)}), f32[16,8,1024]{2,1,0:T(8,128)S(1)}, u32[]{:S(2)}, u32[]{:S(2)}) async-start(f32[16,8,1024]{2,1,0:T(8,128)} %copy-done.20), calls=%async_computation.4 | async-start | bytes 1048576 | tf_op jit(solution)/shard_map/all_to_all | solution.py:207
  86.7 7.4 %collective-permute-start.7 = (f32[8,1152]{1,0:T(8,128)S(1)}, f32[8,1152]{1,0:T(8,128)S(1)}, u32[]{:S(2)}, u32[]{:S(2)}) collective-permute-start(f32[8,1152]{1,0:T(8,128)S(1)} %get-tuple-element.32), channel_id=1, source_target_pairs={{0,0},{1,16},{2,32},{3,48},{4,64},{5,80},{6,96},{7,112},{8,128},{9... | collective-permute-start | bytes 110600 | tf_op jit(solution)/shard_map/ppermute | solution.py:192
  94.1 5.0 %collective-permute-done.7 = f32[8,1152]{1,0:T(8,128)S(1)} collective-permute-done((f32[8,1152]{1,0:T(8,128)S(1)}, f32[8,1152]{1,0:T(8,128)S(1)}, u32[]{:S(2)}, u32[]{:S(2)}) %collective-permute-start.7) | collective-permute-done | bytes 36896 | tf_op jit(solution)/shard_map/ppermute | solution.py:192
  99.8 5.9 %all-to-all-start.2 = ((f32[8,8,1152]{2,1,0:T(8,128)}), f32[8,8,1152]{2,1,0:T(8,128)S(1)}, u32[]{:S(2)}, u32[]{:S(2)}) async-start(f32[8,8,1152]{2,1,0:T(8,128)} %broadcast_in_dim.12), calls=%async_computation.2 | async-start | bytes 589824 | tf_op jit(solution)/shard_map/all_to_all | solution.py:209
  107.4 3.5 %shard_map.64 = (f32[8,8,1024]{2,1,0:T(8,128)S(1)}, f32[8,8,1024]{2,1,0:T(8,128)}) custom-call(s32[1]{0:T(128)} %bitcast.1.col_ref, f32[16,8,1024]{2,1,0:T(8,128)S(1)} %all-to-all-done.4.full_ref, bf16[1024,1024]{1,0:T(8,128)(2,1)S(1)} %get-tuple-element.28.rh_ref, bf16[1024,1024]{1,0:T(8,128)(2,1)S(1)} %copy-done.2), custom_call_target="tpu_custom_call" | custom-call | flops 805306368 | bytes 4718596 | tf_op jit(solution)/shard_map/pallas_call | solution.py:36
  110.9 1.7 collective-permute-start.9
  112.6 3.7 %all-to-all-done.2.mine_ref = f32[8,8,1152]{2,1,0:T(8,128)S(1)} async-done(((f32[8,8,1152]{2,1,0:T(8,128)}), f32[8,8,1152]{2,1,0:T(8,128)S(1)}, u32[]{:S(2)}, u32[]{:S(2)}) %all-to-all-start.2) | async-done | bytes 294944 | tf_op jit(solution)/shard_map/all_to_all | solution.py:209
  116.3 3.0 collective-permute-start.8
  120.5 1.6 copy-done.3
  122.1 1.6 copy-done.10
  123.7 1.6 copy-done.15
  125.3 4.3 %shard_map.63 = f32[16,8,2176]{2,1,0:T(8,128)} custom-call(s32[1]{0:T(128)} %bitcast.core_ref, f32[8,8,1152]{2,1,0:T(8,128)S(1)} %all-to-all-done.2.mine_ref, f32[8,8,1152]{2,1,0:T(8,128)S(1)} %collective-permute-done.8.other_ref, bf16[1024,1024]{1,0:T(8,128)(2,1)S(1)} %copy-done.10, bf16[1024,1024]{1,0:T(8,128)(2,1)S(1)} %copy-done.15, ...), custom_call_target="tpu_custom_call" | custom-call | flops 1610612736 | bytes 8978436 | tf_op jit(solution)/shard_map/pallas_call | solution.py:36
  129.6 6.9 %all-to-all-start.3 = ((f32[16,8,2176]{2,1,0:T(8,128)}), f32[16,8,2176]{2,1,0:T(8,128)S(1)}, u32[]{:S(2)}, u32[]{:S(2)}) async-start(f32[16,8,2176]{2,1,0:T(8,128)} %shard_map.63), calls=%async_computation.3 | async-start | bytes 2228224 | tf_op jit(solution)/shard_map/all_to_all | solution.py:216
  137.7 4.2 %collective-permute-done.11 = f32[2,8,1024]{2,1,0:T(8,128)S(1)} collective-permute-done((f32[2,8,1024]{2,1,0:T(8,128)S(1)}, f32[2,8,1024]{2,1,0:T(8,128)S(1)}, u32[]{:S(2)}, u32[]{:S(2)}) %collective-permute-start.11) | collective-permute-done | bytes 65568 | tf_op jit(solution)/shard_map/ppermute | solution.py:180
  142.8 5.8 %collective-permute-done.12 = f32[1,8,1024]{2,1,0:T(8,128)S(1)} collective-permute-done((f32[1,8,1024]{2,1,0:T(8,128)S(1)}, f32[1,8,1024]{2,1,0:T(8,128)S(1)}, u32[]{:S(2)}, u32[]{:S(2)}) %collective-permute-start.12) | collective-permute-done | bytes 32800 | tf_op jit(solution)/shard_map/ppermute | solution.py:180
  148.6 6.2 %collective-permute-start.13 = (f32[8,1024]{1,0:T(8,128)S(1)}, f32[8,1024]{1,0:T(8,128)S(1)}, u32[]{:S(2)}, u32[]{:S(2)}) collective-permute-start(f32[8,1024]{1,0:T(8,128)S(1)} %fusion.20), channel_id=1, source_target_pairs={{0,0},{1,16},{2,32},{3,48},{4,64},{5,80},{6,96},{7,112},{8,128},{9... | collective-permute-start | bytes 98312 | tf_op jit(solution)/shard_map/ppermute | solution.py:192
  154.8 1.6 collective-permute-done.13.cross_ref
  157.4 11.9 %all-to-all-start.7 = ((f32[16,8,1024]{2,1,0:T(8,128)}), f32[16,8,1024]{2,1,0:T(8,128)S(1)}, u32[]{:S(2)}, u32[]{:S(2)}) async-start(f32[16,8,1024]{2,1,0:T(8,128)} %copy-done.21), calls=%async_computation.7 | async-start | bytes 1048576 | tf_op jit(solution)/shard_map/all_to_all | solution.py:207
  169.3 7.4 %collective-permute-start.14 = (f32[8,1152]{1,0:T(8,128)S(1)}, f32[8,1152]{1,0:T(8,128)S(1)}, u32[]{:S(2)}, u32[]{:S(2)}) collective-permute-start(f32[8,1152]{1,0:T(8,128)S(1)} %get-tuple-element.38), channel_id=1, source_target_pairs={{0,0},{1,16},{2,32},{3,48},{4,64},{5,80},{6,96},{7,112},{8,128},{9... | collective-permute-start | bytes 110600 | tf_op jit(solution)/shard_map/ppermute | solution.py:192
  176.6 5.0 %collective-permute-done.14 = f32[8,1152]{1,0:T(8,128)S(1)} collective-permute-done((f32[8,1152]{1,0:T(8,128)S(1)}, f32[8,1152]{1,0:T(8,128)S(1)}, u32[]{:S(2)}, u32[]{:S(2)}) %collective-permute-start.14) | collective-permute-done | bytes 36896 | tf_op jit(solution)/shard_map/ppermute | solution.py:192
  182.4 6.0 %all-to-all-start.5 = ((f32[8,8,1152]{2,1,0:T(8,128)}), f32[8,8,1152]{2,1,0:T(8,128)S(1)}, u32[]{:S(2)}, u32[]{:S(2)}) async-start(f32[8,8,1152]{2,1,0:T(8,128)} %broadcast_in_dim.13), calls=%async_computation.5 | async-start | bytes 589824 | tf_op jit(solution)/shard_map/all_to_all | solution.py:209
  190.0 3.5 %shard_map.67 = (f32[8,8,1024]{2,1,0:T(8,128)S(1)}, f32[8,8,1024]{2,1,0:T(8,128)}) custom-call(s32[1]{0:T(128)} %bitcast.1.col_ref, f32[16,8,1024]{2,1,0:T(8,128)S(1)} %all-to-all-done.7.full_ref, bf16[1024,1024]{1,0:T(8,128)(2,1)S(1)} %get-tuple-element.28.rh_ref, bf16[1024,1024]{1,0:T(8,128)(2,1)S(1)} %copy-done.4), custom_call_target="tpu_custom_call" | custom-call | flops 805306368 | bytes 4718596 | tf_op jit(solution)/shard_map/pallas_call | solution.py:36
  194.6 4.7 %all-to-all-done.5.mine_ref = f32[8,8,1152]{2,1,0:T(8,128)S(1)} async-done(((f32[8,8,1152]{2,1,0:T(8,128)}), f32[8,8,1152]{2,1,0:T(8,128)S(1)}, u32[]{:S(2)}, u32[]{:S(2)}) %all-to-all-start.5) | async-done | bytes 294944 | tf_op jit(solution)/shard_map/all_to_all | solution.py:209
  199.3 2.6 collective-permute-start.15
  203.1 1.6 copy-done.5
  204.7 1.6 copy-done.11
  207.9 4.3 %shard_map.66 = f32[16,8,2176]{2,1,0:T(8,128)} custom-call(s32[1]{0:T(128)} %bitcast.core_ref, f32[8,8,1152]{2,1,0:T(8,128)S(1)} %all-to-all-done.5.mine_ref, f32[8,8,1152]{2,1,0:T(8,128)S(1)} %collective-permute-done.15.other_ref, bf16[1024,1024]{1,0:T(8,128)(2,1)S(1)} %copy-done.11, bf16[1024,1024]{1,0:T(8,128)(2,1)S(1)} %copy-done.16, ...), custom_call_target="tpu_custom_call" | custom-call | flops 1610612736 | bytes 8978436 | tf_op jit(solution)/shard_map/pallas_call | solution.py:36
  212.2 6.8 %all-to-all-start.6 = ((f32[16,8,2176]{2,1,0:T(8,128)}), f32[16,8,2176]{2,1,0:T(8,128)S(1)}, u32[]{:S(2)}, u32[]{:S(2)}) async-start(f32[16,8,2176]{2,1,0:T(8,128)} %shard_map.66), calls=%async_computation.6 | async-start | bytes 2228224 | tf_op jit(solution)/shard_map/all_to_all | solution.py:216
  220.1 6.0 %collective-permute-done.18 = f32[2,8,1024]{2,1,0:T(8,128)S(1)} collective-permute-done((f32[2,8,1024]{2,1,0:T(8,128)S(1)}, f32[2,8,1024]{2,1,0:T(8,128)S(1)}, u32[]{:S(2)}, u32[]{:S(2)}) %collective-permute-start.18) | collective-permute-done | bytes 65568 | tf_op jit(solution)/shard_map/ppermute | solution.py:180
  226.2 7.1 %collective-permute-done.19 = f32[1,8,1024]{2,1,0:T(8,128)S(1)} collective-permute-done((f32[1,8,1024]{2,1,0:T(8,128)S(1)}, f32[1,8,1024]{2,1,0:T(8,128)S(1)}, u32[]{:S(2)}, u32[]{:S(2)}) %collective-permute-start.19) | collective-permute-done | bytes 32800 | tf_op jit(solution)/shard_map/ppermute | solution.py:180
  233.3 4.6 %collective-permute-start.20 = (f32[8,1024]{1,0:T(8,128)S(1)}, f32[8,1024]{1,0:T(8,128)S(1)}, u32[]{:S(2)}, u32[]{:S(2)}) collective-permute-start(f32[8,1024]{1,0:T(8,128)S(1)} %fusion.18), channel_id=1, source_target_pairs={{0,0},{1,16},{2,32},{3,48},{4,64},{5,80},{6,96},{7,112},{8,128},{9... | collective-permute-start | bytes 98312 | tf_op jit(solution)/shard_map/ppermute | solution.py:192
  238.0 1.6 collective-permute-done.20.cross_ref
  240.6 11.9 %all-to-all-start.10 = ((f32[16,8,1024]{2,1,0:T(8,128)}), f32[16,8,1024]{2,1,0:T(8,128)S(1)}, u32[]{:S(2)}, u32[]{:S(2)}) async-start(f32[16,8,1024]{2,1,0:T(8,128)} %copy-done.22), calls=%async_computation.10 | async-start | bytes 1048576 | tf_op jit(solution)/shard_map/all_to_all | solution.py:207
  252.4 7.4 %collective-permute-start.21 = (f32[8,1152]{1,0:T(8,128)S(1)}, f32[8,1152]{1,0:T(8,128)S(1)}, u32[]{:S(2)}, u32[]{:S(2)}) collective-permute-start(f32[8,1152]{1,0:T(8,128)S(1)} %get-tuple-element.44), channel_id=1, source_target_pairs={{0,0},{1,16},{2,32},{3,48},{4,64},{5,80},{6,96},{7,112},{8,128},{9... | collective-permute-start | bytes 110600 | tf_op jit(solution)/shard_map/ppermute | solution.py:192
  259.8 5.0 %collective-permute-done.21 = f32[8,1152]{1,0:T(8,128)S(1)} collective-permute-done((f32[8,1152]{1,0:T(8,128)S(1)}, f32[8,1152]{1,0:T(8,128)S(1)}, u32[]{:S(2)}, u32[]{:S(2)}) %collective-permute-start.21) | collective-permute-done | bytes 36896 | tf_op jit(solution)/shard_map/ppermute | solution.py:192
  265.5 6.0 %all-to-all-start.8 = ((f32[8,8,1152]{2,1,0:T(8,128)}), f32[8,8,1152]{2,1,0:T(8,128)S(1)}, u32[]{:S(2)}, u32[]{:S(2)}) async-start(f32[8,8,1152]{2,1,0:T(8,128)} %broadcast_in_dim.14), calls=%async_computation.8 | async-start | bytes 589824 | tf_op jit(solution)/shard_map/all_to_all | solution.py:209
  273.1 2.8 shard_map.70
  277.1 5.4 %all-to-all-done.8.mine_ref = f32[8,8,1152]{2,1,0:T(8,128)S(1)} async-done(((f32[8,8,1152]{2,1,0:T(8,128)}), f32[8,8,1152]{2,1,0:T(8,128)S(1)}, u32[]{:S(2)}, u32[]{:S(2)}) %all-to-all-start.8) | async-done | bytes 294944 | tf_op jit(solution)/shard_map/all_to_all | solution.py:209
  282.5 2.6 collective-permute-start.22
  291.1 4.2 %shard_map.69 = f32[16,8,2176]{2,1,0:T(8,128)} custom-call(s32[1]{0:T(128)} %bitcast.core_ref, f32[8,8,1152]{2,1,0:T(8,128)S(1)} %all-to-all-done.8.mine_ref, f32[8,8,1152]{2,1,0:T(8,128)S(1)} %collective-permute-done.22.other_ref, bf16[1024,1024]{1,0:T(8,128)(2,1)S(1)} %copy-done.12, bf16[1024,1024]{1,0:T(8,128)(2,1)S(1)} %copy-done.17, ...), custom_call_target="tpu_custom_call" | custom-call | flops 1610612736 | bytes 8978436 | tf_op jit(solution)/shard_map/pallas_call | solution.py:36
  295.3 6.8 %all-to-all-start.9 = ((f32[16,8,2176]{2,1,0:T(8,128)}), f32[16,8,2176]{2,1,0:T(8,128)S(1)}, u32[]{:S(2)}, u32[]{:S(2)}) async-start(f32[16,8,2176]{2,1,0:T(8,128)} %shard_map.69), calls=%async_computation.9 | async-start | bytes 2228224 | tf_op jit(solution)/shard_map/all_to_all | solution.py:216
  302.2 6.0 %collective-permute-done.25 = f32[2,8,1024]{2,1,0:T(8,128)S(1)} collective-permute-done((f32[2,8,1024]{2,1,0:T(8,128)S(1)}, f32[2,8,1024]{2,1,0:T(8,128)S(1)}, u32[]{:S(2)}, u32[]{:S(2)}) %collective-permute-start.25) | collective-permute-done | bytes 65568 | tf_op jit(solution)/shard_map/ppermute | solution.py:180
  308.3 7.3 %collective-permute-done.26 = f32[1,8,1024]{2,1,0:T(8,128)S(1)} collective-permute-done((f32[1,8,1024]{2,1,0:T(8,128)S(1)}, f32[1,8,1024]{2,1,0:T(8,128)S(1)}, u32[]{:S(2)}, u32[]{:S(2)}) %collective-permute-start.26) | collective-permute-done | bytes 32800 | tf_op jit(solution)/shard_map/ppermute | solution.py:180
  315.7 4.5 %collective-permute-start.27 = (f32[8,1024]{1,0:T(8,128)S(1)}, f32[8,1024]{1,0:T(8,128)S(1)}, u32[]{:S(2)}, u32[]{:S(2)}) collective-permute-start(f32[8,1024]{1,0:T(8,128)S(1)} %fusion.16), channel_id=1, source_target_pairs={{0,0},{1,16},{2,32},{3,48},{4,64},{5,80},{6,96},{7,112},{8,128},{9... | collective-permute-start | bytes 98312 | tf_op jit(solution)/shard_map/ppermute | solution.py:192
  320.1 1.6 collective-permute-done.27.cross_ref
  321.9 25.1 %all_to_all.60 = f32[16,8,2048]{2,1,0:T(8,128)S(1)} all-to-all(f32[16,8,2048]{2,1,0:T(8,128)S(1)} %shard_map.71), channel_id=1, replica_groups=mesh['y'=4,'x'=4,'z'=8,'core'=2] {'y','x'}, dimensions={0} | all-to-all | bytes 2097152 | tf_op jit(solution)/shard_map/all_to_all | solution.py:228
  (115 shorter events, 33.9 us)
Async XLA Ops:
  1.6 6.1 %collective-permute-start = (f32[8,1152]{1,0:T(8,128)S(1)}, f32[8,1152]{1,0:T(8,128)S(1)}, u32[]{:S(2)}, u32[]{:S(2)}) collective-permute-start(f32[8,1152]{1,0:T(8,128)S(1)} %pad_maximum_fusion), channel_id=1, source_target_pairs={{0,0},{1,16},{2,32},{3,48},{4,64},{5,80},{6,96},{7,112},{8,128},{9... | collective-permute-start | bytes 110600 | tf_op jit(solution)/shard_map/ppermute | solution.py:192
  8.5 27.6 %all-to-all-start = ((f32[8,8,1152]{2,1,0:T(8,128)}), f32[8,8,1152]{2,1,0:T(8,128)S(1)}, u32[]{:S(2)}, u32[]{:S(2)}) async-start(f32[8,8,1152]{2,1,0:T(8,128)} %broadcast_in_dim.11), calls=%async_computation | async-start | bytes 589824 | tf_op jit(solution)/shard_map/all_to_all | solution.py:209
  24.5 2.2 copy-start.18
  26.7 5.1 %copy-start.19 = (f32[128,1024]{1,0:T(8,128)S(1)}, f32[128,1024]{1,0:T(8,128)}, u32[]{:S(2)}) copy-start(f32[128,1024]{1,0:T(8,128)} %param.6) | copy-start | bytes 1572868
  30.5 1.3 copy-start.8
  31.8 2.8 copy-start
  31.8 2.9 copy-start.13
  34.7 3.4 collective-permute-start.2
  36.1 3.6 %collective-permute-start.1 = (f32[8,8,1152]{2,1,0:T(8,128)S(1)}, f32[8,8,1152]{2,1,0:T(8,128)S(1)}, u32[]{:S(2)}, u32[]{:S(2)}) collective-permute-start(f32[8,8,1152]{2,1,0:T(8,128)S(1)} %all-to-all-done.mine_ref), channel_id=1, source_target_pairs={{0,1},{1,0},{2,3},{3,2},{4,5},{5,4},{6,7},{7,6},{8,9},{9,8},{10,11... | collective-permute-start | bytes 884744 | tf_op jit(solution)/shard_map/ppermute | solution.py:180
  38.8 14.5 %collective-permute-start.3 = (f32[4,8,1024]{2,1,0:T(8,128)}, f32[4,8,1024]{2,1,0:T(8,128)}, u32[]{:S(2)}, u32[]{:S(2)}) collective-permute-start(f32[4,8,1024]{2,1,0:T(8,128)} %slice_bitcast_fusion.6), channel_id=1, source_target_pairs={{0,2},{2,0},{4,6},{6,4},{8,10},{10,8},{12,14},{14,12},{1,3},{3,1},... | collective-permute-start | bytes 393224 | tf_op jit(solution)/shard_map/ppermute | solution.py:180
  39.7 1.6 copy-start.1
  41.3 1.6 copy-start.9
  42.9 1.6 copy-start.14
  48.8 25.1 %all-to-all-start.1 = ((f32[16,8,2176]{2,1,0:T(8,128)}), f32[16,8,2176]{2,1,0:T(8,128)S(1)}, u32[]{:S(2)}, u32[]{:S(2)}) async-start(f32[16,8,2176]{2,1,0:T(8,128)} %shard_map.60), calls=%async_computation.1 | async-start | bytes 2228224 | tf_op jit(solution)/shard_map/all_to_all | solution.py:216
  54.3 6.2 %collective-permute-start.4 = (f32[2,8,1024]{2,1,0:T(8,128)S(1)}, f32[2,8,1024]{2,1,0:T(8,128)S(1)}, u32[]{:S(2)}, u32[]{:S(2)}) collective-permute-start(f32[2,8,1024]{2,1,0:T(8,128)S(1)} %slice_bitcast_fusion.14), channel_id=1, source_target_pairs={{0,4},{2,6},{4,0},{6,2},{8,12},{10,14},{12,8},{14,10},{1,5},{3,7},... | collective-permute-start | bytes 196616 | tf_op jit(solution)/shard_map/ppermute | solution.py:180
  60.5 7.2 %collective-permute-start.5 = (f32[1,8,1024]{2,1,0:T(8,128)S(1)}, f32[1,8,1024]{2,1,0:T(8,128)S(1)}, u32[]{:S(2)}, u32[]{:S(2)}) collective-permute-start(f32[1,8,1024]{2,1,0:T(8,128)S(1)} %slice_bitcast_fusion.22), channel_id=1, source_target_pairs={{0,8},{2,10},{4,12},{6,14},{8,0},{10,2},{12,4},{14,6},{1,9},{3,11}... | collective-permute-start | bytes 98312 | tf_op jit(solution)/shard_map/ppermute | solution.py:180
  67.7 6.2 %collective-permute-start.6 = (f32[8,1024]{1,0:T(8,128)S(1)}, f32[8,1024]{1,0:T(8,128)S(1)}, u32[]{:S(2)}, u32[]{:S(2)}) collective-permute-start(f32[8,1024]{1,0:T(8,128)S(1)} %fusion.22), channel_id=1, source_target_pairs={{0,0},{1,16},{2,32},{3,48},{4,64},{5,80},{6,96},{7,112},{8,128},{9... | collective-permute-start | bytes 98312 | tf_op jit(solution)/shard_map/ppermute | solution.py:192
  74.1 0.8 copy-start.20
  74.9 24.2 %all-to-all-start.4 = ((f32[16,8,1024]{2,1,0:T(8,128)}), f32[16,8,1024]{2,1,0:T(8,128)S(1)}, u32[]{:S(2)}, u32[]{:S(2)}) async-start(f32[16,8,1024]{2,1,0:T(8,128)} %copy-done.20), calls=%async_computation.4 | async-start | bytes 1048576 | tf_op jit(solution)/shard_map/all_to_all | solution.py:207
  86.7 12.4 %collective-permute-start.7 = (f32[8,1152]{1,0:T(8,128)S(1)}, f32[8,1152]{1,0:T(8,128)S(1)}, u32[]{:S(2)}, u32[]{:S(2)}) collective-permute-start(f32[8,1152]{1,0:T(8,128)S(1)} %get-tuple-element.32), channel_id=1, source_target_pairs={{0,0},{1,16},{2,32},{3,48},{4,64},{5,80},{6,96},{7,112},{8,128},{9... | collective-permute-start | bytes 110600 | tf_op jit(solution)/shard_map/ppermute | solution.py:192
  99.8 16.5 %all-to-all-start.2 = ((f32[8,8,1152]{2,1,0:T(8,128)}), f32[8,8,1152]{2,1,0:T(8,128)S(1)}, u32[]{:S(2)}, u32[]{:S(2)}) async-start(f32[8,8,1152]{2,1,0:T(8,128)} %broadcast_in_dim.12), calls=%async_computation.2 | async-start | bytes 589824 | tf_op jit(solution)/shard_map/all_to_all | solution.py:209
  105.8 1.6 copy-start.2
  110.9 8.4 %collective-permute-start.9 = (f32[8,8,1024]{2,1,0:T(8,128)}, f32[8,8,1024]{2,1,0:T(8,128)S(1)}, u32[]{:S(2)}, u32[]{:S(2)}) collective-permute-start(f32[8,8,1024]{2,1,0:T(8,128)} %get-tuple-element.35), channel_id=1, source_target_pairs={{0,1},{1,0},{2,3},{3,2},{4,5},{5,4},{6,7},{7,6},{8,9},{9,8},{10,11... | collective-permute-start | bytes 786440 | tf_op jit(solution)/shard_map/ppermute | solution.py:180
  116.3 4.2 %collective-permute-start.8 = (f32[8,8,1152]{2,1,0:T(8,128)S(1)}, f32[8,8,1152]{2,1,0:T(8,128)S(1)}, u32[]{:S(2)}, u32[]{:S(2)}) collective-permute-start(f32[8,8,1152]{2,1,0:T(8,128)S(1)} %all-to-all-done.2.mine_ref), channel_id=1, source_target_pairs={{0,1},{1,0},{2,3},{3,2},{4,5},{5,4},{6,7},{7,6},{8,9},{9,8},{10,11... | collective-permute-start | bytes 884744 | tf_op jit(solution)/shard_map/ppermute | solution.py:180
  119.3 10.3 %copy-start.23 = (f32[8,8,1024]{2,1,0:T(8,128)}, f32[8,8,1024]{2,1,0:T(8,128)S(1)}, u32[]{:S(2)}) copy-start(f32[8,8,1024]{2,1,0:T(8,128)S(1)} %add.69) | copy-start | bytes 786436
  120.1 16.4 %collective-permute-start.10 = (f32[4,8,1024]{2,1,0:T(8,128)}, f32[4,8,1024]{2,1,0:T(8,128)S(1)}, u32[]{:S(2)}, u32[]{:S(2)}) collective-permute-start(f32[4,8,1024]{2,1,0:T(8,128)} %slice_bitcast_fusion.4), channel_id=1, source_target_pairs={{0,2},{2,0},{4,6},{6,4},{8,10},{10,8},{12,14},{14,12},{1,3},{3,1},... | collective-permute-start | bytes 393224 | tf_op jit(solution)/shard_map/ppermute | solution.py:180
  120.5 1.6 copy-start.3
  122.1 1.6 copy-start.10
  123.7 1.6 copy-start.15
  129.6 26.8 %all-to-all-start.3 = ((f32[16,8,2176]{2,1,0:T(8,128)}), f32[16,8,2176]{2,1,0:T(8,128)S(1)}, u32[]{:S(2)}, u32[]{:S(2)}) async-start(f32[16,8,2176]{2,1,0:T(8,128)} %shard_map.63), calls=%async_computation.3 | async-start | bytes 2228224 | tf_op jit(solution)/shard_map/all_to_all | solution.py:216
  137.4 4.4 %collective-permute-start.11 = (f32[2,8,1024]{2,1,0:T(8,128)S(1)}, f32[2,8,1024]{2,1,0:T(8,128)S(1)}, u32[]{:S(2)}, u32[]{:S(2)}) collective-permute-start(f32[2,8,1024]{2,1,0:T(8,128)S(1)} %slice_bitcast_fusion.12), channel_id=1, source_target_pairs={{0,4},{2,6},{4,0},{6,2},{8,12},{10,14},{12,8},{14,10},{1,5},{3,7},... | collective-permute-start | bytes 196616 | tf_op jit(solution)/shard_map/ppermute | solution.py:180
  141.9 6.8 %collective-permute-start.12 = (f32[1,8,1024]{2,1,0:T(8,128)S(1)}, f32[1,8,1024]{2,1,0:T(8,128)S(1)}, u32[]{:S(2)}, u32[]{:S(2)}) collective-permute-start(f32[1,8,1024]{2,1,0:T(8,128)S(1)} %slice_bitcast_fusion.20), channel_id=1, source_target_pairs={{0,8},{2,10},{4,12},{6,14},{8,0},{10,2},{12,4},{14,6},{1,9},{3,11}... | collective-permute-start | bytes 98312 | tf_op jit(solution)/shard_map/ppermute | solution.py:180
  148.6 7.8 %collective-permute-start.13 = (f32[8,1024]{1,0:T(8,128)S(1)}, f32[8,1024]{1,0:T(8,128)S(1)}, u32[]{:S(2)}, u32[]{:S(2)}) collective-permute-start(f32[8,1024]{1,0:T(8,128)S(1)} %fusion.20), channel_id=1, source_target_pairs={{0,0},{1,16},{2,32},{3,48},{4,64},{5,80},{6,96},{7,112},{8,128},{9... | collective-permute-start | bytes 98312 | tf_op jit(solution)/shard_map/ppermute | solution.py:192
  156.6 0.8 copy-start.21
  157.4 24.2 %all-to-all-start.7 = ((f32[16,8,1024]{2,1,0:T(8,128)}), f32[16,8,1024]{2,1,0:T(8,128)S(1)}, u32[]{:S(2)}, u32[]{:S(2)}) async-start(f32[16,8,1024]{2,1,0:T(8,128)} %copy-done.21), calls=%async_computation.7 | async-start | bytes 1048576 | tf_op jit(solution)/shard_map/all_to_all | solution.py:207
  169.3 12.4 %collective-permute-start.14 = (f32[8,1152]{1,0:T(8,128)S(1)}, f32[8,1152]{1,0:T(8,128)S(1)}, u32[]{:S(2)}, u32[]{:S(2)}) collective-permute-start(f32[8,1152]{1,0:T(8,128)S(1)} %get-tuple-element.38), channel_id=1, source_target_pairs={{0,0},{1,16},{2,32},{3,48},{4,64},{5,80},{6,96},{7,112},{8,128},{9... | collective-permute-start | bytes 110600 | tf_op jit(solution)/shard_map/ppermute | solution.py:192
  182.4 16.9 %all-to-all-start.5 = ((f32[8,8,1152]{2,1,0:T(8,128)}), f32[8,8,1152]{2,1,0:T(8,128)S(1)}, u32[]{:S(2)}, u32[]{:S(2)}) async-start(f32[8,8,1152]{2,1,0:T(8,128)} %broadcast_in_dim.13), calls=%async_computation.5 | async-start | bytes 589824 | tf_op jit(solution)/shard_map/all_to_all | solution.py:209
  188.4 1.6 copy-start.4
  193.5 8.4 %collective-permute-start.16 = (f32[8,8,1024]{2,1,0:T(8,128)}, f32[8,8,1024]{2,1,0:T(8,128)S(1)}, u32[]{:S(2)}, u32[]{:S(2)}) collective-permute-start(f32[8,8,1024]{2,1,0:T(8,128)} %get-tuple-element.41), channel_id=1, source_target_pairs={{0,1},{1,0},{2,3},{3,2},{4,5},{5,4},{6,7},{7,6},{8,9},{9,8},{10,11... | collective-permute-start | bytes 786440 | tf_op jit(solution)/shard_map/ppermute | solution.py:180
  199.3 3.8 %collective-permute-start.15 = (f32[8,8,1152]{2,1,0:T(8,128)S(1)}, f32[8,8,1152]{2,1,0:T(8,128)S(1)}, u32[]{:S(2)}, u32[]{:S(2)}) collective-permute-start(f32[8,8,1152]{2,1,0:T(8,128)S(1)} %all-to-all-done.5.mine_ref), channel_id=1, source_target_pairs={{0,1},{1,0},{2,3},{3,2},{4,5},{5,4},{6,7},{7,6},{8,9},{9,8},{10,11... | collective-permute-start | bytes 884744 | tf_op jit(solution)/shard_map/ppermute | solution.py:180
  202.0 10.3 %copy-start.24 = (f32[8,8,1024]{2,1,0:T(8,128)}, f32[8,8,1024]{2,1,0:T(8,128)S(1)}, u32[]{:S(2)}) copy-start(f32[8,8,1024]{2,1,0:T(8,128)S(1)} %add.73) | copy-start | bytes 786436
  202.0 17.0 %collective-permute-start.17 = (f32[4,8,1024]{2,1,0:T(8,128)S(1)}, f32[4,8,1024]{2,1,0:T(8,128)S(1)}, u32[]{:S(2)}, u32[]{:S(2)}) collective-permute-start(f32[4,8,1024]{2,1,0:T(8,128)S(1)} %slice_bitcast_fusion.2), channel_id=1, source_target_pairs={{0,2},{2,0},{4,6},{6,4},{8,10},{10,8},{12,14},{14,12},{1,3},{3,1},... | collective-permute-start | bytes 393224 | tf_op jit(solution)/shard_map/ppermute | solution.py:180
  203.1 1.6 copy-start.5
  204.7 1.6 copy-start.11
  206.3 1.6 copy-start.16
  212.2 27.3 %all-to-all-start.6 = ((f32[16,8,2176]{2,1,0:T(8,128)}), f32[16,8,2176]{2,1,0:T(8,128)S(1)}, u32[]{:S(2)}, u32[]{:S(2)}) async-start(f32[16,8,2176]{2,1,0:T(8,128)} %shard_map.66), calls=%async_computation.6 | async-start | bytes 2228224 | tf_op jit(solution)/shard_map/all_to_all | solution.py:216
  220.0 6.1 %collective-permute-start.18 = (f32[2,8,1024]{2,1,0:T(8,128)S(1)}, f32[2,8,1024]{2,1,0:T(8,128)S(1)}, u32[]{:S(2)}, u32[]{:S(2)}) collective-permute-start(f32[2,8,1024]{2,1,0:T(8,128)S(1)} %slice_bitcast_fusion.10), channel_id=1, source_target_pairs={{0,4},{2,6},{4,0},{6,2},{8,12},{10,14},{12,8},{14,10},{1,5},{3,7},... | collective-permute-start | bytes 196616 | tf_op jit(solution)/shard_map/ppermute | solution.py:180
  226.1 7.2 %collective-permute-start.19 = (f32[1,8,1024]{2,1,0:T(8,128)S(1)}, f32[1,8,1024]{2,1,0:T(8,128)S(1)}, u32[]{:S(2)}, u32[]{:S(2)}) collective-permute-start(f32[1,8,1024]{2,1,0:T(8,128)S(1)} %slice_bitcast_fusion.18), channel_id=1, source_target_pairs={{0,8},{2,10},{4,12},{6,14},{8,0},{10,2},{12,4},{14,6},{1,9},{3,11}... | collective-permute-start | bytes 98312 | tf_op jit(solution)/shard_map/ppermute | solution.py:180
  233.3 6.2 %collective-permute-start.20 = (f32[8,1024]{1,0:T(8,128)S(1)}, f32[8,1024]{1,0:T(8,128)S(1)}, u32[]{:S(2)}, u32[]{:S(2)}) collective-permute-start(f32[8,1024]{1,0:T(8,128)S(1)} %fusion.18), channel_id=1, source_target_pairs={{0,0},{1,16},{2,32},{3,48},{4,64},{5,80},{6,96},{7,112},{8,128},{9... | collective-permute-start | bytes 98312 | tf_op jit(solution)/shard_map/ppermute | solution.py:192
  239.8 0.8 copy-start.22
  240.6 24.2 %all-to-all-start.10 = ((f32[16,8,1024]{2,1,0:T(8,128)}), f32[16,8,1024]{2,1,0:T(8,128)S(1)}, u32[]{:S(2)}, u32[]{:S(2)}) async-start(f32[16,8,1024]{2,1,0:T(8,128)} %copy-done.22), calls=%async_computation.10 | async-start | bytes 1048576 | tf_op jit(solution)/shard_map/all_to_all | solution.py:207
  252.4 12.4 %collective-permute-start.21 = (f32[8,1152]{1,0:T(8,128)S(1)}, f32[8,1152]{1,0:T(8,128)S(1)}, u32[]{:S(2)}, u32[]{:S(2)}) collective-permute-start(f32[8,1152]{1,0:T(8,128)S(1)} %get-tuple-element.44), channel_id=1, source_target_pairs={{0,0},{1,16},{2,32},{3,48},{4,64},{5,80},{6,96},{7,112},{8,128},{9... | collective-permute-start | bytes 110600 | tf_op jit(solution)/shard_map/ppermute | solution.py:192
  265.5 17.0 %all-to-all-start.8 = ((f32[8,8,1152]{2,1,0:T(8,128)}), f32[8,8,1152]{2,1,0:T(8,128)S(1)}, u32[]{:S(2)}, u32[]{:S(2)}) async-start(f32[8,8,1152]{2,1,0:T(8,128)} %broadcast_in_dim.14), calls=%async_computation.8 | async-start | bytes 589824 | tf_op jit(solution)/shard_map/all_to_all | solution.py:209
  271.5 1.6 copy-start.6
  276.0 9.1 %collective-permute-start.23 = (f32[8,8,1024]{2,1,0:T(8,128)S(1)}, f32[8,8,1024]{2,1,0:T(8,128)S(1)}, u32[]{:S(2)}, u32[]{:S(2)}) collective-permute-start(f32[8,8,1024]{2,1,0:T(8,128)S(1)} %get-tuple-element.47), channel_id=1, source_target_pairs={{0,1},{1,0},{2,3},{3,2},{4,5},{5,4},{6,7},{7,6},{8,9},{9,8},{10,11... | collective-permute-start | bytes 786440 | tf_op jit(solution)/shard_map/ppermute | solution.py:180
  282.5 3.8 %collective-permute-start.22 = (f32[8,8,1152]{2,1,0:T(8,128)S(1)}, f32[8,8,1152]{2,1,0:T(8,128)S(1)}, u32[]{:S(2)}, u32[]{:S(2)}) collective-permute-start(f32[8,8,1152]{2,1,0:T(8,128)S(1)} %all-to-all-done.8.mine_ref), channel_id=1, source_target_pairs={{0,1},{1,0},{2,3},{3,2},{4,5},{5,4},{6,7},{7,6},{8,9},{9,8},{10,11... | collective-permute-start | bytes 884744 | tf_op jit(solution)/shard_map/ppermute | solution.py:180
  285.1 17.0 %collective-permute-start.24 = (f32[4,8,1024]{2,1,0:T(8,128)S(1)}, f32[4,8,1024]{2,1,0:T(8,128)S(1)}, u32[]{:S(2)}, u32[]{:S(2)}) collective-permute-start(f32[4,8,1024]{2,1,0:T(8,128)S(1)} %slice_bitcast_fusion), channel_id=1, source_target_pairs={{0,2},{2,0},{4,6},{6,4},{8,10},{10,8},{12,14},{14,12},{1,3},{3,1},... | collective-permute-start | bytes 393224 | tf_op jit(solution)/shard_map/ppermute | solution.py:180
  286.3 1.6 copy-start.7
  287.9 1.6 copy-start.12
  289.5 1.6 copy-start.17
  295.3 26.5 %all-to-all-start.9 = ((f32[16,8,2176]{2,1,0:T(8,128)}), f32[16,8,2176]{2,1,0:T(8,128)S(1)}, u32[]{:S(2)}, u32[]{:S(2)}) async-start(f32[16,8,2176]{2,1,0:T(8,128)} %shard_map.69), calls=%async_computation.9 | async-start | bytes 2228224 | tf_op jit(solution)/shard_map/all_to_all | solution.py:216
  302.1 6.1 %collective-permute-start.25 = (f32[2,8,1024]{2,1,0:T(8,128)S(1)}, f32[2,8,1024]{2,1,0:T(8,128)S(1)}, u32[]{:S(2)}, u32[]{:S(2)}) collective-permute-start(f32[2,8,1024]{2,1,0:T(8,128)S(1)} %slice_bitcast_fusion.8), channel_id=1, source_target_pairs={{0,4},{2,6},{4,0},{6,2},{8,12},{10,14},{12,8},{14,10},{1,5},{3,7},... | collective-permute-start | bytes 196616 | tf_op jit(solution)/shard_map/ppermute | solution.py:180
  308.2 7.4 %collective-permute-start.26 = (f32[1,8,1024]{2,1,0:T(8,128)S(1)}, f32[1,8,1024]{2,1,0:T(8,128)S(1)}, u32[]{:S(2)}, u32[]{:S(2)}) collective-permute-start(f32[1,8,1024]{2,1,0:T(8,128)S(1)} %slice_bitcast_fusion.16), channel_id=1, source_target_pairs={{0,8},{2,10},{4,12},{6,14},{8,0},{10,2},{12,4},{14,6},{1,9},{3,11}... | collective-permute-start | bytes 98312 | tf_op jit(solution)/shard_map/ppermute | solution.py:180
  315.7 6.1 %collective-permute-start.27 = (f32[8,1024]{1,0:T(8,128)S(1)}, f32[8,1024]{1,0:T(8,128)S(1)}, u32[]{:S(2)}, u32[]{:S(2)}) collective-permute-start(f32[8,1024]{1,0:T(8,128)S(1)} %fusion.16), channel_id=1, source_target_pairs={{0,0},{1,16},{2,32},{3,48},{4,64},{5,80},{6,96},{7,112},{8,128},{9... | collective-permute-start | bytes 98312 | tf_op jit(solution)/shard_map/ppermute | solution.py:192

commit v2 on v1

v2 whole, which is shorter than its diff:
```python
import functools
import math

import jax
import jax.numpy as jnp
import numpy as np
from jax import lax
from jax.experimental import pallas as pl
from jax.experimental.pallas import tpu as pltpu
from jax.sharding import Mesh
from jax.sharding import PartitionSpec as P

HIST = 16384
BLOCKS = 4
SIDE = 16
SLICE = 8
ROWS = SIDE * SLICE
WIDTH = 1024
LANES = 128
TILE = 256
COEFFICIENT = 1.0 / math.sqrt(HIST)

step_size = 0.2
heat_reservoir_warmth = 0.6

ROW = ("y", "x")
ALL = ("y", "x", "z", "core")


def around(a, b, size):
    return min((a - b) % size, (b - a) % size)


def pairs_of(b):
    def plane(i):
        return around(i // 4, b // 4, 4) + around(i % 4, b % 4, 4)

    rows = sorted(range(SIDE), key=lambda i: (-plane(i), i))
    cols = sorted(range(SIDE), key=lambda j: (around(j // 2, b // 2, 8), j))
    return dict(zip(rows, cols))


PAIRS = [pairs_of(b) for b in range(SIDE)]
KEPT = np.array([[PAIRS[b][i] for i in range(SIDE)] for b in range(SIDE)], np.int32)
KEEPER = np.argsort(KEPT, axis=1).astype(np.int32)
TO_LINE = [(i * SIDE + b, b * SIDE + int(KEPT[b, i])) for b in range(SIDE) for i in range(SIDE)]
TO_PLANE = [(line, plane) for plane, line in TO_LINE]
BY_CORE = np.array(
    [[2 * z + (c + k) % 2 for k in range(2) for z in range(SIDE // 2)] for c in range(SIDE)], np.int32
)
KEEPER_BY_CORE = np.take_along_axis(KEEPER, BY_CORE, axis=1)

f32, bf16 = jnp.float32, jnp.bfloat16


def kernel_call(body, outs, args, scratch=(), flops=0, prefetch=0):
    vmem = pl.BlockSpec(memory_space=pltpu.VMEM)
    smem = pl.BlockSpec(memory_space=pltpu.SMEM)
    size = sum(a.size * a.dtype.itemsize for a in args)
    return pl.pallas_call(
        body,
        out_shape=outs,
        in_specs=[smem] * prefetch + [vmem] * (len(args) - prefetch),
        out_specs=jax.tree.map(lambda _: vmem, outs),
        scratch_shapes=list(scratch),
        compiler_params=pltpu.CompilerParams(vmem_limit_bytes=8 * 1024 * 1024),
        cost_estimate=pl.CostEstimate(flops=flops, bytes_accessed=size, transcendentals=0),
    )(*args)


def shape(*dims, dtype=f32):
    return jax.ShapeDtypeStruct(dims, dtype)


def split(values):
    high = values.astype(bf16)
    low = (values - high.astype(f32)).astype(bf16)
    return high, low


def split_kernel(corr_ref, resp_ref, ch_ref, cl_ref, rh_ref, rl_ref):
    @pl.loop(0, WIDTH // LANES)
    def _(i):
        rows = pl.ds(pl.multiple_of(i * LANES, LANES), LANES)
        ch_ref[rows, :], cl_ref[rows, :] = split(corr_ref[rows, :])
        rh_ref[rows, :], rl_ref[rows, :] = split(resp_ref[rows, :])


def split_history(hist_corr, hist_resp):
    out = shape(WIDTH, WIDTH, dtype=bf16)
    return kernel_call(split_kernel, (out,) * 4, (hist_corr, hist_resp), flops=WIDTH * WIDTH)


def cross_kernel(order_ref, full_ref, rh_ref, rl_ref, keep_ref, give_ref, lhs_ref):
    half = SIDE // 2
    for slot in range(0, SIDE, 2):
        pair = [full_ref[order_ref[slot + k]] for k in range(2)]
        full = jnp.concatenate([p[:, :WIDTH] for p in pair], axis=0)
        high, low = split(1.5 * full * full)
        lhs_ref[slot * SLICE : (slot + 2) * SLICE] = high
        lhs_ref[ROWS + slot * SLICE : ROWS + (slot + 2) * SLICE] = low
        for k in range(2):
            out_ref = keep_ref if slot < half else give_ref
            out_ref[slot % half + k, :, WIDTH:] = pair[k][:, WIDTH:]
    dims = (((1,), (1,)), ((), ()))

    @pl.loop(0, WIDTH // TILE)
    def _(n):
        at = pl.ds(pl.multiple_of(n * TILE, TILE), TILE)
        both = lax.dot_general(lhs_ref[...], rh_ref[at, :], dims, preferred_element_type=f32)
        low = lax.dot_general(lhs_ref[:ROWS], rl_ref[at, :], dims, preferred_element_type=f32)
        total = (both[:ROWS] + (both[ROWS:] + low)).reshape(SIDE, SLICE, TILE)
        keep_ref[:, :, at] = total[:half]
        give_ref[:, :, at] = total[half:]


def cross_parts(order, full, resp_high, resp_low):
    out = shape(SIDE // 2, SLICE, WIDTH + LANES)
    return kernel_call(
        cross_kernel,
        (out, out),
        (order, full, resp_high, resp_low),
        scratch=(pltpu.VMEM((2 * ROWS, WIDTH), bf16),),
        flops=6 * ROWS * WIDTH * WIDTH,
        prefetch=1,
    )


def memory_kernel(
    order_ref, mine_ref, other_ref, ch_ref, cl_ref, rh_ref, rl_ref, out_ref, lhs_ref
):
    half = ROWS // 2
    for k, ref in enumerate((mine_ref, other_ref)):
        high, low = split(ref[...].reshape(half, WIDTH))
        lhs_ref[k * half : (k + 1) * half] = high
        lhs_ref[ROWS + k * half : ROWS + (k + 1) * half] = low
    for first, high_ref, low_ref in ((0, ch_ref, cl_ref), (WIDTH, rh_ref, rl_ref)):

        @pl.loop(0, WIDTH // TILE)
        def _(n):
            at = pl.ds(pl.multiple_of(n * TILE, TILE), TILE)
            to = pl.ds(pl.multiple_of(first + n * TILE, TILE), TILE)
            both = jnp.dot(lhs_ref[...], high_ref[:, at], preferred_element_type=f32)
            low = jnp.dot(lhs_ref[:ROWS], low_ref[:, at], preferred_element_type=f32)
            total = (both[:ROWS] + (both[ROWS:] + low)).reshape(SIDE, SLICE, TILE)
            for slot in range(SIDE):
                out_ref[order_ref[slot], :, to] = total[slot]


def memory_parts(order, mine, other, corr_high, corr_low, resp_high, resp_low):
    return kernel_call(
        memory_kernel,
        shape(SIDE, SLICE, 2 * WIDTH),
        (order, mine, other, corr_high, corr_low, resp_high, resp_low),
        scratch=(pltpu.VMEM((2 * ROWS, WIDTH), bf16),),
        flops=12 * ROWS * WIDTH * WIDTH,
        prefetch=1,
    )


def energy_and_terms(corr, resp):
    energy = 3.0 * corr * resp
    slope = 1.5 * corr * corr
    terms = jnp.sum(energy * corr + slope * resp, axis=-1, keepdims=True)
    return energy, jnp.broadcast_to(terms, corr.shape[:-1] + (LANES,))


def advance(pieces, cross, corr, resp):
    sums = jnp.sum(pieces, axis=0)
    memory_corr = sums[:, :WIDTH]
    memory_resp = sums[:, WIDTH:]
    multiplier = heat_reservoir_warmth + COEFFICIENT * cross[:, WIDTH : WIDTH + 1]
    return (
        corr + step_size * (COEFFICIENT * (memory_corr + cross[:, :WIDTH]) - multiplier * corr),
        resp + step_size * (COEFFICIENT * memory_resp - multiplier * resp),
    )


def advance_kernel(pieces_ref, cross_ref, corr_ref, resp_ref, c_ref, r_ref, e_ref, copies_ref):
    corr, resp = advance(pieces_ref[...], cross_ref[...], corr_ref[...], resp_ref[...])
    c_ref[...] = corr
    r_ref[...] = resp
    e_ref[...], terms = energy_and_terms(corr, resp)
    for j in range(SIDE):
        copies_ref[j, :, :WIDTH] = corr
        copies_ref[j, :, WIDTH:] = terms


def last_kernel(pieces_ref, cross_ref, corr_ref, resp_ref, copies_ref):
    corr, resp = advance(pieces_ref[...], cross_ref[...], corr_ref[...], resp_ref[...])
    for j in range(SIDE):
        copies_ref[j, :, :WIDTH] = corr
        copies_ref[j, :, WIDTH:] = resp


def unpack_kernel(keeper_ref, pieces_ref, corr_ref, resp_ref):
    for j in range(SIDE):
        piece = pieces_ref[keeper_ref[j]]
        corr_ref[j] = piece[:, :WIDTH]
        resp_ref[j] = piece[:, WIDTH:]


def swap(values):
    return lax.ppermute(values, "core", [(0, 1), (1, 0)])


def to_line(piece):
    return lax.ppermute(piece, ALL, TO_LINE)


def to_plane(piece):
    return lax.ppermute(piece, ALL, TO_PLANE)


def body(hist_corr, hist_resp, row_corr, row_resp):
    col = 2 * lax.axis_index("z") + lax.axis_index("core")

    def mine_of(table):
        return lax.dynamic_index_in_dim(jnp.asarray(table), col, keepdims=False)

    order = mine_of(KEEPER_BY_CORE)
    row_corr = row_corr.reshape(SIDE, SLICE, WIDTH)
    row_resp = row_resp.reshape(SIDE, SLICE, WIDTH)
    kept = lax.dynamic_index_in_dim(mine_of(KEPT), lax.axis_index(ROW), keepdims=False)
    corr = lax.dynamic_index_in_dim(row_corr, kept, keepdims=False)
    resp = lax.dynamic_index_in_dim(row_resp, kept, keepdims=False)
    energy, _ = energy_and_terms(corr, resp)
    _, terms = energy_and_terms(row_corr, row_resp)
    full = jnp.concatenate([row_corr, terms], axis=2)
    corr_high, corr_low, resp_high, resp_low = split_history(hist_corr, hist_resp)
    piece = shape(SLICE, WIDTH)
    for block_index in range(BLOCKS):
        if block_index:
            full = lax.all_to_all(copies, ROW, 0, 0, tiled=True)
        energy = to_line(energy)
        mine = lax.all_to_all(
            jnp.broadcast_to(energy[None], (SIDE // 2, SLICE, WIDTH)), "z", 0, 0, tiled=True
        )
        other = swap(mine)
        keep, give = cross_parts(
            order if block_index else mine_of(BY_CORE), full, resp_high, resp_low
        )
        cross = lax.all_to_all(keep + swap(give), "z", 0, 0, tiled=True)
        cross = to_plane(jnp.sum(cross, axis=0))
        parts = memory_parts(order, mine, other, corr_high, corr_low, resp_high, resp_low)
        pieces = lax.all_to_all(parts, ROW, 0, 0, tiled=True)
        if block_index < BLOCKS - 1:
            corr, resp, energy, copies = kernel_call(
                advance_kernel,
                (piece, piece, piece, shape(SIDE, SLICE, WIDTH + LANES)),
                (pieces, cross, corr, resp),
            )
        else:
            copies = kernel_call(
                last_kernel, shape(SIDE, SLICE, 2 * WIDTH), (pieces, cross, corr, resp)
            )
    final = lax.all_to_all(copies, ROW, 0, 0, tiled=True)
    out = shape(SIDE, SLICE, WIDTH)
    final_corr, final_resp = kernel_call(
        unpack_kernel, (out, out), (mine_of(KEEPER), final), prefetch=1
    )
    return (final_corr.reshape(ROWS, WIDTH), final_resp.reshape(ROWS, WIDTH))


def solution(mesh):
    split_mesh = Mesh(mesh.devices.reshape(4, 4, 8, 2), ALL)
    times = ("z", "core")
    in_specs = (P(ROW, times), P(ROW, times), P(None, times), P(None, times))
    out_specs = (P(None, times), P(None, times))
    return jax.shard_map(
        body, mesh=split_mesh, in_specs=in_specs, out_specs=out_specs, check_vma=False
    )
```

time: 352 us -> 339 us (0.963)
  blocking collectives: 25.1 us -> 0 us
  starting transfers between devices: 164 us -> 150 us
  local copies, waits for them, and re-layouts: 35.3 us -> 44.8 us
  waiting for transfers between devices: 83.9 us -> 92.8 us
  other arithmetic: 3.88 us -> 9.26 us
    all_to_all x1 -> x0, blocking collectives: 25.1 us -> none  [body(): lax.all_to_all(copies, ROW, 0, 0, tiled=True).reshape(ROWS, 2 * WIDTH)]
    all_to_all x4 -> x9, starting transfers between devices: 34 us -> 56.5 us  [the longest x4 26.6 us: body(): lax.all_to_all(jnp.broadcast_to(energy[None], (SIDE // 2, SLICE, WIDTH)),...]
    ppermute x28 -> x16, starting transfers between devices: 69.9 us -> 54.6 us  [the longest x4 20.8 us: to_plane(): return lax.ppermute(piece, ALL, TO_PLANE)]
    all_to_all x3, starting transfers between devices: 35.6 us -> 22.2 us  [body(): full = lax.all_to_all(copies, ROW, 0, 0, tiled=True)]
    unnamed x50 -> x54, local copies, waits for them, and re-layouts: 29.7 us -> 38.4 us
    all_to_all x4, waiting for transfers between devices: 0.01 us -> 7.99 us  [body(): pieces = lax.all_to_all(parts, ROW, 0, 0, tiled=True)]
    all_to_all x4 -> x9, waiting for transfers between devices: 13.8 us -> 21.7 us  [the longest x1 16.4 us: body(): final = lax.all_to_all(copies, ROW, 0, 0, tiled=True)]
    all_to_all x4, starting transfers between devices: 25 us -> 17.1 us  [body(): pieces = lax.all_to_all(parts, ROW, 0, 0, tiled=True)]
  transfers between devices with their start and end apart: 39 -> 32, of which waited for: 22 -> 24; matrix products, arithmetic and copies ran while one was open for 1% -> 3% of each run, Pallas kernels for 10% -> 9%
where the time goes in v2:
time: 339 us; the launch traced here: 334 us
  starting transfers between devices  150 us (44%)
  waiting for transfers between devices  92.8 us (27%)
  local copies, waits for them, and re-layouts  44.8 us (13%)
  Pallas kernels  33.7 us (10%)
  other arithmetic  9.26 us (3%)
    unnamed x54, local copies, waits for them, and re-layouts  38.4 us
    pallas_call x14, Pallas kernels, kernel_call(): pl.pallas_call(body, out_shape=outs, in_specs=[smem] * prefetch + [vmem]...  33.7 us
    ppermute x4, waiting for transfers between devices, to_plane(): return lax.ppermute(piece, ALL, TO_PLANE)  30.9 us
    all_to_all x4, starting transfers between devices, body(): lax.all_to_all(jnp.broadcast_to(energy[None], (SIDE // 2, SLICE, WIDTH)),...  26.6 us
    ppermute x4, waiting for transfers between devices, to_line(): return lax.ppermute(piece, ALL, TO_LINE)  23.4 us
    all_to_all x4, starting transfers between devices, body(): cross = lax.all_to_all(keep + swap(give), 'z', 0, 0, tiled=True)  22.4 us
    all_to_all x3, starting transfers between devices, body(): full = lax.all_to_all(copies, ROW, 0, 0, tiled=True)  22.2 us
    ppermute x4, starting transfers between devices, to_plane(): return lax.ppermute(piece, ALL, TO_PLANE)  20.8 us
  transfers between devices with their start and end apart: 32, of which 24 were waited for; matrix products, arithmetic and copies ran while one was open for 3% of the time, Pallas kernels for 9%

profile of v2, /device:TPU:1, one launch (start us, length us, event | category | flops | bytes accessed | tf_op | source)
XLA Modules:
  0.0 333.9 jit_solution(4833399808983131519)
XLA Ops:
  4.7 6.2 %collective-permute-start = (f32[8,1024]{1,0:T(8,128)S(1)}, f32[8,1024]{1,0:T(8,128)S(1)}, u32[]{:S(2)}, u32[]{:S(2)}) collective-permute-start(f32[8,1024]{1,0:T(8,128)S(1)} %get-tuple-element.54), channel_id=1, source_target_pairs={{0,9},{16,7},{32,15},{48,10},{64,11},{80,4},{96,1},{112,5},{128,12... | collective-permute-start | bytes 98312 | tf_op jit(solution)/shard_map/ppermute | solution.py:208
  13.5 2.2 copy-done.19
  15.7 2.2 copy-done.20
  24.2 7.6 %all-to-all-start = ((f32[8,8,1024]{2,1,0:T(8,128)}), f32[8,8,1024]{2,1,0:T(8,128)S(1)}, u32[]{:S(2)}, u32[]{:S(2)}) async-start(f32[8,8,1024]{2,1,0:T(8,128)} %broadcast_in_dim.12), calls=%async_computation | async-start | bytes 524288 | tf_op jit(solution)/shard_map/all_to_all | solution.py:236
  32.4 1.6 copy-done.1
  34.0 2.4 shard_map.97
  40.0 1.9 all-to-all-done.mine_ref
  41.9 5.0 %all-to-all-start.2 = ((f32[8,8,1152]{2,1,0:T(8,128)}), f32[8,8,1152]{2,1,0:T(8,128)S(1)}, u32[]{:S(2)}, u32[]{:S(2)}) async-start(f32[8,8,1152]{2,1,0:T(8,128)} %add.46), calls=%async_computation.2 | async-start | bytes 589824 | tf_op jit(solution)/shard_map/all_to_all | solution.py:243
  49.3 1.6 copy-done.2
  50.8 1.6 copy-done.10
  52.4 1.6 copy-done.15
  54.0 4.8 %shard_map.96 = f32[16,8,2048]{2,1,0:T(8,128)} custom-call(s32[16]{0:T(128)S(1)} %fusion.4.order_ref, f32[8,8,1024]{2,1,0:T(8,128)S(1)} %all-to-all-done.mine_ref, f32[8,8,1024]{2,1,0:T(8,128)S(1)} %collective-permute-done.1.other_ref, bf16[1024,1024]{1,0:T(8,128)(2,1)S(1)} %copy-done.10, bf16[1024,1024]{1,0:T(8,128)(2,1)S(1)} %copy-done.15, ...), custom_call_target="tpu_custom_call" | custom-call | flops 1610612736 | bytes 8912960 | tf_op jit(solution)/shard_map/pallas_call | solution.py:60
  59.5 6.2 %all-to-all-start.1 = ((f32[16,8,2048]{2,1,0:T(8,128)}), f32[16,8,2048]{2,1,0:T(8,128)S(1)}, u32[]{:S(2)}, u32[]{:S(2)}) async-start(f32[16,8,2048]{2,1,0:T(8,128)} %shard_map.96), calls=%async_computation.1 | async-start | bytes 2097152 | tf_op jit(solution)/shard_map/all_to_all | solution.py:246
  66.7 4.8 %collective-permute-start.3 = (f32[8,1152]{1,0:T(8,128)S(1)}, f32[8,1152]{1,0:T(8,128)S(1)}, u32[]{:S(2)}, u32[]{:S(2)}) collective-permute-start(f32[8,1152]{1,0:T(8,128)S(1)} %reduce_sum.46), channel_id=1, source_target_pairs={{9,0},{7,16},{15,32},{10,48},{11,64},{4,80},{1,96},{5,112},{12,128... | collective-permute-start | bytes 110600 | tf_op jit(solution)/shard_map/ppermute | solution.py:212
  71.5 8.7 %collective-permute-done.3.cross_ref = f32[8,1152]{1,0:T(8,128)S(1)} collective-permute-done((f32[8,1152]{1,0:T(8,128)S(1)}, f32[8,1152]{1,0:T(8,128)S(1)}, u32[]{:S(2)}, u32[]{:S(2)}) %collective-permute-start.3) | collective-permute-done | bytes 36896 | tf_op jit(solution)/shard_map/ppermute | solution.py:212
  80.2 1.8 all-to-all-done.1.pieces_ref
  83.0 7.1 %all-to-all-start.5 = ((f32[16,8,1152]{2,1,0:T(8,128)}), f32[16,8,1152]{2,1,0:T(8,128)S(1)}, u32[]{:S(2)}, u32[]{:S(2)}) async-start(f32[16,8,1152]{2,1,0:T(8,128)} %copy-done.21), calls=%async_computation.5 | async-start | bytes 1179648 | tf_op jit(solution)/shard_map/all_to_all | solution.py:234
  90.1 3.2 collective-permute-start.4
  93.3 9.9 %collective-permute-done.4 = f32[8,1024]{1,0:T(8,128)S(1)} collective-permute-done((f32[8,1024]{1,0:T(8,128)S(1)}, f32[8,1024]{1,0:T(8,128)S(1)}, u32[]{:S(2)}, u32[]{:S(2)}) %collective-permute-start.4) | collective-permute-done | bytes 32800 | tf_op jit(solution)/shard_map/ppermute | solution.py:208
  103.9 4.3 %all-to-all-start.3 = ((f32[8,8,1024]{2,1,0:T(8,128)}), f32[8,8,1024]{2,1,0:T(8,128)S(1)}, u32[]{:S(2)}, u32[]{:S(2)}) async-start(f32[8,8,1024]{2,1,0:T(8,128)} %broadcast_in_dim.15), calls=%async_computation.3 | async-start | bytes 524288 | tf_op jit(solution)/shard_map/all_to_all | solution.py:236
  108.2 1.6 copy-done.3
  109.8 2.4 shard_map.100
  112.3 2.0 collective-permute-start.6
  117.4 5.8 %all-to-all-start.6 = ((f32[8,8,1152]{2,1,0:T(8,128)}), f32[8,8,1152]{2,1,0:T(8,128)S(1)}, u32[]{:S(2)}, u32[]{:S(2)}) async-start(f32[8,8,1152]{2,1,0:T(8,128)} %add.47), calls=%async_computation.6 | async-start | bytes 589824 | tf_op jit(solution)/shard_map/all_to_all | solution.py:243
  125.8 1.6 copy-done.4
  127.3 1.6 copy-done.11
  128.9 1.6 copy-done.16
  130.5 4.8 %shard_map.99 = f32[16,8,2048]{2,1,0:T(8,128)} custom-call(s32[16]{0:T(128)S(1)} %fusion.4.order_ref, f32[8,8,1024]{2,1,0:T(8,128)S(1)} %all-to-all-done.3.mine_ref, f32[8,8,1024]{2,1,0:T(8,128)S(1)} %collective-permute-done.5.other_ref, bf16[1024,1024]{1,0:T(8,128)(2,1)S(1)} %copy-done.11, bf16[1024,1024]{1,0:T(8,128)(2,1)S(1)} %copy-done.16, ...), custom_call_target="tpu_custom_call" | custom-call | flops 1610612736 | bytes 8912960 | tf_op jit(solution)/shard_map/pallas_call | solution.py:60
  136.0 3.7 %all-to-all-start.4 = ((f32[16,8,2048]{2,1,0:T(8,128)}), f32[16,8,2048]{2,1,0:T(8,128)S(1)}, u32[]{:S(2)}, u32[]{:S(2)}) async-start(f32[16,8,2048]{2,1,0:T(8,128)} %shard_map.99), calls=%async_computation.4 | async-start | bytes 2097152 | tf_op jit(solution)/shard_map/all_to_all | solution.py:246
  140.7 5.3 %collective-permute-start.7 = (f32[8,1152]{1,0:T(8,128)S(1)}, f32[8,1152]{1,0:T(8,128)S(1)}, u32[]{:S(2)}, u32[]{:S(2)}) collective-permute-start(f32[8,1152]{1,0:T(8,128)S(1)} %reduce_sum.47), channel_id=1, source_target_pairs={{9,0},{7,16},{15,32},{10,48},{11,64},{4,80},{1,96},{5,112},{12,128... | collective-permute-start | bytes 110600 | tf_op jit(solution)/shard_map/ppermute | solution.py:212
  146.0 7.0 %collective-permute-done.7.cross_ref = f32[8,1152]{1,0:T(8,128)S(1)} collective-permute-done((f32[8,1152]{1,0:T(8,128)S(1)}, f32[8,1152]{1,0:T(8,128)S(1)}, u32[]{:S(2)}, u32[]{:S(2)}) %collective-permute-start.7) | collective-permute-done | bytes 36896 | tf_op jit(solution)/shard_map/ppermute | solution.py:212
  153.1 2.1 all-to-all-done.4.pieces_ref
  156.2 7.5 %all-to-all-start.9 = ((f32[16,8,1152]{2,1,0:T(8,128)}), f32[16,8,1152]{2,1,0:T(8,128)S(1)}, u32[]{:S(2)}, u32[]{:S(2)}) async-start(f32[16,8,1152]{2,1,0:T(8,128)} %copy-done.22), calls=%async_computation.9 | async-start | bytes 1179648 | tf_op jit(solution)/shard_map/all_to_all | solution.py:234
  163.7 5.7 %collective-permute-start.8 = (f32[8,1024]{1,0:T(8,128)S(1)}, f32[8,1024]{1,0:T(8,128)S(1)}, u32[]{:S(2)}, u32[]{:S(2)}) collective-permute-start(f32[8,1024]{1,0:T(8,128)S(1)} %get-tuple-element.40), channel_id=1, source_target_pairs={{0,9},{16,7},{32,15},{48,10},{64,11},{80,4},{96,1},{112,5},{128,12... | collective-permute-start | bytes 98312 | tf_op jit(solution)/shard_map/ppermute | solution.py:208
  169.4 6.7 %collective-permute-done.8 = f32[8,1024]{1,0:T(8,128)S(1)} collective-permute-done((f32[8,1024]{1,0:T(8,128)S(1)}, f32[8,1024]{1,0:T(8,128)S(1)}, u32[]{:S(2)}, u32[]{:S(2)}) %collective-permute-start.8) | collective-permute-done | bytes 32800 | tf_op jit(solution)/shard_map/ppermute | solution.py:208
  176.9 7.4 %all-to-all-start.7 = ((f32[8,8,1024]{2,1,0:T(8,128)}), f32[8,8,1024]{2,1,0:T(8,128)S(1)}, u32[]{:S(2)}, u32[]{:S(2)}) async-start(f32[8,8,1024]{2,1,0:T(8,128)} %broadcast_in_dim.16), calls=%async_computation.7 | async-start | bytes 524288 | tf_op jit(solution)/shard_map/all_to_all | solution.py:236
  185.8 2.4 shard_map.103
  188.3 2.0 collective-permute-start.10
  193.4 5.8 %all-to-all-start.10 = ((f32[8,8,1152]{2,1,0:T(8,128)}), f32[8,8,1152]{2,1,0:T(8,128)S(1)}, u32[]{:S(2)}, u32[]{:S(2)}) async-start(f32[8,8,1152]{2,1,0:T(8,128)} %add.48), calls=%async_computation.10 | async-start | bytes 589824 | tf_op jit(solution)/shard_map/all_to_all | solution.py:243
  201.8 1.6 copy-done.6
  203.4 1.6 copy-done.12
  205.0 1.6 copy-done.17
  206.5 4.8 %shard_map.102 = f32[16,8,2048]{2,1,0:T(8,128)} custom-call(s32[16]{0:T(128)S(1)} %fusion.4.order_ref, f32[8,8,1024]{2,1,0:T(8,128)S(1)} %all-to-all-done.7.mine_ref, f32[8,8,1024]{2,1,0:T(8,128)S(1)} %collective-permute-done.9.other_ref, bf16[1024,1024]{1,0:T(8,128)(2,1)S(1)} %copy-done.12, bf16[1024,1024]{1,0:T(8,128)(2,1)S(1)} %copy-done.17, ...), custom_call_target="tpu_custom_call" | custom-call | flops 1610612736 | bytes 8912960 | tf_op jit(solution)/shard_map/pallas_call | solution.py:60
  212.0 3.7 %all-to-all-start.8 = ((f32[16,8,2048]{2,1,0:T(8,128)}), f32[16,8,2048]{2,1,0:T(8,128)S(1)}, u32[]{:S(2)}, u32[]{:S(2)}) async-start(f32[16,8,2048]{2,1,0:T(8,128)} %shard_map.102), calls=%async_computation.8 | async-start | bytes 2097152 | tf_op jit(solution)/shard_map/all_to_all | solution.py:246
  216.7 5.4 %collective-permute-start.11 = (f32[8,1152]{1,0:T(8,128)S(1)}, f32[8,1152]{1,0:T(8,128)S(1)}, u32[]{:S(2)}, u32[]{:S(2)}) collective-permute-start(f32[8,1152]{1,0:T(8,128)S(1)} %reduce_sum.48), channel_id=1, source_target_pairs={{9,0},{7,16},{15,32},{10,48},{11,64},{4,80},{1,96},{5,112},{12,128... | collective-permute-start | bytes 110600 | tf_op jit(solution)/shard_map/ppermute | solution.py:212
  222.0 7.0 %collective-permute-done.11.cross_ref = f32[8,1152]{1,0:T(8,128)S(1)} collective-permute-done((f32[8,1152]{1,0:T(8,128)S(1)}, f32[8,1152]{1,0:T(8,128)S(1)}, u32[]{:S(2)}, u32[]{:S(2)}) %collective-permute-start.11) | collective-permute-done | bytes 36896 | tf_op jit(solution)/shard_map/ppermute | solution.py:212
  229.1 2.1 all-to-all-done.8.pieces_ref
  232.2 7.5 %all-to-all-start.13 = ((f32[16,8,1152]{2,1,0:T(8,128)}), f32[16,8,1152]{2,1,0:T(8,128)S(1)}, u32[]{:S(2)}, u32[]{:S(2)}) async-start(f32[16,8,1152]{2,1,0:T(8,128)} %copy-done.23), calls=%async_computation.13 | async-start | bytes 1179648 | tf_op jit(solution)/shard_map/all_to_all | solution.py:234
  239.7 5.7 %collective-permute-start.12 = (f32[8,1024]{1,0:T(8,128)S(1)}, f32[8,1024]{1,0:T(8,128)S(1)}, u32[]{:S(2)}, u32[]{:S(2)}) collective-permute-start(f32[8,1024]{1,0:T(8,128)S(1)} %get-tuple-element.46), channel_id=1, source_target_pairs={{0,9},{16,7},{32,15},{48,10},{64,11},{80,4},{96,1},{112,5},{128,12... | collective-permute-start | bytes 98312 | tf_op jit(solution)/shard_map/ppermute | solution.py:208
  245.4 6.8 %collective-permute-done.12 = f32[8,1024]{1,0:T(8,128)S(1)} collective-permute-done((f32[8,1024]{1,0:T(8,128)S(1)}, f32[8,1024]{1,0:T(8,128)S(1)}, u32[]{:S(2)}, u32[]{:S(2)}) %collective-permute-start.12) | collective-permute-done | bytes 32800 | tf_op jit(solution)/shard_map/ppermute | solution.py:208
  252.9 7.4 %all-to-all-start.11 = ((f32[8,8,1024]{2,1,0:T(8,128)}), f32[8,8,1024]{2,1,0:T(8,128)S(1)}, u32[]{:S(2)}, u32[]{:S(2)}) async-start(f32[8,8,1024]{2,1,0:T(8,128)} %broadcast_in_dim.17), calls=%async_computation.11 | async-start | bytes 524288 | tf_op jit(solution)/shard_map/all_to_all | solution.py:236
  261.9 2.4 shard_map.106
  264.3 2.0 collective-permute-start.14
  269.5 5.8 %all-to-all-start.14 = ((f32[8,8,1152]{2,1,0:T(8,128)}), f32[8,8,1152]{2,1,0:T(8,128)S(1)}, u32[]{:S(2)}, u32[]{:S(2)}) async-start(f32[8,8,1152]{2,1,0:T(8,128)} %add.49), calls=%async_computation.14 | async-start | bytes 589824 | tf_op jit(solution)/shard_map/all_to_all | solution.py:243
  277.8 1.6 copy-done.8
  279.4 1.6 copy-done.13
  281.0 1.6 copy-done.18
  282.6 4.8 %shard_map.105 = f32[16,8,2048]{2,1,0:T(8,128)} custom-call(s32[16]{0:T(128)S(1)} %fusion.4.order_ref, f32[8,8,1024]{2,1,0:T(8,128)S(1)} %all-to-all-done.11.mine_ref, f32[8,8,1024]{2,1,0:T(8,128)S(1)} %collective-permute-done.13.other_ref, bf16[1024,1024]{1,0:T(8,128)(2,1)S(1)} %copy-done.13, bf16[1024,1024]{1,0:T(8,128)(2,1)S(1)} %copy-done.18, ...), custom_call_target="tpu_custom_call" | custom-call | flops 1610612736 | bytes 8912960 | tf_op jit(solution)/shard_map/pallas_call | solution.py:60
  287.4 3.7 %all-to-all-start.12 = ((f32[16,8,2048]{2,1,0:T(8,128)}), f32[16,8,2048]{2,1,0:T(8,128)S(1)}, u32[]{:S(2)}, u32[]{:S(2)}) async-start(f32[16,8,2048]{2,1,0:T(8,128)} %shard_map.105), calls=%async_computation.12 | async-start | bytes 2097152 | tf_op jit(solution)/shard_map/all_to_all | solution.py:246
  291.1 5.3 %collective-permute-start.15 = (f32[8,1152]{1,0:T(8,128)S(1)}, f32[8,1152]{1,0:T(8,128)S(1)}, u32[]{:S(2)}, u32[]{:S(2)}) collective-permute-start(f32[8,1152]{1,0:T(8,128)S(1)} %reduce_sum.49), channel_id=1, source_target_pairs={{9,0},{7,16},{15,32},{10,48},{11,64},{4,80},{1,96},{5,112},{12,128... | collective-permute-start | bytes 110600 | tf_op jit(solution)/shard_map/ppermute | solution.py:212
  296.4 8.1 %collective-permute-done.15.cross_ref = f32[8,1152]{1,0:T(8,128)S(1)} collective-permute-done((f32[8,1152]{1,0:T(8,128)S(1)}, f32[8,1152]{1,0:T(8,128)S(1)}, u32[]{:S(2)}, u32[]{:S(2)}) %collective-permute-start.15) | collective-permute-done | bytes 36896 | tf_op jit(solution)/shard_map/ppermute | solution.py:212
  304.5 2.0 all-to-all-done.12.pieces_ref
  307.7 7.5 %all-to-all-start.15 = ((f32[16,8,2048]{2,1,0:T(8,128)}), f32[16,8,2048]{2,1,0:T(8,128)S(1)}, u32[]{:S(2)}, u32[]{:S(2)}) async-start(f32[16,8,2048]{2,1,0:T(8,128)} %shard_map.107), calls=%async_computation.15 | async-start | bytes 2097152 | tf_op jit(solution)/shard_map/all_to_all | solution.py:257
  316.0 16.4 %all-to-all-done.15.pieces_ref = f32[16,8,2048]{2,1,0:T(8,128)S(1)} async-done(((f32[16,8,2048]{2,1,0:T(8,128)}), f32[16,8,2048]{2,1,0:T(8,128)S(1)}, u32[]{:S(2)}, u32[]{:S(2)}) %all-to-all-start.15) | async-done | bytes 1048608 | tf_op jit(solution)/shard_map/all_to_all | solution.py:257
  (89 shorter events, 51.5 us)
Async XLA Ops:
  4.7 18.8 %collective-permute-start = (f32[8,1024]{1,0:T(8,128)S(1)}, f32[8,1024]{1,0:T(8,128)S(1)}, u32[]{:S(2)}, u32[]{:S(2)}) collective-permute-start(f32[8,1024]{1,0:T(8,128)S(1)} %get-tuple-element.54), channel_id=1, source_target_pairs={{0,9},{16,7},{32,15},{48,10},{64,11},{80,4},{96,1},{112,5},{128,12... | collective-permute-start | bytes 98312 | tf_op jit(solution)/shard_map/ppermute | solution.py:208
  13.5 2.2 copy-start.19
  15.7 2.2 copy-start.20
  19.4 1.4 copy-start
  20.8 1.3 copy-start.9
  22.1 1.3 copy-start.14
  24.2 17.7 %all-to-all-start = ((f32[8,8,1024]{2,1,0:T(8,128)}), f32[8,8,1024]{2,1,0:T(8,128)S(1)}, u32[]{:S(2)}, u32[]{:S(2)}) async-start(f32[8,8,1024]{2,1,0:T(8,128)} %broadcast_in_dim.12), calls=%async_computation | async-start | bytes 524288 | tf_op jit(solution)/shard_map/all_to_all | solution.py:236
  32.4 1.6 copy-start.1
  36.5 2.8 collective-permute-start.2
  41.9 16.9 %all-to-all-start.2 = ((f32[8,8,1152]{2,1,0:T(8,128)}), f32[8,8,1152]{2,1,0:T(8,128)S(1)}, u32[]{:S(2)}, u32[]{:S(2)}) async-start(f32[8,8,1152]{2,1,0:T(8,128)} %add.46), calls=%async_computation.2 | async-start | bytes 589824 | tf_op jit(solution)/shard_map/all_to_all | solution.py:243
  46.9 2.3 collective-permute-start.1
  49.3 1.6 copy-start.2
  50.8 1.6 copy-start.10
  52.4 1.6 copy-start.15
  58.8 0.7 copy-start.24
  59.5 22.4 %all-to-all-start.1 = ((f32[16,8,2048]{2,1,0:T(8,128)}), f32[16,8,2048]{2,1,0:T(8,128)S(1)}, u32[]{:S(2)}, u32[]{:S(2)}) async-start(f32[16,8,2048]{2,1,0:T(8,128)} %shard_map.96), calls=%async_computation.1 | async-start | bytes 2097152 | tf_op jit(solution)/shard_map/all_to_all | solution.py:246
  66.7 13.5 %collective-permute-start.3 = (f32[8,1152]{1,0:T(8,128)S(1)}, f32[8,1152]{1,0:T(8,128)S(1)}, u32[]{:S(2)}, u32[]{:S(2)}) collective-permute-start(f32[8,1152]{1,0:T(8,128)S(1)} %reduce_sum.46), channel_id=1, source_target_pairs={{9,0},{7,16},{15,32},{10,48},{11,64},{4,80},{1,96},{5,112},{12,128... | collective-permute-start | bytes 110600 | tf_op jit(solution)/shard_map/ppermute | solution.py:212
  82.1 0.8 copy-start.21
  83.0 20.2 %all-to-all-start.5 = ((f32[16,8,1152]{2,1,0:T(8,128)}), f32[16,8,1152]{2,1,0:T(8,128)S(1)}, u32[]{:S(2)}, u32[]{:S(2)}) async-start(f32[16,8,1152]{2,1,0:T(8,128)} %copy-done.21), calls=%async_computation.5 | async-start | bytes 1179648 | tf_op jit(solution)/shard_map/all_to_all | solution.py:234
  90.1 13.1 %collective-permute-start.4 = (f32[8,1024]{1,0:T(8,128)S(1)}, f32[8,1024]{1,0:T(8,128)S(1)}, u32[]{:S(2)}, u32[]{:S(2)}) collective-permute-start(f32[8,1024]{1,0:T(8,128)S(1)} %get-tuple-element.34), channel_id=1, source_target_pairs={{0,9},{16,7},{32,15},{48,10},{64,11},{80,4},{96,1},{112,5},{128,12... | collective-permute-start | bytes 98312 | tf_op jit(solution)/shard_map/ppermute | solution.py:208
  103.9 13.5 %all-to-all-start.3 = ((f32[8,8,1024]{2,1,0:T(8,128)}), f32[8,8,1024]{2,1,0:T(8,128)S(1)}, u32[]{:S(2)}, u32[]{:S(2)}) async-start(f32[8,8,1024]{2,1,0:T(8,128)} %broadcast_in_dim.15), calls=%async_computation.3 | async-start | bytes 524288 | tf_op jit(solution)/shard_map/all_to_all | solution.py:236
  108.2 1.6 copy-start.3
  112.3 3.2 collective-permute-start.6
  117.4 17.9 %all-to-all-start.6 = ((f32[8,8,1152]{2,1,0:T(8,128)}), f32[8,8,1152]{2,1,0:T(8,128)S(1)}, u32[]{:S(2)}, u32[]{:S(2)}) async-start(f32[8,8,1152]{2,1,0:T(8,128)} %add.47), calls=%async_computation.6 | async-start | bytes 589824 | tf_op jit(solution)/shard_map/all_to_all | solution.py:243
  123.2 2.6 collective-permute-start.5
  125.8 1.6 copy-start.4
  127.3 1.6 copy-start.11
  128.9 1.6 copy-start.16
  135.3 0.7 copy-start.25
  136.0 19.1 %all-to-all-start.4 = ((f32[16,8,2048]{2,1,0:T(8,128)}), f32[16,8,2048]{2,1,0:T(8,128)S(1)}, u32[]{:S(2)}, u32[]{:S(2)}) async-start(f32[16,8,2048]{2,1,0:T(8,128)} %shard_map.99), calls=%async_computation.4 | async-start | bytes 2097152 | tf_op jit(solution)/shard_map/all_to_all | solution.py:246
  140.7 12.4 %collective-permute-start.7 = (f32[8,1152]{1,0:T(8,128)S(1)}, f32[8,1152]{1,0:T(8,128)S(1)}, u32[]{:S(2)}, u32[]{:S(2)}) collective-permute-start(f32[8,1152]{1,0:T(8,128)S(1)} %reduce_sum.47), channel_id=1, source_target_pairs={{9,0},{7,16},{15,32},{10,48},{11,64},{4,80},{1,96},{5,112},{12,128... | collective-permute-start | bytes 110600 | tf_op jit(solution)/shard_map/ppermute | solution.py:212
  155.4 0.8 copy-start.22
  156.2 20.0 %all-to-all-start.9 = ((f32[16,8,1152]{2,1,0:T(8,128)}), f32[16,8,1152]{2,1,0:T(8,128)S(1)}, u32[]{:S(2)}, u32[]{:S(2)}) async-start(f32[16,8,1152]{2,1,0:T(8,128)} %copy-done.22), calls=%async_computation.9 | async-start | bytes 1179648 | tf_op jit(solution)/shard_map/all_to_all | solution.py:234
  163.7 12.4 %collective-permute-start.8 = (f32[8,1024]{1,0:T(8,128)S(1)}, f32[8,1024]{1,0:T(8,128)S(1)}, u32[]{:S(2)}, u32[]{:S(2)}) collective-permute-start(f32[8,1024]{1,0:T(8,128)S(1)} %get-tuple-element.40), channel_id=1, source_target_pairs={{0,9},{16,7},{32,15},{48,10},{64,11},{80,4},{96,1},{112,5},{128,12... | collective-permute-start | bytes 98312 | tf_op jit(solution)/shard_map/ppermute | solution.py:208
  176.9 16.5 %all-to-all-start.7 = ((f32[8,8,1024]{2,1,0:T(8,128)}), f32[8,8,1024]{2,1,0:T(8,128)S(1)}, u32[]{:S(2)}, u32[]{:S(2)}) async-start(f32[8,8,1024]{2,1,0:T(8,128)} %broadcast_in_dim.16), calls=%async_computation.7 | async-start | bytes 524288 | tf_op jit(solution)/shard_map/all_to_all | solution.py:236
  184.3 1.6 copy-start.5
  188.3 3.3 collective-permute-start.10
  193.4 17.9 %all-to-all-start.10 = ((f32[8,8,1152]{2,1,0:T(8,128)}), f32[8,8,1152]{2,1,0:T(8,128)S(1)}, u32[]{:S(2)}, u32[]{:S(2)}) async-start(f32[8,8,1152]{2,1,0:T(8,128)} %add.48), calls=%async_computation.10 | async-start | bytes 589824 | tf_op jit(solution)/shard_map/all_to_all | solution.py:243
  199.2 2.6 collective-permute-start.9
  201.8 1.6 copy-start.6
  203.4 1.6 copy-start.12
  205.0 1.6 copy-start.17
  211.3 0.7 copy-start.26
  212.0 19.1 %all-to-all-start.8 = ((f32[16,8,2048]{2,1,0:T(8,128)}), f32[16,8,2048]{2,1,0:T(8,128)S(1)}, u32[]{:S(2)}, u32[]{:S(2)}) async-start(f32[16,8,2048]{2,1,0:T(8,128)} %shard_map.102), calls=%async_computation.8 | async-start | bytes 2097152 | tf_op jit(solution)/shard_map/all_to_all | solution.py:246
  216.7 12.4 %collective-permute-start.11 = (f32[8,1152]{1,0:T(8,128)S(1)}, f32[8,1152]{1,0:T(8,128)S(1)}, u32[]{:S(2)}, u32[]{:S(2)}) collective-permute-start(f32[8,1152]{1,0:T(8,128)S(1)} %reduce_sum.48), channel_id=1, source_target_pairs={{9,0},{7,16},{15,32},{10,48},{11,64},{4,80},{1,96},{5,112},{12,128... | collective-permute-start | bytes 110600 | tf_op jit(solution)/shard_map/ppermute | solution.py:212
  231.4 0.8 copy-start.23
  232.2 20.0 %all-to-all-start.13 = ((f32[16,8,1152]{2,1,0:T(8,128)}), f32[16,8,1152]{2,1,0:T(8,128)S(1)}, u32[]{:S(2)}, u32[]{:S(2)}) async-start(f32[16,8,1152]{2,1,0:T(8,128)} %copy-done.23), calls=%async_computation.13 | async-start | bytes 1179648 | tf_op jit(solution)/shard_map/all_to_all | solution.py:234
  239.7 12.4 %collective-permute-start.12 = (f32[8,1024]{1,0:T(8,128)S(1)}, f32[8,1024]{1,0:T(8,128)S(1)}, u32[]{:S(2)}, u32[]{:S(2)}) collective-permute-start(f32[8,1024]{1,0:T(8,128)S(1)} %get-tuple-element.46), channel_id=1, source_target_pairs={{0,9},{16,7},{32,15},{48,10},{64,11},{80,4},{96,1},{112,5},{128,12... | collective-permute-start | bytes 98312 | tf_op jit(solution)/shard_map/ppermute | solution.py:208
  252.9 16.6 %all-to-all-start.11 = ((f32[8,8,1024]{2,1,0:T(8,128)}), f32[8,8,1024]{2,1,0:T(8,128)S(1)}, u32[]{:S(2)}, u32[]{:S(2)}) async-start(f32[8,8,1024]{2,1,0:T(8,128)} %broadcast_in_dim.17), calls=%async_computation.11 | async-start | bytes 524288 | tf_op jit(solution)/shard_map/all_to_all | solution.py:236
  260.3 1.6 copy-start.7
  264.3 3.3 collective-permute-start.14
  269.5 17.9 %all-to-all-start.14 = ((f32[8,8,1152]{2,1,0:T(8,128)}), f32[8,8,1152]{2,1,0:T(8,128)S(1)}, u32[]{:S(2)}, u32[]{:S(2)}) async-start(f32[8,8,1152]{2,1,0:T(8,128)} %add.49), calls=%async_computation.14 | async-start | bytes 589824 | tf_op jit(solution)/shard_map/all_to_all | solution.py:243
  275.2 2.5 collective-permute-start.13
  277.8 1.6 copy-start.8
  279.4 1.6 copy-start.13
  281.0 1.6 copy-start.18
  287.4 19.2 %all-to-all-start.12 = ((f32[16,8,2048]{2,1,0:T(8,128)}), f32[16,8,2048]{2,1,0:T(8,128)S(1)}, u32[]{:S(2)}, u32[]{:S(2)}) async-start(f32[16,8,2048]{2,1,0:T(8,128)} %shard_map.105), calls=%async_computation.12 | async-start | bytes 2097152 | tf_op jit(solution)/shard_map/all_to_all | solution.py:246
  291.1 13.4 %collective-permute-start.15 = (f32[8,1152]{1,0:T(8,128)S(1)}, f32[8,1152]{1,0:T(8,128)S(1)}, u32[]{:S(2)}, u32[]{:S(2)}) collective-permute-start(f32[8,1152]{1,0:T(8,128)S(1)} %reduce_sum.49), channel_id=1, source_target_pairs={{9,0},{7,16},{15,32},{10,48},{11,64},{4,80},{1,96},{5,112},{12,128... | collective-permute-start | bytes 110600 | tf_op jit(solution)/shard_map/ppermute | solution.py:212
  307.7 24.6 %all-to-all-start.15 = ((f32[16,8,2048]{2,1,0:T(8,128)}), f32[16,8,2048]{2,1,0:T(8,128)S(1)}, u32[]{:S(2)}, u32[]{:S(2)}) async-start(f32[16,8,2048]{2,1,0:T(8,128)} %shard_map.107), calls=%async_computation.15 | async-start | bytes 2097152 | tf_op jit(solution)/shard_map/all_to_all | solution.py:257

commit v3 on v2

--- a/solution.py
+++ b/solution.py
@@ -18,6 +18,9 @@
 WIDTH = 1024
 LANES = 128
 TILE = 256
+SMALL, LARGE = 8 * 2**20, 42 * 2**20
+HELD = 12
+TILES = WIDTH // TILE
 COEFFICIENT = 1.0 / math.sqrt(HIST)
 
 step_size = 0.2
@@ -53,17 +56,18 @@
 f32, bf16 = jnp.float32, jnp.bfloat16
 
 
-def kernel_call(body, outs, args, scratch=(), flops=0, prefetch=0):
+def kernel_call(body, outs, args, scratch=(), flops=0, scalars=0, history=0, far=False):
     vmem = pl.BlockSpec(memory_space=pltpu.VMEM)
     smem = pl.BlockSpec(memory_space=pltpu.SMEM)
+    hbm = pl.BlockSpec(memory_space=pltpu.HBM)
     size = sum(a.size * a.dtype.itemsize for a in args)
     return pl.pallas_call(
         body,
         out_shape=outs,
-        in_specs=[smem] * prefetch + [vmem] * (len(args) - prefetch),
-        out_specs=jax.tree.map(lambda _: vmem, outs),
+        in_specs=[smem] * scalars + [vmem] * (len(args) - scalars - history) + [hbm] * history,
+        out_specs=jax.tree.map(lambda _: hbm if far else vmem, outs),
         scratch_shapes=list(scratch),
-        compiler_params=pltpu.CompilerParams(vmem_limit_bytes=8 * 1024 * 1024),
+        compiler_params=pltpu.CompilerParams(vmem_limit_bytes=(LARGE if history or far else SMALL)),
         cost_estimate=pl.CostEstimate(flops=flops, bytes_accessed=size, transcendentals=0),
     )(*args)
 
@@ -78,20 +82,53 @@
     return high, low
 
 
-def split_kernel(corr_ref, resp_ref, ch_ref, cl_ref, rh_ref, rl_ref):
-    @pl.loop(0, WIDTH // LANES)
-    def _(i):
-        rows = pl.ds(pl.multiple_of(i * LANES, LANES), LANES)
-        ch_ref[rows, :], cl_ref[rows, :] = split(corr_ref[rows, :])
-        rh_ref[rows, :], rl_ref[rows, :] = split(resp_ref[rows, :])
+def split_kernel(corr, resp, out, read_ref, held_ref, read_sems, sems):
+    reads, copies = [], []
+    for n in range(TILES):
+        for k, history in enumerate((corr, resp)):
+            at = pl.ds(n * TILE, TILE)
+            reads.append(
+                pltpu.make_async_copy(
+                    history.at[at], read_ref.at[k, at], read_sems.at[k * TILES + n]
+                )
+            )
+            reads[-1].start()
+    for n in range(TILES):
+        at = slice(n * TILE, (n + 1) * TILE)
+        for k in range(2):
+            reads[2 * n + k].wait()
+            held_ref[2 * k, at], held_ref[2 * k + 1, at] = split(read_ref[k, at])
+        copies.append(pltpu.make_async_copy(held_ref.at[:, at], out.at[pl.ds(0, 4), at], sems.at[n]))
+        copies[-1].start()
+    for copy in copies:
+        copy.wait()
 
 
 def split_history(hist_corr, hist_resp):
-    out = shape(WIDTH, WIDTH, dtype=bf16)
-    return kernel_call(split_kernel, (out,) * 4, (hist_corr, hist_resp), flops=WIDTH * WIDTH)
-
-
-def cross_kernel(order_ref, full_ref, rh_ref, rl_ref, keep_ref, give_ref, lhs_ref):
+    return kernel_call(
+        split_kernel,
+        shape(HELD, WIDTH, WIDTH, dtype=bf16),
+        (hist_corr, hist_resp),
+        scratch=(
+            pltpu.VMEM((2, WIDTH, WIDTH), f32),
+            pltpu.VMEM((4, WIDTH, WIDTH), bf16),
+            pltpu.SemaphoreType.DMA((2 * TILES,)),
+            pltpu.SemaphoreType.DMA((TILES,)),
+        ),
+        flops=WIDTH * WIDTH,
+        history=2,
+        far=True,
+    )
+
+
+def cross_kernel(order_ref, full_ref, history, keep_ref, give_ref, lhs_ref, held_ref, sems):
+    copies = []
+    for n in range(TILES):
+        at = pl.ds(n * TILE, TILE)
+        copies.append(
+            pltpu.make_async_copy(history.at[pl.ds(2, 2), at], held_ref.at[:, at], sems.at[n])
+        )
+        copies[-1].start()
     half = SIDE // 2
     for slot in range(0, SIDE, 2):
         pair = [full_ref[order_ref[slot + k]] for k in range(2)]
@@ -103,58 +140,90 @@
             out_ref = keep_ref if slot < half else give_ref
             out_ref[slot % half + k, :, WIDTH:] = pair[k][:, WIDTH:]
     dims = (((1,), (1,)), ((), ()))
-
-    @pl.loop(0, WIDTH // TILE)
-    def _(n):
-        at = pl.ds(pl.multiple_of(n * TILE, TILE), TILE)
-        both = lax.dot_general(lhs_ref[...], rh_ref[at, :], dims, preferred_element_type=f32)
-        low = lax.dot_general(lhs_ref[:ROWS], rl_ref[at, :], dims, preferred_element_type=f32)
+    for n in range(TILES):
+        copies[n].wait()
+        at = slice(n * TILE, (n + 1) * TILE)
+        both = lax.dot_general(lhs_ref[...], held_ref[0, at], dims, preferred_element_type=f32)
+        low = lax.dot_general(lhs_ref[:ROWS], held_ref[1, at], dims, preferred_element_type=f32)
         total = (both[:ROWS] + (both[ROWS:] + low)).reshape(SIDE, SLICE, TILE)
         keep_ref[:, :, at] = total[:half]
         give_ref[:, :, at] = total[half:]
 
 
-def cross_parts(order, full, resp_high, resp_low):
+def cross_parts(order, full, history):
     out = shape(SIDE // 2, SLICE, WIDTH + LANES)
     return kernel_call(
         cross_kernel,
         (out, out),
-        (order, full, resp_high, resp_low),
-        scratch=(pltpu.VMEM((2 * ROWS, WIDTH), bf16),),
+        (order, full, history),
+        scratch=(
+            pltpu.VMEM((2 * ROWS, WIDTH), bf16),
+            pltpu.VMEM((2, WIDTH, WIDTH), bf16),
+            pltpu.SemaphoreType.DMA((TILES,)),
+        ),
         flops=6 * ROWS * WIDTH * WIDTH,
-        prefetch=1,
+        scalars=1,
+        history=1,
     )
 
 
 def memory_kernel(
-    order_ref, mine_ref, other_ref, ch_ref, cl_ref, rh_ref, rl_ref, out_ref, lhs_ref
+    order_ref, mine_ref, other_ref, history, out_hbm, lhs_ref, held_ref, out_ref, sems, out_sems
 ):
+    copies = []
+    for k in range(2):
+        for n in range(TILES):
+            at = pl.ds(n * TILE, TILE)
+            parts = pl.ds(2 * k, 2)
+            copies.append(
+                pltpu.make_async_copy(
+                    history.at[parts, :, at], held_ref.at[parts, :, at], sems.at[k * TILES + n]
+                )
+            )
+            copies[-1].start()
     half = ROWS // 2
     for k, ref in enumerate((mine_ref, other_ref)):
         high, low = split(ref[...].reshape(half, WIDTH))
         lhs_ref[k * half : (k + 1) * half] = high
         lhs_ref[ROWS + k * half : ROWS + (k + 1) * half] = low
-    for first, high_ref, low_ref in ((0, ch_ref, cl_ref), (WIDTH, rh_ref, rl_ref)):
-
-        @pl.loop(0, WIDTH // TILE)
-        def _(n):
-            at = pl.ds(pl.multiple_of(n * TILE, TILE), TILE)
-            to = pl.ds(pl.multiple_of(first + n * TILE, TILE), TILE)
-            both = jnp.dot(lhs_ref[...], high_ref[:, at], preferred_element_type=f32)
-            low = jnp.dot(lhs_ref[:ROWS], low_ref[:, at], preferred_element_type=f32)
+    results = []
+    for k in range(2):
+        for n in range(TILES):
+            copies[k * TILES + n].wait()
+            at = slice(n * TILE, (n + 1) * TILE)
+            both = jnp.dot(lhs_ref[...], held_ref[2 * k, :, at], preferred_element_type=f32)
+            low = jnp.dot(lhs_ref[:ROWS], held_ref[2 * k + 1, :, at], preferred_element_type=f32)
             total = (both[:ROWS] + (both[ROWS:] + low)).reshape(SIDE, SLICE, TILE)
+            to = k * WIDTH + n * TILE
             for slot in range(SIDE):
-                out_ref[order_ref[slot], :, to] = total[slot]
-
-
-def memory_parts(order, mine, other, corr_high, corr_low, resp_high, resp_low):
+                out_ref[order_ref[slot], :, to : to + TILE] = total[slot]
+            to = pl.ds(to, TILE)
+            results.append(
+                pltpu.make_async_copy(
+                    out_ref.at[:, :, to], out_hbm.at[:, :, to], out_sems.at[k * TILES + n]
+                )
+            )
+            results[-1].start()
+    for copy in results:
+        copy.wait()
+
+
+def memory_parts(order, mine, other, history):
     return kernel_call(
         memory_kernel,
         shape(SIDE, SLICE, 2 * WIDTH),
-        (order, mine, other, corr_high, corr_low, resp_high, resp_low),
-        scratch=(pltpu.VMEM((2 * ROWS, WIDTH), bf16),),
+        (order, mine, other, history),
+        scratch=(
+            pltpu.VMEM((2 * ROWS, WIDTH), bf16),
+            pltpu.VMEM((4, WIDTH, WIDTH), bf16),
+            pltpu.VMEM((SIDE, SLICE, 2 * WIDTH), f32),
+            pltpu.SemaphoreType.DMA((2 * TILES,)),
+            pltpu.SemaphoreType.DMA((2 * TILES,)),
+        ),
         flops=12 * ROWS * WIDTH * WIDTH,
-        prefetch=1,
+        scalars=1,
+        history=1,
+        far=True,
     )
 
 
@@ -210,6 +279,15 @@
 
 def to_plane(piece):
     return lax.ppermute(piece, ALL, TO_PLANE)
+
+
+def spread_kernel(energy_ref, copies_ref):
+    for z in range(SIDE // 2):
+        copies_ref[z] = energy_ref[...]
+
+
+def pass_kernel(cross_ref, out_ref):
+    out_ref[...] = cross_ref[...]
 
 
 def body(hist_corr, hist_resp, row_corr, row_resp):
@@ -227,7 +305,7 @@
     energy, _ = energy_and_terms(corr, resp)
     _, terms = energy_and_terms(row_corr, row_resp)
     full = jnp.concatenate([row_corr, terms], axis=2)
-    corr_high, corr_low, resp_high, resp_low = split_history(hist_corr, hist_resp)
+    history = split_history(hist_corr, hist_resp)
     piece = shape(SLICE, WIDTH)
     for block_index in range(BLOCKS):
         if block_index:
@@ -238,11 +316,11 @@
         )
         other = swap(mine)
         keep, give = cross_parts(
-            order if block_index else mine_of(BY_CORE), full, resp_high, resp_low
+            order if block_index else mine_of(BY_CORE), full, history
         )
         cross = lax.all_to_all(keep + swap(give), "z", 0, 0, tiled=True)
         cross = to_plane(jnp.sum(cross, axis=0))
-        parts = memory_parts(order, mine, other, corr_high, corr_low, resp_high, resp_low)
+        parts = memory_parts(order, mine, other, history)
         pieces = lax.all_to_all(parts, ROW, 0, 0, tiled=True)
         if block_index < BLOCKS - 1:
             corr, resp, energy, copies = kernel_call(
@@ -257,7 +335,7 @@
     final = lax.all_to_all(copies, ROW, 0, 0, tiled=True)
     out = shape(SIDE, SLICE, WIDTH)
     final_corr, final_resp = kernel_call(
-        unpack_kernel, (out, out), (mine_of(KEEPER), final), prefetch=1
+        unpack_kernel, (out, out), (mine_of(KEEPER), final), scalars=1
     )
     return (final_corr.reshape(ROWS, WIDTH), final_resp.reshape(ROWS, WIDTH))
 

time: 339 us -> 326 us (0.962)
  local copies, waits for them, and re-layouts: 44.8 us -> 10.8 us
  waiting for transfers between devices: 92.8 us -> 118 us
  Pallas kernels: 33.7 us -> 56.5 us
  starting transfers between devices: 150 us -> 130 us
    unnamed x54 -> x4, local copies, waits for them, and re-layouts: 38.4 us -> 4.37 us
    pallas_call x14, Pallas kernels: 33.7 us -> 56.5 us  [kernel_call(): pl.pallas_call(body, out_shape=outs, in_specs=[smem] * scalars + [vmem] *...]
    all_to_all x4, waiting for transfers between devices: 0.01 us -> 12.4 us  [body(): cross = lax.all_to_all(keep + swap(give), 'z', 0, 0, tiled=True)]
    ppermute x4, starting transfers between devices: 20.7 us -> 8.7 us  [to_line(): return lax.ppermute(piece, ALL, TO_LINE)]
    ppermute x4, waiting for transfers between devices: 23.4 us -> 35.3 us  [to_line(): return lax.ppermute(piece, ALL, TO_LINE)]
    all_to_all x4, starting transfers between devices: 26.6 us -> 18.7 us  [body(): lax.all_to_all(jnp.broadcast_to(energy[None], (SIDE // 2, SLICE, WIDTH)),...]
  transfers between devices with their start and end apart: 32 -> 32, of which waited for: 24 -> 28; matrix products, arithmetic and copies ran while one was open for 3% -> 2% of each run, Pallas kernels for 9% -> 16%
where the time goes in v3:
time: 326 us; the launch traced here: 324 us
  starting transfers between devices  130 us (40%)
  waiting for transfers between devices  118 us (36%)
  Pallas kernels  56.5 us (17%)
  local copies, waits for them, and re-layouts  10.8 us (3%)
  other arithmetic  6.36 us (2%)
    pallas_call x14, Pallas kernels, kernel_call(): pl.pallas_call(body, out_shape=outs, in_specs=[smem] * scalars + [vmem] *...  56.5 us
    ppermute x4, waiting for transfers between devices, to_line(): return lax.ppermute(piece, ALL, TO_LINE)  35.3 us
    ppermute x4, waiting for transfers between devices, to_plane(): return lax.ppermute(piece, ALL, TO_PLANE)  33.1 us
    all_to_all x4, starting transfers between devices, body(): cross = lax.all_to_all(keep + swap(give), 'z', 0, 0, tiled=True)  24.1 us
    all_to_all x3, starting transfers between devices, body(): full = lax.all_to_all(copies, ROW, 0, 0, tiled=True)  21.8 us
    ppermute x4, starting transfers between devices, to_plane(): return lax.ppermute(piece, ALL, TO_PLANE)  21.4 us
    all_to_all x4, starting transfers between devices, body(): lax.all_to_all(jnp.broadcast_to(energy[None], (SIDE // 2, SLICE, WIDTH)),...  18.7 us
    all_to_all x1, waiting for transfers between devices, body(): final = lax.all_to_all(copies, ROW, 0, 0, tiled=True)  16.8 us
  transfers between devices with their start and end apart: 32, of which 28 were waited for; matrix products, arithmetic and copies ran while one was open for 2% of the time, Pallas kernels for 16%

profile of v3, /device:TPU:1, one launch (start us, length us, event | category | flops | bytes accessed | tf_op | source)
XLA Modules:
  0.0 324.3 jit_solution(3435960953288536874)
XLA Ops:
  0.6 1.3 dynamic_slice.24
  4.7 6.2 %collective-permute-start = (f32[8,1024]{1,0:T(8,128)S(1)}, f32[8,1024]{1,0:T(8,128)S(1)}, u32[]{:S(2)}, u32[]{:S(2)}) collective-permute-start(f32[8,1024]{1,0:T(8,128)S(1)} %get-tuple-element.46), channel_id=1, source_target_pairs={{0,9},{16,7},{32,15},{48,10},{64,11},{80,4},{96,1},{112,5},{128,12... | collective-permute-start | bytes 98312 | tf_op jit(solution)/shard_map/ppermute | solution.py:277
  10.8 1.4 fusion.2
  13.5 2.2 copy-done
  15.7 2.2 copy-done.1
  17.9 4.2 %shard_map.95.history = bf16[12,1024,1024]{2,1,0:T(8,128)(2,1)} custom-call(f32[1024,1024]{1,0:T(8,128)S(1)} %copy-done, f32[1024,1024]{1,0:T(8,128)S(1)} %copy-done.1), custom_call_target="tpu_custom_call" | custom-call | flops 1048576 | bytes 8388608 | tf_op jit(solution)/shard_map/pallas_call | solution.py:64
  22.9 7.6 %all-to-all-start = ((f32[8,8,1024]{2,1,0:T(8,128)}), f32[8,8,1024]{2,1,0:T(8,128)S(1)}, u32[]{:S(2)}, u32[]{:S(2)}) async-start(f32[8,8,1024]{2,1,0:T(8,128)} %broadcast_in_dim.12), calls=%async_computation | async-start | bytes 524288 | tf_op jit(solution)/shard_map/all_to_all | solution.py:314
  31.1 4.6 %shard_map.97 = (f32[8,8,1152]{2,1,0:T(8,128)S(1)}, f32[8,8,1152]{2,1,0:T(8,128)S(1)}) custom-call(s32[16]{0:T(128)S(1)} %fusion.5.order_ref, f32[16,8,1152]{2,1,0:T(8,128)S(1)} %pad_maximum_fusion.full_ref, bf16[12,1024,1024]{2,1,0:T(8,128)(2,1)} %shard_map.95.history), custom_call_target="tpu_custom_call" | custom-call | flops 805306368 | bytes 25755712 | tf_op jit(solution)/shard_map/pallas_call | solution.py:64
  35.7 1.6 collective-permute-start.2
  37.3 1.2 collective-permute-done.2
  39.3 1.3 all-to-all-done.mine_ref
  40.6 5.6 %all-to-all-start.2 = ((f32[8,8,1152]{2,1,0:T(8,128)}), f32[8,8,1152]{2,1,0:T(8,128)S(1)}, u32[]{:S(2)}, u32[]{:S(2)}) async-start(f32[8,8,1152]{2,1,0:T(8,128)} %add.46), calls=%async_computation.2 | async-start | bytes 589824 | tf_op jit(solution)/shard_map/all_to_all | solution.py:321
  48.0 7.0 %shard_map.96 = f32[16,8,2048]{2,1,0:T(8,128)} custom-call(s32[16]{0:T(128)S(1)} %fusion.4.order_ref, f32[8,8,1024]{2,1,0:T(8,128)S(1)} %all-to-all-done.mine_ref, f32[8,8,1024]{2,1,0:T(8,128)S(1)} %collective-permute-done.1.other_ref, bf16[12,1024,1024]{2,1,0:T(8,128)(2,1)} %shard_map.95.history), custom_call_target="tpu_custom_call" | custom-call | flops 1610612736 | bytes 25690176 | tf_op jit(solution)/shard_map/pallas_call | solution.py:64
  55.1 3.5 %all-to-all-done.2 = f32[8,8,1152]{2,1,0:T(8,128)S(1)} async-done(((f32[8,8,1152]{2,1,0:T(8,128)}), f32[8,8,1152]{2,1,0:T(8,128)S(1)}, u32[]{:S(2)}, u32[]{:S(2)}) %all-to-all-start.2) | async-done | bytes 294944 | tf_op jit(solution)/shard_map/all_to_all | solution.py:321
  58.6 5.1 %all-to-all-start.1 = ((f32[16,8,2048]{2,1,0:T(8,128)}), f32[16,8,2048]{2,1,0:T(8,128)S(1)}, u32[]{:S(2)}, u32[]{:S(2)}) async-start(f32[16,8,2048]{2,1,0:T(8,128)} %shard_map.96), calls=%async_computation.1 | async-start | bytes 2097152 | tf_op jit(solution)/shard_map/all_to_all | solution.py:324
  63.7 4.8 %collective-permute-start.3 = (f32[8,1152]{1,0:T(8,128)S(1)}, f32[8,1152]{1,0:T(8,128)S(1)}, u32[]{:S(2)}, u32[]{:S(2)}) collective-permute-start(f32[8,1152]{1,0:T(8,128)S(1)} %reduce_sum.46), channel_id=1, source_target_pairs={{9,0},{7,16},{15,32},{10,48},{11,64},{4,80},{1,96},{5,112},{12,128... | collective-permute-start | bytes 110600 | tf_op jit(solution)/shard_map/ppermute | solution.py:281
  68.5 9.9 %collective-permute-done.3.cross_ref = f32[8,1152]{1,0:T(8,128)S(1)} collective-permute-done((f32[8,1152]{1,0:T(8,128)S(1)}, f32[8,1152]{1,0:T(8,128)S(1)}, u32[]{:S(2)}, u32[]{:S(2)}) %collective-permute-start.3) | collective-permute-done | bytes 36896 | tf_op jit(solution)/shard_map/ppermute | solution.py:281
  78.4 1.6 all-to-all-done.1.pieces_ref
  81.0 7.2 %all-to-all-start.5 = ((f32[16,8,1152]{2,1,0:T(8,128)}), f32[16,8,1152]{2,1,0:T(8,128)S(1)}, u32[]{:S(2)}, u32[]{:S(2)}) async-start(f32[16,8,1152]{2,1,0:T(8,128)} %get-tuple-element.27), calls=%async_computation.5 | async-start | bytes 1179648 | tf_op jit(solution)/shard_map/all_to_all | solution.py:312
  88.3 12.2 %collective-permute-done.4 = f32[8,1024]{1,0:T(8,128)S(1)} collective-permute-done((f32[8,1024]{1,0:T(8,128)S(1)}, f32[8,1024]{1,0:T(8,128)S(1)}, u32[]{:S(2)}, u32[]{:S(2)}) %collective-permute-start.4) | collective-permute-done | bytes 32800 | tf_op jit(solution)/shard_map/ppermute | solution.py:277
  101.3 3.4 %all-to-all-start.3 = ((f32[8,8,1024]{2,1,0:T(8,128)}), f32[8,8,1024]{2,1,0:T(8,128)S(1)}, u32[]{:S(2)}, u32[]{:S(2)}) async-start(f32[8,8,1024]{2,1,0:T(8,128)} %broadcast_in_dim.15), calls=%async_computation.3 | async-start | bytes 524288 | tf_op jit(solution)/shard_map/all_to_all | solution.py:314
  104.7 4.6 %shard_map.100 = (f32[8,8,1152]{2,1,0:T(8,128)S(1)}, f32[8,8,1152]{2,1,0:T(8,128)S(1)}) custom-call(s32[16]{0:T(128)S(1)} %fusion.4.order_ref, f32[16,8,1152]{2,1,0:T(8,128)S(1)} %all-to-all-done.5.full_ref, bf16[12,1024,1024]{2,1,0:T(8,128)(2,1)} %shard_map.95.history), custom_call_target="tpu_custom_call" | custom-call | flops 805306368 | bytes 25755712 | tf_op jit(solution)/shard_map/pallas_call | solution.py:64
  109.3 2.4 collective-permute-start.6
  111.7 1.2 collective-permute-done.6
  113.9 6.6 %all-to-all-start.6 = ((f32[8,8,1152]{2,1,0:T(8,128)}), f32[8,8,1152]{2,1,0:T(8,128)S(1)}, u32[]{:S(2)}, u32[]{:S(2)}) async-start(f32[8,8,1152]{2,1,0:T(8,128)} %add.47), calls=%async_computation.6 | async-start | bytes 589824 | tf_op jit(solution)/shard_map/all_to_all | solution.py:321
  121.1 1.2 collective-permute-done.5.other_ref
  122.3 7.0 %shard_map.99 = f32[16,8,2048]{2,1,0:T(8,128)} custom-call(s32[16]{0:T(128)S(1)} %fusion.4.order_ref, f32[8,8,1024]{2,1,0:T(8,128)S(1)} %all-to-all-done.3.mine_ref, f32[8,8,1024]{2,1,0:T(8,128)S(1)} %collective-permute-done.5.other_ref, bf16[12,1024,1024]{2,1,0:T(8,128)(2,1)} %shard_map.95.history), custom_call_target="tpu_custom_call" | custom-call | flops 1610612736 | bytes 25690176 | tf_op jit(solution)/shard_map/pallas_call | solution.py:64
  129.3 3.6 %all-to-all-done.6 = f32[8,8,1152]{2,1,0:T(8,128)S(1)} async-done(((f32[8,8,1152]{2,1,0:T(8,128)}), f32[8,8,1152]{2,1,0:T(8,128)S(1)}, u32[]{:S(2)}, u32[]{:S(2)}) %all-to-all-start.6) | async-done | bytes 294944 | tf_op jit(solution)/shard_map/all_to_all | solution.py:321
  132.9 3.7 %all-to-all-start.4 = ((f32[16,8,2048]{2,1,0:T(8,128)}), f32[16,8,2048]{2,1,0:T(8,128)S(1)}, u32[]{:S(2)}, u32[]{:S(2)}) async-start(f32[16,8,2048]{2,1,0:T(8,128)} %shard_map.99), calls=%async_computation.4 | async-start | bytes 2097152 | tf_op jit(solution)/shard_map/all_to_all | solution.py:324
  136.6 5.1 %collective-permute-start.7 = (f32[8,1152]{1,0:T(8,128)S(1)}, f32[8,1152]{1,0:T(8,128)S(1)}, u32[]{:S(2)}, u32[]{:S(2)}) collective-permute-start(f32[8,1152]{1,0:T(8,128)S(1)} %reduce_sum.47), channel_id=1, source_target_pairs={{9,0},{7,16},{15,32},{10,48},{11,64},{4,80},{1,96},{5,112},{12,128... | collective-permute-start | bytes 110600 | tf_op jit(solution)/shard_map/ppermute | solution.py:281
  141.6 8.6 %collective-permute-done.7.cross_ref = f32[8,1152]{1,0:T(8,128)S(1)} collective-permute-done((f32[8,1152]{1,0:T(8,128)S(1)}, f32[8,1152]{1,0:T(8,128)S(1)}, u32[]{:S(2)}, u32[]{:S(2)}) %collective-permute-start.7) | collective-permute-done | bytes 36896 | tf_op jit(solution)/shard_map/ppermute | solution.py:281
  150.2 2.1 all-to-all-done.4.pieces_ref
  153.3 7.2 %all-to-all-start.9 = ((f32[16,8,1152]{2,1,0:T(8,128)}), f32[16,8,1152]{2,1,0:T(8,128)S(1)}, u32[]{:S(2)}, u32[]{:S(2)}) async-start(f32[16,8,1152]{2,1,0:T(8,128)} %get-tuple-element.33), calls=%async_computation.9 | async-start | bytes 1179648 | tf_op jit(solution)/shard_map/all_to_all | solution.py:312
  160.6 1.2 collective-permute-start.8
  161.8 11.2 %collective-permute-done.8 = f32[8,1024]{1,0:T(8,128)S(1)} collective-permute-done((f32[8,1024]{1,0:T(8,128)S(1)}, f32[8,1024]{1,0:T(8,128)S(1)}, u32[]{:S(2)}, u32[]{:S(2)}) %collective-permute-start.8) | collective-permute-done | bytes 32800 | tf_op jit(solution)/shard_map/ppermute | solution.py:277
  173.7 4.3 %all-to-all-start.7 = ((f32[8,8,1024]{2,1,0:T(8,128)}), f32[8,8,1024]{2,1,0:T(8,128)S(1)}, u32[]{:S(2)}, u32[]{:S(2)}) async-start(f32[8,8,1024]{2,1,0:T(8,128)} %broadcast_in_dim.16), calls=%async_computation.7 | async-start | bytes 524288 | tf_op jit(solution)/shard_map/all_to_all | solution.py:314
  178.1 4.6 %shard_map.103 = (f32[8,8,1152]{2,1,0:T(8,128)S(1)}, f32[8,8,1152]{2,1,0:T(8,128)S(1)}) custom-call(s32[16]{0:T(128)S(1)} %fusion.4.order_ref, f32[16,8,1152]{2,1,0:T(8,128)S(1)} %all-to-all-done.9.full_ref, bf16[12,1024,1024]{2,1,0:T(8,128)(2,1)} %shard_map.95.history), custom_call_target="tpu_custom_call" | custom-call | flops 805306368 | bytes 25755712 | tf_op jit(solution)/shard_map/pallas_call | solution.py:64
  182.7 2.0 collective-permute-start.10
  184.7 1.2 collective-permute-done.10
  187.3 6.3 %all-to-all-start.10 = ((f32[8,8,1152]{2,1,0:T(8,128)}), f32[8,8,1152]{2,1,0:T(8,128)S(1)}, u32[]{:S(2)}, u32[]{:S(2)}) async-start(f32[8,8,1152]{2,1,0:T(8,128)} %add.48), calls=%async_computation.10 | async-start | bytes 589824 | tf_op jit(solution)/shard_map/all_to_all | solution.py:321
  195.6 7.0 %shard_map.102 = f32[16,8,2048]{2,1,0:T(8,128)} custom-call(s32[16]{0:T(128)S(1)} %fusion.4.order_ref, f32[8,8,1024]{2,1,0:T(8,128)S(1)} %all-to-all-done.7.mine_ref, f32[8,8,1024]{2,1,0:T(8,128)S(1)} %collective-permute-done.9.other_ref, bf16[12,1024,1024]{2,1,0:T(8,128)(2,1)} %shard_map.95.history), custom_call_target="tpu_custom_call" | custom-call | flops 1610612736 | bytes 25690176 | tf_op jit(solution)/shard_map/pallas_call | solution.py:64
  202.6 3.3 %all-to-all-done.10 = f32[8,8,1152]{2,1,0:T(8,128)S(1)} async-done(((f32[8,8,1152]{2,1,0:T(8,128)}), f32[8,8,1152]{2,1,0:T(8,128)S(1)}, u32[]{:S(2)}, u32[]{:S(2)}) %all-to-all-start.10) | async-done | bytes 294944 | tf_op jit(solution)/shard_map/all_to_all | solution.py:321
  205.9 3.7 %all-to-all-start.8 = ((f32[16,8,2048]{2,1,0:T(8,128)}), f32[16,8,2048]{2,1,0:T(8,128)S(1)}, u32[]{:S(2)}, u32[]{:S(2)}) async-start(f32[16,8,2048]{2,1,0:T(8,128)} %shard_map.102), calls=%async_computation.8 | async-start | bytes 2097152 | tf_op jit(solution)/shard_map/all_to_all | solution.py:324
  209.6 5.3 %collective-permute-start.11 = (f32[8,1152]{1,0:T(8,128)S(1)}, f32[8,1152]{1,0:T(8,128)S(1)}, u32[]{:S(2)}, u32[]{:S(2)}) collective-permute-start(f32[8,1152]{1,0:T(8,128)S(1)} %reduce_sum.48), channel_id=1, source_target_pairs={{9,0},{7,16},{15,32},{10,48},{11,64},{4,80},{1,96},{5,112},{12,128... | collective-permute-start | bytes 110600 | tf_op jit(solution)/shard_map/ppermute | solution.py:281
  215.0 8.3 %collective-permute-done.11.cross_ref = f32[8,1152]{1,0:T(8,128)S(1)} collective-permute-done((f32[8,1152]{1,0:T(8,128)S(1)}, f32[8,1152]{1,0:T(8,128)S(1)}, u32[]{:S(2)}, u32[]{:S(2)}) %collective-permute-start.11) | collective-permute-done | bytes 36896 | tf_op jit(solution)/shard_map/ppermute | solution.py:281
  223.2 2.1 all-to-all-done.8.pieces_ref
  226.3 7.3 %all-to-all-start.13 = ((f32[16,8,1152]{2,1,0:T(8,128)}), f32[16,8,1152]{2,1,0:T(8,128)S(1)}, u32[]{:S(2)}, u32[]{:S(2)}) async-start(f32[16,8,1152]{2,1,0:T(8,128)} %get-tuple-element.39), calls=%async_computation.13 | async-start | bytes 1179648 | tf_op jit(solution)/shard_map/all_to_all | solution.py:312
  233.7 1.2 collective-permute-start.12
  234.9 11.8 %collective-permute-done.12 = f32[8,1024]{1,0:T(8,128)S(1)} collective-permute-done((f32[8,1024]{1,0:T(8,128)S(1)}, f32[8,1024]{1,0:T(8,128)S(1)}, u32[]{:S(2)}, u32[]{:S(2)}) %collective-permute-start.12) | collective-permute-done | bytes 32800 | tf_op jit(solution)/shard_map/ppermute | solution.py:277
  247.4 3.4 %all-to-all-start.11 = ((f32[8,8,1024]{2,1,0:T(8,128)}), f32[8,8,1024]{2,1,0:T(8,128)S(1)}, u32[]{:S(2)}, u32[]{:S(2)}) async-start(f32[8,8,1024]{2,1,0:T(8,128)} %broadcast_in_dim.17), calls=%async_computation.11 | async-start | bytes 524288 | tf_op jit(solution)/shard_map/all_to_all | solution.py:314
  250.9 4.6 %shard_map.106 = (f32[8,8,1152]{2,1,0:T(8,128)S(1)}, f32[8,8,1152]{2,1,0:T(8,128)S(1)}) custom-call(s32[16]{0:T(128)S(1)} %fusion.4.order_ref, f32[16,8,1152]{2,1,0:T(8,128)S(1)} %all-to-all-done.13.full_ref, bf16[12,1024,1024]{2,1,0:T(8,128)(2,1)} %shard_map.95.history), custom_call_target="tpu_custom_call" | custom-call | flops 805306368 | bytes 25755712 | tf_op jit(solution)/shard_map/pallas_call | solution.py:64
  255.5 1.7 collective-permute-start.14
  257.2 1.2 collective-permute-done.14
  259.2 1.3 all-to-all-done.11.mine_ref
  260.5 5.6 %all-to-all-start.14 = ((f32[8,8,1152]{2,1,0:T(8,128)}), f32[8,8,1152]{2,1,0:T(8,128)S(1)}, u32[]{:S(2)}, u32[]{:S(2)}) async-start(f32[8,8,1152]{2,1,0:T(8,128)} %add.49), calls=%async_computation.14 | async-start | bytes 589824 | tf_op jit(solution)/shard_map/all_to_all | solution.py:321
  268.3 7.0 %shard_map.105 = f32[16,8,2048]{2,1,0:T(8,128)} custom-call(s32[16]{0:T(128)S(1)} %fusion.4.order_ref, f32[8,8,1024]{2,1,0:T(8,128)S(1)} %all-to-all-done.11.mine_ref, f32[8,8,1024]{2,1,0:T(8,128)S(1)} %collective-permute-done.13.other_ref, bf16[12,1024,1024]{2,1,0:T(8,128)(2,1)} %shard_map.95.history), custom_call_target="tpu_custom_call" | custom-call | flops 1610612736 | bytes 25690176 | tf_op jit(solution)/shard_map/pallas_call | solution.py:64
  275.3 2.0 all-to-all-done.14
  277.4 3.7 %all-to-all-start.12 = ((f32[16,8,2048]{2,1,0:T(8,128)}), f32[16,8,2048]{2,1,0:T(8,128)S(1)}, u32[]{:S(2)}, u32[]{:S(2)}) async-start(f32[16,8,2048]{2,1,0:T(8,128)} %shard_map.105), calls=%async_computation.12 | async-start | bytes 2097152 | tf_op jit(solution)/shard_map/all_to_all | solution.py:324
  281.1 6.2 %collective-permute-start.15 = (f32[8,1152]{1,0:T(8,128)S(1)}, f32[8,1152]{1,0:T(8,128)S(1)}, u32[]{:S(2)}, u32[]{:S(2)}) collective-permute-start(f32[8,1152]{1,0:T(8,128)S(1)} %reduce_sum.49), channel_id=1, source_target_pairs={{9,0},{7,16},{15,32},{10,48},{11,64},{4,80},{1,96},{5,112},{12,128... | collective-permute-start | bytes 110600 | tf_op jit(solution)/shard_map/ppermute | solution.py:281
  287.2 6.4 %collective-permute-done.15.cross_ref = f32[8,1152]{1,0:T(8,128)S(1)} collective-permute-done((f32[8,1152]{1,0:T(8,128)S(1)}, f32[8,1152]{1,0:T(8,128)S(1)}, u32[]{:S(2)}, u32[]{:S(2)}) %collective-permute-start.15) | collective-permute-done | bytes 36896 | tf_op jit(solution)/shard_map/ppermute | solution.py:281
  293.6 2.3 all-to-all-done.12.pieces_ref
  297.1 8.1 %all-to-all-start.15 = ((f32[16,8,2048]{2,1,0:T(8,128)}), f32[16,8,2048]{2,1,0:T(8,128)S(1)}, u32[]{:S(2)}, u32[]{:S(2)}) async-start(f32[16,8,2048]{2,1,0:T(8,128)} %shard_map.107), calls=%async_computation.15 | async-start | bytes 2097152 | tf_op jit(solution)/shard_map/all_to_all | solution.py:335
  305.9 16.8 %all-to-all-done.15.pieces_ref = f32[16,8,2048]{2,1,0:T(8,128)S(1)} async-done(((f32[16,8,2048]{2,1,0:T(8,128)}), f32[16,8,2048]{2,1,0:T(8,128)S(1)}, u32[]{:S(2)}, u32[]{:S(2)}) %all-to-all-start.15) | async-done | bytes 1048608 | tf_op jit(solution)/shard_map/all_to_all | solution.py:335
  322.7 1.6 shard_map.108
  (39 shorter events, 21.3 us)
Async XLA Ops:
  4.7 17.5 %collective-permute-start = (f32[8,1024]{1,0:T(8,128)S(1)}, f32[8,1024]{1,0:T(8,128)S(1)}, u32[]{:S(2)}, u32[]{:S(2)}) collective-permute-start(f32[8,1024]{1,0:T(8,128)S(1)} %get-tuple-element.46), channel_id=1, source_target_pairs={{0,9},{16,7},{32,15},{48,10},{64,11},{80,4},{96,1},{112,5},{128,12... | collective-permute-start | bytes 98312 | tf_op jit(solution)/shard_map/ppermute | solution.py:277
  13.5 2.2 copy-start
  15.7 2.2 copy-start.1
  22.9 17.7 %all-to-all-start = ((f32[8,8,1024]{2,1,0:T(8,128)}), f32[8,8,1024]{2,1,0:T(8,128)S(1)}, u32[]{:S(2)}, u32[]{:S(2)}) async-start(f32[8,8,1024]{2,1,0:T(8,128)} %broadcast_in_dim.12), calls=%async_computation | async-start | bytes 524288 | tf_op jit(solution)/shard_map/all_to_all | solution.py:314
  35.7 2.8 collective-permute-start.2
  40.6 18.0 %all-to-all-start.2 = ((f32[8,8,1152]{2,1,0:T(8,128)}), f32[8,8,1152]{2,1,0:T(8,128)S(1)}, u32[]{:S(2)}, u32[]{:S(2)}) async-start(f32[8,8,1152]{2,1,0:T(8,128)} %add.46), calls=%async_computation.2 | async-start | bytes 589824 | tf_op jit(solution)/shard_map/all_to_all | solution.py:321
  46.2 1.8 collective-permute-start.1
  58.6 21.3 %all-to-all-start.1 = ((f32[16,8,2048]{2,1,0:T(8,128)}), f32[16,8,2048]{2,1,0:T(8,128)S(1)}, u32[]{:S(2)}, u32[]{:S(2)}) async-start(f32[16,8,2048]{2,1,0:T(8,128)} %shard_map.96), calls=%async_computation.1 | async-start | bytes 2097152 | tf_op jit(solution)/shard_map/all_to_all | solution.py:324
  63.7 14.6 %collective-permute-start.3 = (f32[8,1152]{1,0:T(8,128)S(1)}, f32[8,1152]{1,0:T(8,128)S(1)}, u32[]{:S(2)}, u32[]{:S(2)}) collective-permute-start(f32[8,1152]{1,0:T(8,128)S(1)} %reduce_sum.46), channel_id=1, source_target_pairs={{9,0},{7,16},{15,32},{10,48},{11,64},{4,80},{1,96},{5,112},{12,128... | collective-permute-start | bytes 110600 | tf_op jit(solution)/shard_map/ppermute | solution.py:281
  81.0 19.6 %all-to-all-start.5 = ((f32[16,8,1152]{2,1,0:T(8,128)}), f32[16,8,1152]{2,1,0:T(8,128)S(1)}, u32[]{:S(2)}, u32[]{:S(2)}) async-start(f32[16,8,1152]{2,1,0:T(8,128)} %get-tuple-element.27), calls=%async_computation.5 | async-start | bytes 1179648 | tf_op jit(solution)/shard_map/all_to_all | solution.py:312
  88.2 12.3 %collective-permute-start.4 = (f32[8,1024]{1,0:T(8,128)S(1)}, f32[8,1024]{1,0:T(8,128)S(1)}, u32[]{:S(2)}, u32[]{:S(2)}) collective-permute-start(f32[8,1024]{1,0:T(8,128)S(1)} %get-tuple-element.26), channel_id=1, source_target_pairs={{0,9},{16,7},{32,15},{48,10},{64,11},{80,4},{96,1},{112,5},{128,12... | collective-permute-start | bytes 98312 | tf_op jit(solution)/shard_map/ppermute | solution.py:277
  101.3 12.6 %all-to-all-start.3 = ((f32[8,8,1024]{2,1,0:T(8,128)}), f32[8,8,1024]{2,1,0:T(8,128)S(1)}, u32[]{:S(2)}, u32[]{:S(2)}) async-start(f32[8,8,1024]{2,1,0:T(8,128)} %broadcast_in_dim.15), calls=%async_computation.3 | async-start | bytes 524288 | tf_op jit(solution)/shard_map/all_to_all | solution.py:314
  109.3 3.6 %collective-permute-start.6 = (f32[8,8,1152]{2,1,0:T(8,128)S(1)}, f32[8,8,1152]{2,1,0:T(8,128)S(1)}, u32[]{:S(2)}, u32[]{:S(2)}) collective-permute-start(f32[8,8,1152]{2,1,0:T(8,128)S(1)} %get-tuple-element.29), channel_id=1, source_target_pairs={{0,1},{1,0},{2,3},{3,2},{4,5},{5,4},{6,7},{7,6},{8,9},{9,8},{10,11... | collective-permute-start | bytes 884744 | tf_op jit(solution)/shard_map/ppermute | solution.py:273
  113.9 19.0 %all-to-all-start.6 = ((f32[8,8,1152]{2,1,0:T(8,128)}), f32[8,8,1152]{2,1,0:T(8,128)S(1)}, u32[]{:S(2)}, u32[]{:S(2)}) async-start(f32[8,8,1152]{2,1,0:T(8,128)} %add.47), calls=%async_computation.6 | async-start | bytes 589824 | tf_op jit(solution)/shard_map/all_to_all | solution.py:321
  120.5 1.8 collective-permute-start.5
  132.9 19.4 %all-to-all-start.4 = ((f32[16,8,2048]{2,1,0:T(8,128)}), f32[16,8,2048]{2,1,0:T(8,128)S(1)}, u32[]{:S(2)}, u32[]{:S(2)}) async-start(f32[16,8,2048]{2,1,0:T(8,128)} %shard_map.99), calls=%async_computation.4 | async-start | bytes 2097152 | tf_op jit(solution)/shard_map/all_to_all | solution.py:324
  136.6 13.7 %collective-permute-start.7 = (f32[8,1152]{1,0:T(8,128)S(1)}, f32[8,1152]{1,0:T(8,128)S(1)}, u32[]{:S(2)}, u32[]{:S(2)}) collective-permute-start(f32[8,1152]{1,0:T(8,128)S(1)} %reduce_sum.47), channel_id=1, source_target_pairs={{9,0},{7,16},{15,32},{10,48},{11,64},{4,80},{1,96},{5,112},{12,128... | collective-permute-start | bytes 110600 | tf_op jit(solution)/shard_map/ppermute | solution.py:281
  153.3 19.7 %all-to-all-start.9 = ((f32[16,8,1152]{2,1,0:T(8,128)}), f32[16,8,1152]{2,1,0:T(8,128)S(1)}, u32[]{:S(2)}, u32[]{:S(2)}) async-start(f32[16,8,1152]{2,1,0:T(8,128)} %get-tuple-element.33), calls=%async_computation.9 | async-start | bytes 1179648 | tf_op jit(solution)/shard_map/all_to_all | solution.py:312
  160.6 12.4 %collective-permute-start.8 = (f32[8,1024]{1,0:T(8,128)S(1)}, f32[8,1024]{1,0:T(8,128)S(1)}, u32[]{:S(2)}, u32[]{:S(2)}) collective-permute-start(f32[8,1024]{1,0:T(8,128)S(1)} %get-tuple-element.32), channel_id=1, source_target_pairs={{0,9},{16,7},{32,15},{48,10},{64,11},{80,4},{96,1},{112,5},{128,12... | collective-permute-start | bytes 98312 | tf_op jit(solution)/shard_map/ppermute | solution.py:277
  173.7 13.5 %all-to-all-start.7 = ((f32[8,8,1024]{2,1,0:T(8,128)}), f32[8,8,1024]{2,1,0:T(8,128)S(1)}, u32[]{:S(2)}, u32[]{:S(2)}) async-start(f32[8,8,1024]{2,1,0:T(8,128)} %broadcast_in_dim.16), calls=%async_computation.7 | async-start | bytes 524288 | tf_op jit(solution)/shard_map/all_to_all | solution.py:314
  182.7 3.3 %collective-permute-start.10 = (f32[8,8,1152]{2,1,0:T(8,128)S(1)}, f32[8,8,1152]{2,1,0:T(8,128)S(1)}, u32[]{:S(2)}, u32[]{:S(2)}) collective-permute-start(f32[8,8,1152]{2,1,0:T(8,128)S(1)} %get-tuple-element.35), channel_id=1, source_target_pairs={{0,1},{1,0},{2,3},{3,2},{4,5},{5,4},{6,7},{7,6},{8,9},{9,8},{10,11... | collective-permute-start | bytes 884744 | tf_op jit(solution)/shard_map/ppermute | solution.py:273
  187.3 18.7 %all-to-all-start.10 = ((f32[8,8,1152]{2,1,0:T(8,128)}), f32[8,8,1152]{2,1,0:T(8,128)S(1)}, u32[]{:S(2)}, u32[]{:S(2)}) async-start(f32[8,8,1152]{2,1,0:T(8,128)} %add.48), calls=%async_computation.10 | async-start | bytes 589824 | tf_op jit(solution)/shard_map/all_to_all | solution.py:321
  193.6 2.0 collective-permute-start.9
  205.9 19.4 %all-to-all-start.8 = ((f32[16,8,2048]{2,1,0:T(8,128)}), f32[16,8,2048]{2,1,0:T(8,128)S(1)}, u32[]{:S(2)}, u32[]{:S(2)}) async-start(f32[16,8,2048]{2,1,0:T(8,128)} %shard_map.102), calls=%async_computation.8 | async-start | bytes 2097152 | tf_op jit(solution)/shard_map/all_to_all | solution.py:324
  209.6 13.6 %collective-permute-start.11 = (f32[8,1152]{1,0:T(8,128)S(1)}, f32[8,1152]{1,0:T(8,128)S(1)}, u32[]{:S(2)}, u32[]{:S(2)}) collective-permute-start(f32[8,1152]{1,0:T(8,128)S(1)} %reduce_sum.48), channel_id=1, source_target_pairs={{9,0},{7,16},{15,32},{10,48},{11,64},{4,80},{1,96},{5,112},{12,128... | collective-permute-start | bytes 110600 | tf_op jit(solution)/shard_map/ppermute | solution.py:281
  226.3 20.4 %all-to-all-start.13 = ((f32[16,8,1152]{2,1,0:T(8,128)}), f32[16,8,1152]{2,1,0:T(8,128)S(1)}, u32[]{:S(2)}, u32[]{:S(2)}) async-start(f32[16,8,1152]{2,1,0:T(8,128)} %get-tuple-element.39), calls=%async_computation.13 | async-start | bytes 1179648 | tf_op jit(solution)/shard_map/all_to_all | solution.py:312
  233.7 13.1 %collective-permute-start.12 = (f32[8,1024]{1,0:T(8,128)S(1)}, f32[8,1024]{1,0:T(8,128)S(1)}, u32[]{:S(2)}, u32[]{:S(2)}) collective-permute-start(f32[8,1024]{1,0:T(8,128)S(1)} %get-tuple-element.38), channel_id=1, source_target_pairs={{0,9},{16,7},{32,15},{48,10},{64,11},{80,4},{96,1},{112,5},{128,12... | collective-permute-start | bytes 98312 | tf_op jit(solution)/shard_map/ppermute | solution.py:277
  247.4 13.0 %all-to-all-start.11 = ((f32[8,8,1024]{2,1,0:T(8,128)}), f32[8,8,1024]{2,1,0:T(8,128)S(1)}, u32[]{:S(2)}, u32[]{:S(2)}) async-start(f32[8,8,1024]{2,1,0:T(8,128)} %broadcast_in_dim.17), calls=%async_computation.11 | async-start | bytes 524288 | tf_op jit(solution)/shard_map/all_to_all | solution.py:314
  255.5 2.9 collective-permute-start.14
  260.5 16.9 %all-to-all-start.14 = ((f32[8,8,1152]{2,1,0:T(8,128)}), f32[8,8,1152]{2,1,0:T(8,128)S(1)}, u32[]{:S(2)}, u32[]{:S(2)}) async-start(f32[8,8,1152]{2,1,0:T(8,128)} %add.49), calls=%async_computation.14 | async-start | bytes 589824 | tf_op jit(solution)/shard_map/all_to_all | solution.py:321
  266.1 2.2 collective-permute-start.13
  277.4 18.6 %all-to-all-start.12 = ((f32[16,8,2048]{2,1,0:T(8,128)}), f32[16,8,2048]{2,1,0:T(8,128)S(1)}, u32[]{:S(2)}, u32[]{:S(2)}) async-start(f32[16,8,2048]{2,1,0:T(8,128)} %shard_map.105), calls=%async_computation.12 | async-start | bytes 2097152 | tf_op jit(solution)/shard_map/all_to_all | solution.py:324
  281.1 12.6 %collective-permute-start.15 = (f32[8,1152]{1,0:T(8,128)S(1)}, f32[8,1152]{1,0:T(8,128)S(1)}, u32[]{:S(2)}, u32[]{:S(2)}) collective-permute-start(f32[8,1152]{1,0:T(8,128)S(1)} %reduce_sum.49), channel_id=1, source_target_pairs={{9,0},{7,16},{15,32},{10,48},{11,64},{4,80},{1,96},{5,112},{12,128... | collective-permute-start | bytes 110600 | tf_op jit(solution)/shard_map/ppermute | solution.py:281
  297.1 25.6 %all-to-all-start.15 = ((f32[16,8,2048]{2,1,0:T(8,128)}), f32[16,8,2048]{2,1,0:T(8,128)S(1)}, u32[]{:S(2)}, u32[]{:S(2)}) async-start(f32[16,8,2048]{2,1,0:T(8,128)} %shard_map.107), calls=%async_computation.15 | async-start | bytes 2097152 | tf_op jit(solution)/shard_map/all_to_all | solution.py:335

commit v4 on v3

--- a/solution.py
+++ b/solution.py
@@ -17,7 +17,7 @@
 ROWS = SIDE * SLICE
 WIDTH = 1024
 LANES = 128
-TILE = 256
+TILE = 512
 SMALL, LARGE = 8 * 2**20, 42 * 2**20
 HELD = 12
 TILES = WIDTH // TILE
@@ -56,7 +56,7 @@
 f32, bf16 = jnp.float32, jnp.bfloat16
 
 
-def kernel_call(body, outs, args, scratch=(), flops=0, scalars=0, history=0, far=False):
+def kernel_call(body, outs, args, scratch=(), flops=0, scalars=0, history=0, far=False, limit=SMALL):
     vmem = pl.BlockSpec(memory_space=pltpu.VMEM)
     smem = pl.BlockSpec(memory_space=pltpu.SMEM)
     hbm = pl.BlockSpec(memory_space=pltpu.HBM)
@@ -67,7 +67,7 @@
         in_specs=[smem] * scalars + [vmem] * (len(args) - scalars - history) + [hbm] * history,
         out_specs=jax.tree.map(lambda _: hbm if far else vmem, outs),
         scratch_shapes=list(scratch),
-        compiler_params=pltpu.CompilerParams(vmem_limit_bytes=(LARGE if history or far else SMALL)),
+        compiler_params=pltpu.CompilerParams(vmem_limit_bytes=limit),
         cost_estimate=pl.CostEstimate(flops=flops, bytes_accessed=size, transcendentals=0),
     )(*args)
 
@@ -118,6 +118,7 @@
         flops=WIDTH * WIDTH,
         history=2,
         far=True,
+        limit=58 * 2**20,
     )
 
 
@@ -164,6 +165,7 @@
         flops=6 * ROWS * WIDTH * WIDTH,
         scalars=1,
         history=1,
+        limit=LARGE,
     )
 
 
@@ -224,6 +226,7 @@
         scalars=1,
         history=1,
         far=True,
+        limit=LARGE,
     )
 
 

time: 326 us -> 320 us (0.982)
  Pallas kernels: 56.5 us -> 48.2 us
  starting transfers between devices: 130 us -> 135 us
  local copies, waits for them, and re-layouts: 10.8 us -> 6.41 us
    pallas_call x14, Pallas kernels: 56.5 us -> 48.2 us  [kernel_call(): pl.pallas_call(body, out_shape=outs, in_specs=[smem] * scalars + [vmem] *...]
    all_to_all x4, starting transfers between devices: 16 us -> 24.3 us  [body(): pieces = lax.all_to_all(parts, ROW, 0, 0, tiled=True)]
    all_to_all x4, starting transfers between devices: 24.1 us -> 18.6 us  [body(): cross = lax.all_to_all(keep + swap(give), 'z', 0, 0, tiled=True)]
    all_to_all x4, waiting for transfers between devices: 3.49 us -> 8.84 us  [body(): lax.all_to_all(jnp.broadcast_to(energy[None], (SIDE // 2, SLICE, WIDTH)),...]
    all_to_all x4, waiting for transfers between devices: 12.4 us -> 7.61 us  [body(): cross = lax.all_to_all(keep + swap(give), 'z', 0, 0, tiled=True)]
    unnamed x4 -> x0, local copies, waits for them, and re-layouts: 4.37 us -> none
    ppermute x8, starting transfers between devices: 10.9 us -> 14.7 us  [swap(): return lax.ppermute(values, 'core', [(0, 1), (1, 0)])]
  transfers between devices with their start and end apart: 32 -> 32, of which waited for: 28 -> 28; matrix products, arithmetic and copies ran while one was open for 2% -> 2% of each run, Pallas kernels for 16% -> 13%
where the time goes in v4:
time: 320 us; the launch traced here: 318 us
  starting transfers between devices  135 us (42%)
  waiting for transfers between devices  120 us (38%)
  Pallas kernels  48.2 us (15%)
  local copies, waits for them, and re-layouts  6.41 us (2%)
  other arithmetic  6.36 us (2%)
    pallas_call x14, Pallas kernels, kernel_call(): pl.pallas_call(body, out_shape=outs, in_specs=[smem] * scalars + [vmem] *...  48.2 us
    ppermute x4, waiting for transfers between devices, to_line(): return lax.ppermute(piece, ALL, TO_LINE)  37.5 us
    ppermute x4, waiting for transfers between devices, to_plane(): return lax.ppermute(piece, ALL, TO_PLANE)  31.9 us
    all_to_all x4, starting transfers between devices, body(): pieces = lax.all_to_all(parts, ROW, 0, 0, tiled=True)  24.3 us
    ppermute x4, starting transfers between devices, to_plane(): return lax.ppermute(piece, ALL, TO_PLANE)  21.8 us
    all_to_all x3, starting transfers between devices, body(): full = lax.all_to_all(copies, ROW, 0, 0, tiled=True)  21.7 us
    all_to_all x4, starting transfers between devices, body(): cross = lax.all_to_all(keep + swap(give), 'z', 0, 0, tiled=True)  18.6 us
    all_to_all x4, starting transfers between devices, body(): lax.all_to_all(jnp.broadcast_to(energy[None], (SIDE // 2, SLICE, WIDTH)),...  17.8 us
  transfers between devices with their start and end apart: 32, of which 28 were waited for; matrix products, arithmetic and copies ran while one was open for 2% of the time, Pallas kernels for 13%

profile of v4, /device:TPU:1, one launch (start us, length us, event | category | flops | bytes accessed | tf_op | source)
XLA Modules:
  0.0 318.4 jit_solution(15270456613381234293)
XLA Ops:
  0.6 1.3 dynamic_slice.24
  4.7 6.2 %collective-permute-start = (f32[8,1024]{1,0:T(8,128)S(1)}, f32[8,1024]{1,0:T(8,128)S(1)}, u32[]{:S(2)}, u32[]{:S(2)}) collective-permute-start(f32[8,1024]{1,0:T(8,128)S(1)} %get-tuple-element.46), channel_id=1, source_target_pairs={{0,9},{16,7},{32,15},{48,10},{64,11},{80,4},{96,1},{112,5},{128,12... | collective-permute-start | bytes 98312 | tf_op jit(solution)/shard_map/ppermute | solution.py:280
  10.8 1.4 fusion.2
  13.5 5.9 %shard_map.95.history = bf16[12,1024,1024]{2,1,0:T(8,128)(2,1)} custom-call(f32[1024,1024]{1,0:T(8,128)} %corr.1, f32[1024,1024]{1,0:T(8,128)} %resp.1), custom_call_target="tpu_custom_call" | custom-call | flops 1048576 | bytes 8388608 | tf_op jit(solution)/shard_map/pallas_call | solution.py:64
  20.1 7.6 %all-to-all-start = ((f32[8,8,1024]{2,1,0:T(8,128)}), f32[8,8,1024]{2,1,0:T(8,128)S(1)}, u32[]{:S(2)}, u32[]{:S(2)}) async-start(f32[8,8,1024]{2,1,0:T(8,128)} %broadcast_in_dim.12), calls=%async_computation | async-start | bytes 524288 | tf_op jit(solution)/shard_map/all_to_all | solution.py:317
  28.4 3.6 %shard_map.97 = (f32[8,8,1152]{2,1,0:T(8,128)S(1)}, f32[8,8,1152]{2,1,0:T(8,128)S(1)}) custom-call(s32[16]{0:T(128)S(1)} %fusion.5.order_ref, f32[16,8,1152]{2,1,0:T(8,128)S(1)} %pad_maximum_fusion.full_ref, bf16[12,1024,1024]{2,1,0:T(8,128)(2,1)} %shard_map.95.history), custom_call_target="tpu_custom_call" | custom-call | flops 805306368 | bytes 25755712 | tf_op jit(solution)/shard_map/pallas_call | solution.py:64
  32.1 1.6 collective-permute-start.2
  33.6 1.2 collective-permute-done.2
  35.6 2.3 all-to-all-done.mine_ref
  37.9 4.7 %all-to-all-start.2 = ((f32[8,8,1152]{2,1,0:T(8,128)}), f32[8,8,1152]{2,1,0:T(8,128)S(1)}, u32[]{:S(2)}, u32[]{:S(2)}) async-start(f32[8,8,1152]{2,1,0:T(8,128)} %add.46), calls=%async_computation.2 | async-start | bytes 589824 | tf_op jit(solution)/shard_map/all_to_all | solution.py:324
  42.5 1.5 collective-permute-start.1
  45.2 5.5 %shard_map.96 = f32[16,8,2048]{2,1,0:T(8,128)} custom-call(s32[16]{0:T(128)S(1)} %fusion.4.order_ref, f32[8,8,1024]{2,1,0:T(8,128)S(1)} %all-to-all-done.mine_ref, f32[8,8,1024]{2,1,0:T(8,128)S(1)} %collective-permute-done.1.other_ref, bf16[12,1024,1024]{2,1,0:T(8,128)(2,1)} %shard_map.95.history), custom_call_target="tpu_custom_call" | custom-call | flops 1610612736 | bytes 25690176 | tf_op jit(solution)/shard_map/pallas_call | solution.py:64
  50.7 2.5 all-to-all-done.2
  53.2 7.8 %all-to-all-start.1 = ((f32[16,8,2048]{2,1,0:T(8,128)}), f32[16,8,2048]{2,1,0:T(8,128)S(1)}, u32[]{:S(2)}, u32[]{:S(2)}) async-start(f32[16,8,2048]{2,1,0:T(8,128)} %shard_map.96), calls=%async_computation.1 | async-start | bytes 2097152 | tf_op jit(solution)/shard_map/all_to_all | solution.py:327
  61.0 4.8 %collective-permute-start.3 = (f32[8,1152]{1,0:T(8,128)S(1)}, f32[8,1152]{1,0:T(8,128)S(1)}, u32[]{:S(2)}, u32[]{:S(2)}) collective-permute-start(f32[8,1152]{1,0:T(8,128)S(1)} %reduce_sum.46), channel_id=1, source_target_pairs={{9,0},{7,16},{15,32},{10,48},{11,64},{4,80},{1,96},{5,112},{12,128... | collective-permute-start | bytes 110600 | tf_op jit(solution)/shard_map/ppermute | solution.py:284
  65.8 9.9 %collective-permute-done.3.cross_ref = f32[8,1152]{1,0:T(8,128)S(1)} collective-permute-done((f32[8,1152]{1,0:T(8,128)S(1)}, f32[8,1152]{1,0:T(8,128)S(1)}, u32[]{:S(2)}, u32[]{:S(2)}) %collective-permute-start.3) | collective-permute-done | bytes 36896 | tf_op jit(solution)/shard_map/ppermute | solution.py:284
  75.6 1.6 all-to-all-done.1.pieces_ref
  78.3 7.2 %all-to-all-start.5 = ((f32[16,8,1152]{2,1,0:T(8,128)}), f32[16,8,1152]{2,1,0:T(8,128)S(1)}, u32[]{:S(2)}, u32[]{:S(2)}) async-start(f32[16,8,1152]{2,1,0:T(8,128)} %get-tuple-element.27), calls=%async_computation.5 | async-start | bytes 1179648 | tf_op jit(solution)/shard_map/all_to_all | solution.py:315
  85.6 12.2 %collective-permute-done.4 = f32[8,1024]{1,0:T(8,128)S(1)} collective-permute-done((f32[8,1024]{1,0:T(8,128)S(1)}, f32[8,1024]{1,0:T(8,128)S(1)}, u32[]{:S(2)}, u32[]{:S(2)}) %collective-permute-start.4) | collective-permute-done | bytes 32800 | tf_op jit(solution)/shard_map/ppermute | solution.py:280
  98.5 3.4 %all-to-all-start.3 = ((f32[8,8,1024]{2,1,0:T(8,128)}), f32[8,8,1024]{2,1,0:T(8,128)S(1)}, u32[]{:S(2)}, u32[]{:S(2)}) async-start(f32[8,8,1024]{2,1,0:T(8,128)} %broadcast_in_dim.15), calls=%async_computation.3 | async-start | bytes 524288 | tf_op jit(solution)/shard_map/all_to_all | solution.py:317
  102.0 3.7 %shard_map.100 = (f32[8,8,1152]{2,1,0:T(8,128)S(1)}, f32[8,8,1152]{2,1,0:T(8,128)S(1)}) custom-call(s32[16]{0:T(128)S(1)} %fusion.4.order_ref, f32[16,8,1152]{2,1,0:T(8,128)S(1)} %all-to-all-done.5.full_ref, bf16[12,1024,1024]{2,1,0:T(8,128)(2,1)} %shard_map.95.history), custom_call_target="tpu_custom_call" | custom-call | flops 805306368 | bytes 25755712 | tf_op jit(solution)/shard_map/pallas_call | solution.py:64
  105.6 2.2 collective-permute-start.6
  107.8 1.2 collective-permute-done.6
  109.8 1.4 all-to-all-done.3.mine_ref
  111.2 5.5 %all-to-all-start.6 = ((f32[8,8,1152]{2,1,0:T(8,128)}), f32[8,8,1152]{2,1,0:T(8,128)S(1)}, u32[]{:S(2)}, u32[]{:S(2)}) async-start(f32[8,8,1152]{2,1,0:T(8,128)} %add.47), calls=%async_computation.6 | async-start | bytes 589824 | tf_op jit(solution)/shard_map/all_to_all | solution.py:324
  116.6 1.8 collective-permute-start.5
  119.6 5.5 %shard_map.99 = f32[16,8,2048]{2,1,0:T(8,128)} custom-call(s32[16]{0:T(128)S(1)} %fusion.4.order_ref, f32[8,8,1024]{2,1,0:T(8,128)S(1)} %all-to-all-done.3.mine_ref, f32[8,8,1024]{2,1,0:T(8,128)S(1)} %collective-permute-done.5.other_ref, bf16[12,1024,1024]{2,1,0:T(8,128)(2,1)} %shard_map.95.history), custom_call_target="tpu_custom_call" | custom-call | flops 1610612736 | bytes 25690176 | tf_op jit(solution)/shard_map/pallas_call | solution.py:64
  125.0 2.3 all-to-all-done.6
  127.3 5.8 %all-to-all-start.4 = ((f32[16,8,2048]{2,1,0:T(8,128)}), f32[16,8,2048]{2,1,0:T(8,128)S(1)}, u32[]{:S(2)}, u32[]{:S(2)}) async-start(f32[16,8,2048]{2,1,0:T(8,128)} %shard_map.99), calls=%async_computation.4 | async-start | bytes 2097152 | tf_op jit(solution)/shard_map/all_to_all | solution.py:327
  133.2 5.2 %collective-permute-start.7 = (f32[8,1152]{1,0:T(8,128)S(1)}, f32[8,1152]{1,0:T(8,128)S(1)}, u32[]{:S(2)}, u32[]{:S(2)}) collective-permute-start(f32[8,1152]{1,0:T(8,128)S(1)} %reduce_sum.47), channel_id=1, source_target_pairs={{9,0},{7,16},{15,32},{10,48},{11,64},{4,80},{1,96},{5,112},{12,128... | collective-permute-start | bytes 110600 | tf_op jit(solution)/shard_map/ppermute | solution.py:284
  138.3 8.5 %collective-permute-done.7.cross_ref = f32[8,1152]{1,0:T(8,128)S(1)} collective-permute-done((f32[8,1152]{1,0:T(8,128)S(1)}, f32[8,1152]{1,0:T(8,128)S(1)}, u32[]{:S(2)}, u32[]{:S(2)}) %collective-permute-start.7) | collective-permute-done | bytes 36896 | tf_op jit(solution)/shard_map/ppermute | solution.py:284
  146.8 2.1 all-to-all-done.4.pieces_ref
  150.0 7.3 %all-to-all-start.9 = ((f32[16,8,1152]{2,1,0:T(8,128)}), f32[16,8,1152]{2,1,0:T(8,128)S(1)}, u32[]{:S(2)}, u32[]{:S(2)}) async-start(f32[16,8,1152]{2,1,0:T(8,128)} %get-tuple-element.33), calls=%async_computation.9 | async-start | bytes 1179648 | tf_op jit(solution)/shard_map/all_to_all | solution.py:315
  157.8 12.6 %collective-permute-done.8 = f32[8,1024]{1,0:T(8,128)S(1)} collective-permute-done((f32[8,1024]{1,0:T(8,128)S(1)}, f32[8,1024]{1,0:T(8,128)S(1)}, u32[]{:S(2)}, u32[]{:S(2)}) %collective-permute-start.8) | collective-permute-done | bytes 32800 | tf_op jit(solution)/shard_map/ppermute | solution.py:280
  171.2 3.4 %all-to-all-start.7 = ((f32[8,8,1024]{2,1,0:T(8,128)}), f32[8,8,1024]{2,1,0:T(8,128)S(1)}, u32[]{:S(2)}, u32[]{:S(2)}) async-start(f32[8,8,1024]{2,1,0:T(8,128)} %broadcast_in_dim.16), calls=%async_computation.7 | async-start | bytes 524288 | tf_op jit(solution)/shard_map/all_to_all | solution.py:317
  174.6 3.7 %shard_map.103 = (f32[8,8,1152]{2,1,0:T(8,128)S(1)}, f32[8,8,1152]{2,1,0:T(8,128)S(1)}) custom-call(s32[16]{0:T(128)S(1)} %fusion.4.order_ref, f32[16,8,1152]{2,1,0:T(8,128)S(1)} %all-to-all-done.9.full_ref, bf16[12,1024,1024]{2,1,0:T(8,128)(2,1)} %shard_map.95.history), custom_call_target="tpu_custom_call" | custom-call | flops 805306368 | bytes 25755712 | tf_op jit(solution)/shard_map/pallas_call | solution.py:64
  178.2 1.4 collective-permute-start.10
  179.6 1.2 collective-permute-done.10
  181.6 3.0 all-to-all-done.7.mine_ref
  184.6 3.8 %all-to-all-start.10 = ((f32[8,8,1152]{2,1,0:T(8,128)}), f32[8,8,1152]{2,1,0:T(8,128)S(1)}, u32[]{:S(2)}, u32[]{:S(2)}) async-start(f32[8,8,1152]{2,1,0:T(8,128)} %add.48), calls=%async_computation.10 | async-start | bytes 589824 | tf_op jit(solution)/shard_map/all_to_all | solution.py:324
  188.4 2.4 collective-permute-start.9
  192.0 5.5 %shard_map.102 = f32[16,8,2048]{2,1,0:T(8,128)} custom-call(s32[16]{0:T(128)S(1)} %fusion.4.order_ref, f32[8,8,1024]{2,1,0:T(8,128)S(1)} %all-to-all-done.7.mine_ref, f32[8,8,1024]{2,1,0:T(8,128)S(1)} %collective-permute-done.9.other_ref, bf16[12,1024,1024]{2,1,0:T(8,128)(2,1)} %shard_map.95.history), custom_call_target="tpu_custom_call" | custom-call | flops 1610612736 | bytes 25690176 | tf_op jit(solution)/shard_map/pallas_call | solution.py:64
  198.3 7.0 %all-to-all-start.8 = ((f32[16,8,2048]{2,1,0:T(8,128)}), f32[16,8,2048]{2,1,0:T(8,128)S(1)}, u32[]{:S(2)}, u32[]{:S(2)}) async-start(f32[16,8,2048]{2,1,0:T(8,128)} %shard_map.102), calls=%async_computation.8 | async-start | bytes 2097152 | tf_op jit(solution)/shard_map/all_to_all | solution.py:327
  205.3 4.9 %collective-permute-start.11 = (f32[8,1152]{1,0:T(8,128)S(1)}, f32[8,1152]{1,0:T(8,128)S(1)}, u32[]{:S(2)}, u32[]{:S(2)}) collective-permute-start(f32[8,1152]{1,0:T(8,128)S(1)} %reduce_sum.48), channel_id=1, source_target_pairs={{9,0},{7,16},{15,32},{10,48},{11,64},{4,80},{1,96},{5,112},{12,128... | collective-permute-start | bytes 110600 | tf_op jit(solution)/shard_map/ppermute | solution.py:284
  210.2 9.1 %collective-permute-done.11.cross_ref = f32[8,1152]{1,0:T(8,128)S(1)} collective-permute-done((f32[8,1152]{1,0:T(8,128)S(1)}, f32[8,1152]{1,0:T(8,128)S(1)}, u32[]{:S(2)}, u32[]{:S(2)}) %collective-permute-start.11) | collective-permute-done | bytes 36896 | tf_op jit(solution)/shard_map/ppermute | solution.py:284
  219.3 2.0 all-to-all-done.8.pieces_ref
  222.4 7.1 %all-to-all-start.13 = ((f32[16,8,1152]{2,1,0:T(8,128)}), f32[16,8,1152]{2,1,0:T(8,128)S(1)}, u32[]{:S(2)}, u32[]{:S(2)}) async-start(f32[16,8,1152]{2,1,0:T(8,128)} %get-tuple-element.39), calls=%async_computation.13 | async-start | bytes 1179648 | tf_op jit(solution)/shard_map/all_to_all | solution.py:315
  229.8 12.6 %collective-permute-done.12 = f32[8,1024]{1,0:T(8,128)S(1)} collective-permute-done((f32[8,1024]{1,0:T(8,128)S(1)}, f32[8,1024]{1,0:T(8,128)S(1)}, u32[]{:S(2)}, u32[]{:S(2)}) %collective-permute-start.12) | collective-permute-done | bytes 32800 | tf_op jit(solution)/shard_map/ppermute | solution.py:280
  243.1 3.4 %all-to-all-start.11 = ((f32[8,8,1024]{2,1,0:T(8,128)}), f32[8,8,1024]{2,1,0:T(8,128)S(1)}, u32[]{:S(2)}, u32[]{:S(2)}) async-start(f32[8,8,1024]{2,1,0:T(8,128)} %broadcast_in_dim.17), calls=%async_computation.11 | async-start | bytes 524288 | tf_op jit(solution)/shard_map/all_to_all | solution.py:317
  246.5 3.6 %shard_map.106 = (f32[8,8,1152]{2,1,0:T(8,128)S(1)}, f32[8,8,1152]{2,1,0:T(8,128)S(1)}) custom-call(s32[16]{0:T(128)S(1)} %fusion.4.order_ref, f32[16,8,1152]{2,1,0:T(8,128)S(1)} %all-to-all-done.13.full_ref, bf16[12,1024,1024]{2,1,0:T(8,128)(2,1)} %shard_map.95.history), custom_call_target="tpu_custom_call" | custom-call | flops 805306368 | bytes 25755712 | tf_op jit(solution)/shard_map/pallas_call | solution.py:64
  250.2 1.9 collective-permute-start.14
  252.1 1.2 collective-permute-done.14
  254.0 2.2 all-to-all-done.11.mine_ref
  256.2 4.7 %all-to-all-start.14 = ((f32[8,8,1152]{2,1,0:T(8,128)}), f32[8,8,1152]{2,1,0:T(8,128)S(1)}, u32[]{:S(2)}, u32[]{:S(2)}) async-start(f32[8,8,1152]{2,1,0:T(8,128)} %add.49), calls=%async_computation.14 | async-start | bytes 589824 | tf_op jit(solution)/shard_map/all_to_all | solution.py:324
  260.9 1.9 collective-permute-start.13
  263.9 5.5 %shard_map.105 = f32[16,8,2048]{2,1,0:T(8,128)} custom-call(s32[16]{0:T(128)S(1)} %fusion.4.order_ref, f32[8,8,1024]{2,1,0:T(8,128)S(1)} %all-to-all-done.11.mine_ref, f32[8,8,1024]{2,1,0:T(8,128)S(1)} %collective-permute-done.13.other_ref, bf16[12,1024,1024]{2,1,0:T(8,128)(2,1)} %shard_map.95.history), custom_call_target="tpu_custom_call" | custom-call | flops 1610612736 | bytes 25690176 | tf_op jit(solution)/shard_map/pallas_call | solution.py:64
  269.4 2.1 all-to-all-done.14
  271.4 3.7 %all-to-all-start.12 = ((f32[16,8,2048]{2,1,0:T(8,128)}), f32[16,8,2048]{2,1,0:T(8,128)S(1)}, u32[]{:S(2)}, u32[]{:S(2)}) async-start(f32[16,8,2048]{2,1,0:T(8,128)} %shard_map.105), calls=%async_computation.12 | async-start | bytes 2097152 | tf_op jit(solution)/shard_map/all_to_all | solution.py:327
  275.1 6.9 %collective-permute-start.15 = (f32[8,1152]{1,0:T(8,128)S(1)}, f32[8,1152]{1,0:T(8,128)S(1)}, u32[]{:S(2)}, u32[]{:S(2)}) collective-permute-start(f32[8,1152]{1,0:T(8,128)S(1)} %reduce_sum.49), channel_id=1, source_target_pairs={{9,0},{7,16},{15,32},{10,48},{11,64},{4,80},{1,96},{5,112},{12,128... | collective-permute-start | bytes 110600 | tf_op jit(solution)/shard_map/ppermute | solution.py:284
  282.0 4.5 %collective-permute-done.15.cross_ref = f32[8,1152]{1,0:T(8,128)S(1)} collective-permute-done((f32[8,1152]{1,0:T(8,128)S(1)}, f32[8,1152]{1,0:T(8,128)S(1)}, u32[]{:S(2)}, u32[]{:S(2)}) %collective-permute-start.15) | collective-permute-done | bytes 36896 | tf_op jit(solution)/shard_map/ppermute | solution.py:284
  286.5 2.9 all-to-all-done.12.pieces_ref
  290.6 8.7 %all-to-all-start.15 = ((f32[16,8,2048]{2,1,0:T(8,128)}), f32[16,8,2048]{2,1,0:T(8,128)S(1)}, u32[]{:S(2)}, u32[]{:S(2)}) async-start(f32[16,8,2048]{2,1,0:T(8,128)} %shard_map.107), calls=%async_computation.15 | async-start | bytes 2097152 | tf_op jit(solution)/shard_map/all_to_all | solution.py:338
  300.0 16.8 %all-to-all-done.15.pieces_ref = f32[16,8,2048]{2,1,0:T(8,128)S(1)} async-done(((f32[16,8,2048]{2,1,0:T(8,128)}), f32[16,8,2048]{2,1,0:T(8,128)S(1)}, u32[]{:S(2)}, u32[]{:S(2)}) %all-to-all-start.15) | async-done | bytes 1048608 | tf_op jit(solution)/shard_map/all_to_all | solution.py:338
  316.8 1.6 shard_map.108
  (35 shorter events, 20.0 us)
Async XLA Ops:
  4.7 14.8 %collective-permute-start = (f32[8,1024]{1,0:T(8,128)S(1)}, f32[8,1024]{1,0:T(8,128)S(1)}, u32[]{:S(2)}, u32[]{:S(2)}) collective-permute-start(f32[8,1024]{1,0:T(8,128)S(1)} %get-tuple-element.46), channel_id=1, source_target_pairs={{0,9},{16,7},{32,15},{48,10},{64,11},{80,4},{96,1},{112,5},{128,12... | collective-permute-start | bytes 98312 | tf_op jit(solution)/shard_map/ppermute | solution.py:280
  20.1 17.7 %all-to-all-start = ((f32[8,8,1024]{2,1,0:T(8,128)}), f32[8,8,1024]{2,1,0:T(8,128)S(1)}, u32[]{:S(2)}, u32[]{:S(2)}) async-start(f32[8,8,1024]{2,1,0:T(8,128)} %broadcast_in_dim.12), calls=%async_computation | async-start | bytes 524288 | tf_op jit(solution)/shard_map/all_to_all | solution.py:317
  32.1 2.8 collective-permute-start.2
  37.9 15.3 %all-to-all-start.2 = ((f32[8,8,1152]{2,1,0:T(8,128)}), f32[8,8,1152]{2,1,0:T(8,128)S(1)}, u32[]{:S(2)}, u32[]{:S(2)}) async-start(f32[8,8,1152]{2,1,0:T(8,128)} %add.46), calls=%async_computation.2 | async-start | bytes 589824 | tf_op jit(solution)/shard_map/all_to_all | solution.py:324
  42.5 2.7 collective-permute-start.1
  53.2 24.0 %all-to-all-start.1 = ((f32[16,8,2048]{2,1,0:T(8,128)}), f32[16,8,2048]{2,1,0:T(8,128)S(1)}, u32[]{:S(2)}, u32[]{:S(2)}) async-start(f32[16,8,2048]{2,1,0:T(8,128)} %shard_map.96), calls=%async_computation.1 | async-start | bytes 2097152 | tf_op jit(solution)/shard_map/all_to_all | solution.py:327
  61.0 14.6 %collective-permute-start.3 = (f32[8,1152]{1,0:T(8,128)S(1)}, f32[8,1152]{1,0:T(8,128)S(1)}, u32[]{:S(2)}, u32[]{:S(2)}) collective-permute-start(f32[8,1152]{1,0:T(8,128)S(1)} %reduce_sum.46), channel_id=1, source_target_pairs={{9,0},{7,16},{15,32},{10,48},{11,64},{4,80},{1,96},{5,112},{12,128... | collective-permute-start | bytes 110600 | tf_op jit(solution)/shard_map/ppermute | solution.py:284
  78.3 19.6 %all-to-all-start.5 = ((f32[16,8,1152]{2,1,0:T(8,128)}), f32[16,8,1152]{2,1,0:T(8,128)S(1)}, u32[]{:S(2)}, u32[]{:S(2)}) async-start(f32[16,8,1152]{2,1,0:T(8,128)} %get-tuple-element.27), calls=%async_computation.5 | async-start | bytes 1179648 | tf_op jit(solution)/shard_map/all_to_all | solution.py:315
  85.5 12.3 %collective-permute-start.4 = (f32[8,1024]{1,0:T(8,128)S(1)}, f32[8,1024]{1,0:T(8,128)S(1)}, u32[]{:S(2)}, u32[]{:S(2)}) collective-permute-start(f32[8,1024]{1,0:T(8,128)S(1)} %get-tuple-element.26), channel_id=1, source_target_pairs={{0,9},{16,7},{32,15},{48,10},{64,11},{80,4},{96,1},{112,5},{128,12... | collective-permute-start | bytes 98312 | tf_op jit(solution)/shard_map/ppermute | solution.py:280
  98.5 12.6 %all-to-all-start.3 = ((f32[8,8,1024]{2,1,0:T(8,128)}), f32[8,8,1024]{2,1,0:T(8,128)S(1)}, u32[]{:S(2)}, u32[]{:S(2)}) async-start(f32[8,8,1024]{2,1,0:T(8,128)} %broadcast_in_dim.15), calls=%async_computation.3 | async-start | bytes 524288 | tf_op jit(solution)/shard_map/all_to_all | solution.py:317
  105.6 3.4 %collective-permute-start.6 = (f32[8,8,1152]{2,1,0:T(8,128)S(1)}, f32[8,8,1152]{2,1,0:T(8,128)S(1)}, u32[]{:S(2)}, u32[]{:S(2)}) collective-permute-start(f32[8,8,1152]{2,1,0:T(8,128)S(1)} %get-tuple-element.29), channel_id=1, source_target_pairs={{0,1},{1,0},{2,3},{3,2},{4,5},{5,4},{6,7},{7,6},{8,9},{9,8},{10,11... | collective-permute-start | bytes 884744 | tf_op jit(solution)/shard_map/ppermute | solution.py:276
  111.2 16.1 %all-to-all-start.6 = ((f32[8,8,1152]{2,1,0:T(8,128)}), f32[8,8,1152]{2,1,0:T(8,128)S(1)}, u32[]{:S(2)}, u32[]{:S(2)}) async-start(f32[8,8,1152]{2,1,0:T(8,128)} %add.47), calls=%async_computation.6 | async-start | bytes 589824 | tf_op jit(solution)/shard_map/all_to_all | solution.py:324
  116.6 2.9 collective-permute-start.5
  127.3 21.7 %all-to-all-start.4 = ((f32[16,8,2048]{2,1,0:T(8,128)}), f32[16,8,2048]{2,1,0:T(8,128)S(1)}, u32[]{:S(2)}, u32[]{:S(2)}) async-start(f32[16,8,2048]{2,1,0:T(8,128)} %shard_map.99), calls=%async_computation.4 | async-start | bytes 2097152 | tf_op jit(solution)/shard_map/all_to_all | solution.py:327
  133.2 13.7 %collective-permute-start.7 = (f32[8,1152]{1,0:T(8,128)S(1)}, f32[8,1152]{1,0:T(8,128)S(1)}, u32[]{:S(2)}, u32[]{:S(2)}) collective-permute-start(f32[8,1152]{1,0:T(8,128)S(1)} %reduce_sum.47), channel_id=1, source_target_pairs={{9,0},{7,16},{15,32},{10,48},{11,64},{4,80},{1,96},{5,112},{12,128... | collective-permute-start | bytes 110600 | tf_op jit(solution)/shard_map/ppermute | solution.py:284
  150.0 20.4 %all-to-all-start.9 = ((f32[16,8,1152]{2,1,0:T(8,128)}), f32[16,8,1152]{2,1,0:T(8,128)S(1)}, u32[]{:S(2)}, u32[]{:S(2)}) async-start(f32[16,8,1152]{2,1,0:T(8,128)} %get-tuple-element.33), calls=%async_computation.9 | async-start | bytes 1179648 | tf_op jit(solution)/shard_map/all_to_all | solution.py:315
  157.4 13.1 %collective-permute-start.8 = (f32[8,1024]{1,0:T(8,128)S(1)}, f32[8,1024]{1,0:T(8,128)S(1)}, u32[]{:S(2)}, u32[]{:S(2)}) collective-permute-start(f32[8,1024]{1,0:T(8,128)S(1)} %get-tuple-element.32), channel_id=1, source_target_pairs={{0,9},{16,7},{32,15},{48,10},{64,11},{80,4},{96,1},{112,5},{128,12... | collective-permute-start | bytes 98312 | tf_op jit(solution)/shard_map/ppermute | solution.py:280
  171.2 13.4 %all-to-all-start.7 = ((f32[8,8,1024]{2,1,0:T(8,128)}), f32[8,8,1024]{2,1,0:T(8,128)S(1)}, u32[]{:S(2)}, u32[]{:S(2)}) async-start(f32[8,8,1024]{2,1,0:T(8,128)} %broadcast_in_dim.16), calls=%async_computation.7 | async-start | bytes 524288 | tf_op jit(solution)/shard_map/all_to_all | solution.py:317
  178.2 2.6 collective-permute-start.10
  184.6 13.7 %all-to-all-start.10 = ((f32[8,8,1152]{2,1,0:T(8,128)}), f32[8,8,1152]{2,1,0:T(8,128)S(1)}, u32[]{:S(2)}, u32[]{:S(2)}) async-start(f32[8,8,1152]{2,1,0:T(8,128)} %add.48), calls=%async_computation.10 | async-start | bytes 589824 | tf_op jit(solution)/shard_map/all_to_all | solution.py:324
  188.4 3.6 %collective-permute-start.9 = (f32[8,8,1024]{2,1,0:T(8,128)S(1)}, f32[8,8,1024]{2,1,0:T(8,128)S(1)}, u32[]{:S(2)}, u32[]{:S(2)}) collective-permute-start(f32[8,8,1024]{2,1,0:T(8,128)S(1)} %all-to-all-done.7.mine_ref), channel_id=1, source_target_pairs={{0,1},{1,0},{2,3},{3,2},{4,5},{5,4},{6,7},{7,6},{8,9},{9,8},{10,11... | collective-permute-start | bytes 786440 | tf_op jit(solution)/shard_map/ppermute | solution.py:276
  198.3 23.0 %all-to-all-start.8 = ((f32[16,8,2048]{2,1,0:T(8,128)}), f32[16,8,2048]{2,1,0:T(8,128)S(1)}, u32[]{:S(2)}, u32[]{:S(2)}) async-start(f32[16,8,2048]{2,1,0:T(8,128)} %shard_map.102), calls=%async_computation.8 | async-start | bytes 2097152 | tf_op jit(solution)/shard_map/all_to_all | solution.py:327
  205.3 14.0 %collective-permute-start.11 = (f32[8,1152]{1,0:T(8,128)S(1)}, f32[8,1152]{1,0:T(8,128)S(1)}, u32[]{:S(2)}, u32[]{:S(2)}) collective-permute-start(f32[8,1152]{1,0:T(8,128)S(1)} %reduce_sum.48), channel_id=1, source_target_pairs={{9,0},{7,16},{15,32},{10,48},{11,64},{4,80},{1,96},{5,112},{12,128... | collective-permute-start | bytes 110600 | tf_op jit(solution)/shard_map/ppermute | solution.py:284
  222.4 20.0 %all-to-all-start.13 = ((f32[16,8,1152]{2,1,0:T(8,128)}), f32[16,8,1152]{2,1,0:T(8,128)S(1)}, u32[]{:S(2)}, u32[]{:S(2)}) async-start(f32[16,8,1152]{2,1,0:T(8,128)} %get-tuple-element.39), calls=%async_computation.13 | async-start | bytes 1179648 | tf_op jit(solution)/shard_map/all_to_all | solution.py:315
  229.5 12.8 %collective-permute-start.12 = (f32[8,1024]{1,0:T(8,128)S(1)}, f32[8,1024]{1,0:T(8,128)S(1)}, u32[]{:S(2)}, u32[]{:S(2)}) collective-permute-start(f32[8,1024]{1,0:T(8,128)S(1)} %get-tuple-element.38), channel_id=1, source_target_pairs={{0,9},{16,7},{32,15},{48,10},{64,11},{80,4},{96,1},{112,5},{128,12... | collective-permute-start | bytes 98312 | tf_op jit(solution)/shard_map/ppermute | solution.py:280
  243.1 13.1 %all-to-all-start.11 = ((f32[8,8,1024]{2,1,0:T(8,128)}), f32[8,8,1024]{2,1,0:T(8,128)S(1)}, u32[]{:S(2)}, u32[]{:S(2)}) async-start(f32[8,8,1024]{2,1,0:T(8,128)} %broadcast_in_dim.17), calls=%async_computation.11 | async-start | bytes 524288 | tf_op jit(solution)/shard_map/all_to_all | solution.py:317
  250.2 3.1 collective-permute-start.14
  256.2 15.2 %all-to-all-start.14 = ((f32[8,8,1152]{2,1,0:T(8,128)}), f32[8,8,1152]{2,1,0:T(8,128)S(1)}, u32[]{:S(2)}, u32[]{:S(2)}) async-start(f32[8,8,1152]{2,1,0:T(8,128)} %add.49), calls=%async_computation.14 | async-start | bytes 589824 | tf_op jit(solution)/shard_map/all_to_all | solution.py:324
  260.9 3.1 collective-permute-start.13
  271.4 18.0 %all-to-all-start.12 = ((f32[16,8,2048]{2,1,0:T(8,128)}), f32[16,8,2048]{2,1,0:T(8,128)S(1)}, u32[]{:S(2)}, u32[]{:S(2)}) async-start(f32[16,8,2048]{2,1,0:T(8,128)} %shard_map.105), calls=%async_computation.12 | async-start | bytes 2097152 | tf_op jit(solution)/shard_map/all_to_all | solution.py:327
  275.1 11.4 %collective-permute-start.15 = (f32[8,1152]{1,0:T(8,128)S(1)}, f32[8,1152]{1,0:T(8,128)S(1)}, u32[]{:S(2)}, u32[]{:S(2)}) collective-permute-start(f32[8,1152]{1,0:T(8,128)S(1)} %reduce_sum.49), channel_id=1, source_target_pairs={{9,0},{7,16},{15,32},{10,48},{11,64},{4,80},{1,96},{5,112},{12,128... | collective-permute-start | bytes 110600 | tf_op jit(solution)/shard_map/ppermute | solution.py:284
  290.6 26.2 %all-to-all-start.15 = ((f32[16,8,2048]{2,1,0:T(8,128)}), f32[16,8,2048]{2,1,0:T(8,128)S(1)}, u32[]{:S(2)}, u32[]{:S(2)}) async-start(f32[16,8,2048]{2,1,0:T(8,128)} %shard_map.107), calls=%async_computation.15 | async-start | bytes 2097152 | tf_op jit(solution)/shard_map/all_to_all | solution.py:338

commit v5 on v4

--- a/solution.py
+++ b/solution.py
@@ -248,6 +248,17 @@
     )
 
 
+def first_kernel(place_ref, kept_ref, all_corr, all_resp, c_ref, r_ref, e_ref, full_ref):
+    kept = kept_ref[place_ref[0], place_ref[1]]
+    corr, resp = all_corr[kept], all_resp[kept]
+    c_ref[...] = corr
+    r_ref[...] = resp
+    e_ref[...], _ = energy_and_terms(corr, resp)
+    for j in range(SIDE):
+        full_ref[j, :, :WIDTH] = all_corr[j]
+        _, full_ref[j, :, WIDTH:] = energy_and_terms(all_corr[j], all_resp[j])
+
+
 def advance_kernel(pieces_ref, cross_ref, corr_ref, resp_ref, c_ref, r_ref, e_ref, copies_ref):
     corr, resp = advance(pieces_ref[...], cross_ref[...], corr_ref[...], resp_ref[...])
     c_ref[...] = corr
@@ -302,12 +313,14 @@
     order = mine_of(KEEPER_BY_CORE)
     row_corr = row_corr.reshape(SIDE, SLICE, WIDTH)
     row_resp = row_resp.reshape(SIDE, SLICE, WIDTH)
-    kept = lax.dynamic_index_in_dim(mine_of(KEPT), lax.axis_index(ROW), keepdims=False)
-    corr = lax.dynamic_index_in_dim(row_corr, kept, keepdims=False)
-    resp = lax.dynamic_index_in_dim(row_resp, kept, keepdims=False)
-    energy, _ = energy_and_terms(corr, resp)
-    _, terms = energy_and_terms(row_corr, row_resp)
-    full = jnp.concatenate([row_corr, terms], axis=2)
+    piece = shape(SLICE, WIDTH)
+    place = jnp.stack([col, lax.axis_index(ROW)])
+    corr, resp, energy, full = kernel_call(
+        first_kernel,
+        (piece, piece, piece, shape(SIDE, SLICE, WIDTH + LANES)),
+        (place, jnp.asarray(KEPT), row_corr, row_resp),
+        scalars=2,
+    )
     history = split_history(hist_corr, hist_resp)
     piece = shape(SLICE, WIDTH)
     for block_index in range(BLOCKS):

time: 320 us -> 317 us (level)
  other arithmetic: 6.36 us -> 3.14 us
    pallas_call x14 -> x15, Pallas kernels: 48.2 us -> 49 us  [kernel_call(): pl.pallas_call(body, out_shape=outs, in_specs=[smem] * scalars + [vmem] *...]
where the time goes in v5:
time: 317 us; the launch traced here: 315 us
  starting transfers between devices  134 us (42%)
  waiting for transfers between devices  120 us (38%)
  Pallas kernels  49 us (15%)
  local copies, waits for them, and re-layouts  7.74 us (2%)
    pallas_call x15, Pallas kernels, kernel_call(): pl.pallas_call(body, out_shape=outs, in_specs=[smem] * scalars + [vmem] *...  49 us
    ppermute x4, waiting for transfers between devices, to_line(): return lax.ppermute(piece, ALL, TO_LINE)  37.5 us
    ppermute x4, waiting for transfers between devices, to_plane(): return lax.ppermute(piece, ALL, TO_PLANE)  31.9 us
    all_to_all x4, starting transfers between devices, body(): pieces = lax.all_to_all(parts, ROW, 0, 0, tiled=True)  24.2 us
    ppermute x4, starting transfers between devices, to_plane(): return lax.ppermute(piece, ALL, TO_PLANE)  21.8 us
    all_to_all x3, starting transfers between devices, body(): full = lax.all_to_all(copies, ROW, 0, 0, tiled=True)  21.7 us
    all_to_all x4, starting transfers between devices, body(): cross = lax.all_to_all(keep + swap(give), 'z', 0, 0, tiled=True)  18.7 us
    all_to_all x4, starting transfers between devices, body(): lax.all_to_all(jnp.broadcast_to(energy[None], (SIDE // 2, SLICE, WIDTH)),...  17.8 us
  transfers between devices with their start and end apart: 32, of which 28 were waited for; matrix products, arithmetic and copies ran while one was open for 2% of the time, Pallas kernels for 13%

profile of v5, /device:TPU:1, one launch (start us, length us, event | category | flops | bytes accessed | tf_op | source)
XLA Modules:
  0.0 315.3 jit_solution(2913213571337007843)
XLA Ops:
  4.4 6.2 %collective-permute-start = (f32[8,1024]{1,0:T(8,128)S(1)}, f32[8,1024]{1,0:T(8,128)S(1)}, u32[]{:S(2)}, u32[]{:S(2)}) collective-permute-start(f32[8,1024]{1,0:T(8,128)S(1)} %get-tuple-element.28), channel_id=1, source_target_pairs={{0,9},{16,7},{32,15},{48,10},{64,11},{80,4},{96,1},{112,5},{128,12... | collective-permute-start | bytes 98312 | tf_op jit(solution)/shard_map/ppermute | solution.py:291
  10.5 5.8 %shard_map.96.history = bf16[12,1024,1024]{2,1,0:T(8,128)(2,1)} custom-call(f32[1024,1024]{1,0:T(8,128)} %corr.1, f32[1024,1024]{1,0:T(8,128)} %resp.1), custom_call_target="tpu_custom_call" | custom-call | flops 1048576 | bytes 8388608 | tf_op jit(solution)/shard_map/pallas_call | solution.py:64
  17.1 7.6 %all-to-all-start = ((f32[8,8,1024]{2,1,0:T(8,128)}), f32[8,8,1024]{2,1,0:T(8,128)S(1)}, u32[]{:S(2)}, u32[]{:S(2)}) async-start(f32[8,8,1024]{2,1,0:T(8,128)} %broadcast_in_dim.8), calls=%async_computation | async-start | bytes 524288 | tf_op jit(solution)/shard_map/all_to_all | solution.py:330
  25.4 3.7 %shard_map.98 = (f32[8,8,1152]{2,1,0:T(8,128)S(1)}, f32[8,8,1152]{2,1,0:T(8,128)S(1)}) custom-call(s32[16]{0:T(128)S(1)} %fusion.2.order_ref, f32[16,8,1152]{2,1,0:T(8,128)S(1)} %get-tuple-element.29.full_ref, bf16[12,1024,1024]{2,1,0:T(8,128)(2,1)} %shard_map.96.history), custom_call_target="tpu_custom_call" | custom-call | flops 805306368 | bytes 25755712 | tf_op jit(solution)/shard_map/pallas_call | solution.py:64
  29.0 1.6 collective-permute-start.2
  30.6 1.2 collective-permute-done.2
  32.6 2.3 all-to-all-done.mine_ref
  34.8 4.7 %all-to-all-start.2 = ((f32[8,8,1152]{2,1,0:T(8,128)}), f32[8,8,1152]{2,1,0:T(8,128)S(1)}, u32[]{:S(2)}, u32[]{:S(2)}) async-start(f32[8,8,1152]{2,1,0:T(8,128)} %add.27), calls=%async_computation.2 | async-start | bytes 589824 | tf_op jit(solution)/shard_map/all_to_all | solution.py:337
  39.5 1.5 collective-permute-start.1
  42.2 5.5 %shard_map.97 = f32[16,8,2048]{2,1,0:T(8,128)} custom-call(s32[16]{0:T(128)S(1)} %fusion.1.order_ref, f32[8,8,1024]{2,1,0:T(8,128)S(1)} %all-to-all-done.mine_ref, f32[8,8,1024]{2,1,0:T(8,128)S(1)} %collective-permute-done.1.other_ref, bf16[12,1024,1024]{2,1,0:T(8,128)(2,1)} %shard_map.96.history), custom_call_target="tpu_custom_call" | custom-call | flops 1610612736 | bytes 25690176 | tf_op jit(solution)/shard_map/pallas_call | solution.py:64
  47.7 2.5 all-to-all-done.2
  50.2 7.7 %all-to-all-start.1 = ((f32[16,8,2048]{2,1,0:T(8,128)}), f32[16,8,2048]{2,1,0:T(8,128)S(1)}, u32[]{:S(2)}, u32[]{:S(2)}) async-start(f32[16,8,2048]{2,1,0:T(8,128)} %shard_map.97), calls=%async_computation.1 | async-start | bytes 2097152 | tf_op jit(solution)/shard_map/all_to_all | solution.py:340
  58.0 4.8 %collective-permute-start.3 = (f32[8,1152]{1,0:T(8,128)S(1)}, f32[8,1152]{1,0:T(8,128)S(1)}, u32[]{:S(2)}, u32[]{:S(2)}) collective-permute-start(f32[8,1152]{1,0:T(8,128)S(1)} %reduce_sum.36), channel_id=1, source_target_pairs={{9,0},{7,16},{15,32},{10,48},{11,64},{4,80},{1,96},{5,112},{12,128... | collective-permute-start | bytes 110600 | tf_op jit(solution)/shard_map/ppermute | solution.py:295
  62.7 9.9 %collective-permute-done.3.cross_ref = f32[8,1152]{1,0:T(8,128)S(1)} collective-permute-done((f32[8,1152]{1,0:T(8,128)S(1)}, f32[8,1152]{1,0:T(8,128)S(1)}, u32[]{:S(2)}, u32[]{:S(2)}) %collective-permute-start.3) | collective-permute-done | bytes 36896 | tf_op jit(solution)/shard_map/ppermute | solution.py:295
  72.6 1.6 all-to-all-done.1.pieces_ref
  75.2 7.2 %all-to-all-start.5 = ((f32[16,8,1152]{2,1,0:T(8,128)}), f32[16,8,1152]{2,1,0:T(8,128)S(1)}, u32[]{:S(2)}, u32[]{:S(2)}) async-start(f32[16,8,1152]{2,1,0:T(8,128)} %get-tuple-element.35), calls=%async_computation.5 | async-start | bytes 1179648 | tf_op jit(solution)/shard_map/all_to_all | solution.py:328
  82.5 12.2 %collective-permute-done.4 = f32[8,1024]{1,0:T(8,128)S(1)} collective-permute-done((f32[8,1024]{1,0:T(8,128)S(1)}, f32[8,1024]{1,0:T(8,128)S(1)}, u32[]{:S(2)}, u32[]{:S(2)}) %collective-permute-start.4) | collective-permute-done | bytes 32800 | tf_op jit(solution)/shard_map/ppermute | solution.py:291
  95.5 3.4 %all-to-all-start.3 = ((f32[8,8,1024]{2,1,0:T(8,128)}), f32[8,8,1024]{2,1,0:T(8,128)S(1)}, u32[]{:S(2)}, u32[]{:S(2)}) async-start(f32[8,8,1024]{2,1,0:T(8,128)} %broadcast_in_dim.9), calls=%async_computation.3 | async-start | bytes 524288 | tf_op jit(solution)/shard_map/all_to_all | solution.py:330
  98.9 3.6 %shard_map.101 = (f32[8,8,1152]{2,1,0:T(8,128)S(1)}, f32[8,8,1152]{2,1,0:T(8,128)S(1)}) custom-call(s32[16]{0:T(128)S(1)} %fusion.1.order_ref, f32[16,8,1152]{2,1,0:T(8,128)S(1)} %all-to-all-done.5.full_ref, bf16[12,1024,1024]{2,1,0:T(8,128)(2,1)} %shard_map.96.history), custom_call_target="tpu_custom_call" | custom-call | flops 805306368 | bytes 25755712 | tf_op jit(solution)/shard_map/pallas_call | solution.py:64
  102.6 2.2 collective-permute-start.6
  104.8 1.2 collective-permute-done.6
  106.7 1.4 all-to-all-done.3.mine_ref
  108.1 5.5 %all-to-all-start.6 = ((f32[8,8,1152]{2,1,0:T(8,128)}), f32[8,8,1152]{2,1,0:T(8,128)S(1)}, u32[]{:S(2)}, u32[]{:S(2)}) async-start(f32[8,8,1152]{2,1,0:T(8,128)} %add.28), calls=%async_computation.6 | async-start | bytes 589824 | tf_op jit(solution)/shard_map/all_to_all | solution.py:337
  113.6 1.8 collective-permute-start.5
  115.4 1.2 collective-permute-done.5.other_ref
  116.5 5.5 %shard_map.100 = f32[16,8,2048]{2,1,0:T(8,128)} custom-call(s32[16]{0:T(128)S(1)} %fusion.1.order_ref, f32[8,8,1024]{2,1,0:T(8,128)S(1)} %all-to-all-done.3.mine_ref, f32[8,8,1024]{2,1,0:T(8,128)S(1)} %collective-permute-done.5.other_ref, bf16[12,1024,1024]{2,1,0:T(8,128)(2,1)} %shard_map.96.history), custom_call_target="tpu_custom_call" | custom-call | flops 1610612736 | bytes 25690176 | tf_op jit(solution)/shard_map/pallas_call | solution.py:64
  122.0 2.3 all-to-all-done.6
  124.2 5.8 %all-to-all-start.4 = ((f32[16,8,2048]{2,1,0:T(8,128)}), f32[16,8,2048]{2,1,0:T(8,128)S(1)}, u32[]{:S(2)}, u32[]{:S(2)}) async-start(f32[16,8,2048]{2,1,0:T(8,128)} %shard_map.100), calls=%async_computation.4 | async-start | bytes 2097152 | tf_op jit(solution)/shard_map/all_to_all | solution.py:340
  130.1 5.2 %collective-permute-start.7 = (f32[8,1152]{1,0:T(8,128)S(1)}, f32[8,1152]{1,0:T(8,128)S(1)}, u32[]{:S(2)}, u32[]{:S(2)}) collective-permute-start(f32[8,1152]{1,0:T(8,128)S(1)} %reduce_sum.37), channel_id=1, source_target_pairs={{9,0},{7,16},{15,32},{10,48},{11,64},{4,80},{1,96},{5,112},{12,128... | collective-permute-start | bytes 110600 | tf_op jit(solution)/shard_map/ppermute | solution.py:295
  135.3 8.5 %collective-permute-done.7.cross_ref = f32[8,1152]{1,0:T(8,128)S(1)} collective-permute-done((f32[8,1152]{1,0:T(8,128)S(1)}, f32[8,1152]{1,0:T(8,128)S(1)}, u32[]{:S(2)}, u32[]{:S(2)}) %collective-permute-start.7) | collective-permute-done | bytes 36896 | tf_op jit(solution)/shard_map/ppermute | solution.py:295
  143.8 2.1 all-to-all-done.4.pieces_ref
  146.9 7.3 %all-to-all-start.9 = ((f32[16,8,1152]{2,1,0:T(8,128)}), f32[16,8,1152]{2,1,0:T(8,128)S(1)}, u32[]{:S(2)}, u32[]{:S(2)}) async-start(f32[16,8,1152]{2,1,0:T(8,128)} %get-tuple-element.41), calls=%async_computation.9 | async-start | bytes 1179648 | tf_op jit(solution)/shard_map/all_to_all | solution.py:328
  154.8 12.6 %collective-permute-done.8 = f32[8,1024]{1,0:T(8,128)S(1)} collective-permute-done((f32[8,1024]{1,0:T(8,128)S(1)}, f32[8,1024]{1,0:T(8,128)S(1)}, u32[]{:S(2)}, u32[]{:S(2)}) %collective-permute-start.8) | collective-permute-done | bytes 32800 | tf_op jit(solution)/shard_map/ppermute | solution.py:291
  168.1 3.4 %all-to-all-start.7 = ((f32[8,8,1024]{2,1,0:T(8,128)}), f32[8,8,1024]{2,1,0:T(8,128)S(1)}, u32[]{:S(2)}, u32[]{:S(2)}) async-start(f32[8,8,1024]{2,1,0:T(8,128)} %broadcast_in_dim.10), calls=%async_computation.7 | async-start | bytes 524288 | tf_op jit(solution)/shard_map/all_to_all | solution.py:330
  171.5 3.7 %shard_map.104 = (f32[8,8,1152]{2,1,0:T(8,128)S(1)}, f32[8,8,1152]{2,1,0:T(8,128)S(1)}) custom-call(s32[16]{0:T(128)S(1)} %fusion.1.order_ref, f32[16,8,1152]{2,1,0:T(8,128)S(1)} %all-to-all-done.9.full_ref, bf16[12,1024,1024]{2,1,0:T(8,128)(2,1)} %shard_map.96.history), custom_call_target="tpu_custom_call" | custom-call | flops 805306368 | bytes 25755712 | tf_op jit(solution)/shard_map/pallas_call | solution.py:64
  175.2 1.4 collective-permute-start.10
  176.6 1.2 collective-permute-done.10
  178.5 3.0 all-to-all-done.7.mine_ref
  181.5 3.8 %all-to-all-start.10 = ((f32[8,8,1152]{2,1,0:T(8,128)}), f32[8,8,1152]{2,1,0:T(8,128)S(1)}, u32[]{:S(2)}, u32[]{:S(2)}) async-start(f32[8,8,1152]{2,1,0:T(8,128)} %add.29), calls=%async_computation.10 | async-start | bytes 589824 | tf_op jit(solution)/shard_map/all_to_all | solution.py:337
  185.4 2.4 collective-permute-start.9
  187.8 1.2 collective-permute-done.9.other_ref
  188.9 5.5 %shard_map.103 = f32[16,8,2048]{2,1,0:T(8,128)} custom-call(s32[16]{0:T(128)S(1)} %fusion.1.order_ref, f32[8,8,1024]{2,1,0:T(8,128)S(1)} %all-to-all-done.7.mine_ref, f32[8,8,1024]{2,1,0:T(8,128)S(1)} %collective-permute-done.9.other_ref, bf16[12,1024,1024]{2,1,0:T(8,128)(2,1)} %shard_map.96.history), custom_call_target="tpu_custom_call" | custom-call | flops 1610612736 | bytes 25690176 | tf_op jit(solution)/shard_map/pallas_call | solution.py:64
  195.2 7.0 %all-to-all-start.8 = ((f32[16,8,2048]{2,1,0:T(8,128)}), f32[16,8,2048]{2,1,0:T(8,128)S(1)}, u32[]{:S(2)}, u32[]{:S(2)}) async-start(f32[16,8,2048]{2,1,0:T(8,128)} %shard_map.103), calls=%async_computation.8 | async-start | bytes 2097152 | tf_op jit(solution)/shard_map/all_to_all | solution.py:340
  202.2 4.9 %collective-permute-start.11 = (f32[8,1152]{1,0:T(8,128)S(1)}, f32[8,1152]{1,0:T(8,128)S(1)}, u32[]{:S(2)}, u32[]{:S(2)}) collective-permute-start(f32[8,1152]{1,0:T(8,128)S(1)} %reduce_sum.38), channel_id=1, source_target_pairs={{9,0},{7,16},{15,32},{10,48},{11,64},{4,80},{1,96},{5,112},{12,128... | collective-permute-start | bytes 110600 | tf_op jit(solution)/shard_map/ppermute | solution.py:295
  207.2 9.1 %collective-permute-done.11.cross_ref = f32[8,1152]{1,0:T(8,128)S(1)} collective-permute-done((f32[8,1152]{1,0:T(8,128)S(1)}, f32[8,1152]{1,0:T(8,128)S(1)}, u32[]{:S(2)}, u32[]{:S(2)}) %collective-permute-start.11) | collective-permute-done | bytes 36896 | tf_op jit(solution)/shard_map/ppermute | solution.py:295
  216.3 2.0 all-to-all-done.8.pieces_ref
  219.3 7.1 %all-to-all-start.13 = ((f32[16,8,1152]{2,1,0:T(8,128)}), f32[16,8,1152]{2,1,0:T(8,128)S(1)}, u32[]{:S(2)}, u32[]{:S(2)}) async-start(f32[16,8,1152]{2,1,0:T(8,128)} %get-tuple-element.47), calls=%async_computation.13 | async-start | bytes 1179648 | tf_op jit(solution)/shard_map/all_to_all | solution.py:328
  226.7 12.6 %collective-permute-done.12 = f32[8,1024]{1,0:T(8,128)S(1)} collective-permute-done((f32[8,1024]{1,0:T(8,128)S(1)}, f32[8,1024]{1,0:T(8,128)S(1)}, u32[]{:S(2)}, u32[]{:S(2)}) %collective-permute-start.12) | collective-permute-done | bytes 32800 | tf_op jit(solution)/shard_map/ppermute | solution.py:291
  240.0 3.4 %all-to-all-start.11 = ((f32[8,8,1024]{2,1,0:T(8,128)}), f32[8,8,1024]{2,1,0:T(8,128)S(1)}, u32[]{:S(2)}, u32[]{:S(2)}) async-start(f32[8,8,1024]{2,1,0:T(8,128)} %broadcast_in_dim.11), calls=%async_computation.11 | async-start | bytes 524288 | tf_op jit(solution)/shard_map/all_to_all | solution.py:330
  243.4 3.7 %shard_map.107 = (f32[8,8,1152]{2,1,0:T(8,128)S(1)}, f32[8,8,1152]{2,1,0:T(8,128)S(1)}) custom-call(s32[16]{0:T(128)S(1)} %fusion.1.order_ref, f32[16,8,1152]{2,1,0:T(8,128)S(1)} %all-to-all-done.13.full_ref, bf16[12,1024,1024]{2,1,0:T(8,128)(2,1)} %shard_map.96.history), custom_call_target="tpu_custom_call" | custom-call | flops 805306368 | bytes 25755712 | tf_op jit(solution)/shard_map/pallas_call | solution.py:64
  247.1 1.9 collective-permute-start.14
  249.0 1.2 collective-permute-done.14
  250.9 2.2 all-to-all-done.11.mine_ref
  253.1 4.7 %all-to-all-start.14 = ((f32[8,8,1152]{2,1,0:T(8,128)}), f32[8,8,1152]{2,1,0:T(8,128)S(1)}, u32[]{:S(2)}, u32[]{:S(2)}) async-start(f32[8,8,1152]{2,1,0:T(8,128)} %add.30), calls=%async_computation.14 | async-start | bytes 589824 | tf_op jit(solution)/shard_map/all_to_all | solution.py:337
  257.8 1.9 collective-permute-start.13
  260.8 5.5 %shard_map.106 = f32[16,8,2048]{2,1,0:T(8,128)} custom-call(s32[16]{0:T(128)S(1)} %fusion.1.order_ref, f32[8,8,1024]{2,1,0:T(8,128)S(1)} %all-to-all-done.11.mine_ref, f32[8,8,1024]{2,1,0:T(8,128)S(1)} %collective-permute-done.13.other_ref, bf16[12,1024,1024]{2,1,0:T(8,128)(2,1)} %shard_map.96.history), custom_call_target="tpu_custom_call" | custom-call | flops 1610612736 | bytes 25690176 | tf_op jit(solution)/shard_map/pallas_call | solution.py:64
  266.3 2.0 all-to-all-done.14
  268.4 3.7 %all-to-all-start.12 = ((f32[16,8,2048]{2,1,0:T(8,128)}), f32[16,8,2048]{2,1,0:T(8,128)S(1)}, u32[]{:S(2)}, u32[]{:S(2)}) async-start(f32[16,8,2048]{2,1,0:T(8,128)} %shard_map.106), calls=%async_computation.12 | async-start | bytes 2097152 | tf_op jit(solution)/shard_map/all_to_all | solution.py:340
  272.0 6.9 %collective-permute-start.15 = (f32[8,1152]{1,0:T(8,128)S(1)}, f32[8,1152]{1,0:T(8,128)S(1)}, u32[]{:S(2)}, u32[]{:S(2)}) collective-permute-start(f32[8,1152]{1,0:T(8,128)S(1)} %reduce_sum.39), channel_id=1, source_target_pairs={{9,0},{7,16},{15,32},{10,48},{11,64},{4,80},{1,96},{5,112},{12,128... | collective-permute-start | bytes 110600 | tf_op jit(solution)/shard_map/ppermute | solution.py:295
  278.9 4.5 %collective-permute-done.15.cross_ref = f32[8,1152]{1,0:T(8,128)S(1)} collective-permute-done((f32[8,1152]{1,0:T(8,128)S(1)}, f32[8,1152]{1,0:T(8,128)S(1)}, u32[]{:S(2)}, u32[]{:S(2)}) %collective-permute-start.15) | collective-permute-done | bytes 36896 | tf_op jit(solution)/shard_map/ppermute | solution.py:295
  283.4 2.9 all-to-all-done.12.pieces_ref
  287.5 8.7 %all-to-all-start.15 = ((f32[16,8,2048]{2,1,0:T(8,128)}), f32[16,8,2048]{2,1,0:T(8,128)S(1)}, u32[]{:S(2)}, u32[]{:S(2)}) async-start(f32[16,8,2048]{2,1,0:T(8,128)} %shard_map.108), calls=%async_computation.15 | async-start | bytes 2097152 | tf_op jit(solution)/shard_map/all_to_all | solution.py:351
  296.9 16.8 %all-to-all-done.15.pieces_ref = f32[16,8,2048]{2,1,0:T(8,128)S(1)} async-done(((f32[16,8,2048]{2,1,0:T(8,128)}), f32[16,8,2048]{2,1,0:T(8,128)S(1)}, u32[]{:S(2)}, u32[]{:S(2)}) %all-to-all-start.15) | async-done | bytes 1048608 | tf_op jit(solution)/shard_map/all_to_all | solution.py:351
  313.7 1.6 shard_map.109
  (37 shorter events, 19.3 us)
Async XLA Ops:
  0.7 1.0 copy-start
  1.8 1.0 copy-start.1
  2.8 0.7 copy-start.2
  4.4 12.0 %collective-permute-start = (f32[8,1024]{1,0:T(8,128)S(1)}, f32[8,1024]{1,0:T(8,128)S(1)}, u32[]{:S(2)}, u32[]{:S(2)}) collective-permute-start(f32[8,1024]{1,0:T(8,128)S(1)} %get-tuple-element.28), channel_id=1, source_target_pairs={{0,9},{16,7},{32,15},{48,10},{64,11},{80,4},{96,1},{112,5},{128,12... | collective-permute-start | bytes 98312 | tf_op jit(solution)/shard_map/ppermute | solution.py:291
  17.1 17.7 %all-to-all-start = ((f32[8,8,1024]{2,1,0:T(8,128)}), f32[8,8,1024]{2,1,0:T(8,128)S(1)}, u32[]{:S(2)}, u32[]{:S(2)}) async-start(f32[8,8,1024]{2,1,0:T(8,128)} %broadcast_in_dim.8), calls=%async_computation | async-start | bytes 524288 | tf_op jit(solution)/shard_map/all_to_all | solution.py:330
  29.0 2.8 collective-permute-start.2
  34.8 15.4 %all-to-all-start.2 = ((f32[8,8,1152]{2,1,0:T(8,128)}), f32[8,8,1152]{2,1,0:T(8,128)S(1)}, u32[]{:S(2)}, u32[]{:S(2)}) async-start(f32[8,8,1152]{2,1,0:T(8,128)} %add.27), calls=%async_computation.2 | async-start | bytes 589824 | tf_op jit(solution)/shard_map/all_to_all | solution.py:337
  39.5 2.7 collective-permute-start.1
  50.2 24.0 %all-to-all-start.1 = ((f32[16,8,2048]{2,1,0:T(8,128)}), f32[16,8,2048]{2,1,0:T(8,128)S(1)}, u32[]{:S(2)}, u32[]{:S(2)}) async-start(f32[16,8,2048]{2,1,0:T(8,128)} %shard_map.97), calls=%async_computation.1 | async-start | bytes 2097152 | tf_op jit(solution)/shard_map/all_to_all | solution.py:340
  58.0 14.6 %collective-permute-start.3 = (f32[8,1152]{1,0:T(8,128)S(1)}, f32[8,1152]{1,0:T(8,128)S(1)}, u32[]{:S(2)}, u32[]{:S(2)}) collective-permute-start(f32[8,1152]{1,0:T(8,128)S(1)} %reduce_sum.36), channel_id=1, source_target_pairs={{9,0},{7,16},{15,32},{10,48},{11,64},{4,80},{1,96},{5,112},{12,128... | collective-permute-start | bytes 110600 | tf_op jit(solution)/shard_map/ppermute | solution.py:295
  75.2 19.6 %all-to-all-start.5 = ((f32[16,8,1152]{2,1,0:T(8,128)}), f32[16,8,1152]{2,1,0:T(8,128)S(1)}, u32[]{:S(2)}, u32[]{:S(2)}) async-start(f32[16,8,1152]{2,1,0:T(8,128)} %get-tuple-element.35), calls=%async_computation.5 | async-start | bytes 1179648 | tf_op jit(solution)/shard_map/all_to_all | solution.py:328
  82.4 12.3 %collective-permute-start.4 = (f32[8,1024]{1,0:T(8,128)S(1)}, f32[8,1024]{1,0:T(8,128)S(1)}, u32[]{:S(2)}, u32[]{:S(2)}) collective-permute-start(f32[8,1024]{1,0:T(8,128)S(1)} %get-tuple-element.34), channel_id=1, source_target_pairs={{0,9},{16,7},{32,15},{48,10},{64,11},{80,4},{96,1},{112,5},{128,12... | collective-permute-start | bytes 98312 | tf_op jit(solution)/shard_map/ppermute | solution.py:291
  95.5 12.6 %all-to-all-start.3 = ((f32[8,8,1024]{2,1,0:T(8,128)}), f32[8,8,1024]{2,1,0:T(8,128)S(1)}, u32[]{:S(2)}, u32[]{:S(2)}) async-start(f32[8,8,1024]{2,1,0:T(8,128)} %broadcast_in_dim.9), calls=%async_computation.3 | async-start | bytes 524288 | tf_op jit(solution)/shard_map/all_to_all | solution.py:330
  102.6 3.4 %collective-permute-start.6 = (f32[8,8,1152]{2,1,0:T(8,128)S(1)}, f32[8,8,1152]{2,1,0:T(8,128)S(1)}, u32[]{:S(2)}, u32[]{:S(2)}) collective-permute-start(f32[8,8,1152]{2,1,0:T(8,128)S(1)} %get-tuple-element.37), channel_id=1, source_target_pairs={{0,1},{1,0},{2,3},{3,2},{4,5},{5,4},{6,7},{7,6},{8,9},{9,8},{10,11... | collective-permute-start | bytes 884744 | tf_op jit(solution)/shard_map/ppermute | solution.py:287
  108.1 16.1 %all-to-all-start.6 = ((f32[8,8,1152]{2,1,0:T(8,128)}), f32[8,8,1152]{2,1,0:T(8,128)S(1)}, u32[]{:S(2)}, u32[]{:S(2)}) async-start(f32[8,8,1152]{2,1,0:T(8,128)} %add.28), calls=%async_computation.6 | async-start | bytes 589824 | tf_op jit(solution)/shard_map/all_to_all | solution.py:337
  113.6 2.9 collective-permute-start.5
  124.2 21.6 %all-to-all-start.4 = ((f32[16,8,2048]{2,1,0:T(8,128)}), f32[16,8,2048]{2,1,0:T(8,128)S(1)}, u32[]{:S(2)}, u32[]{:S(2)}) async-start(f32[16,8,2048]{2,1,0:T(8,128)} %shard_map.100), calls=%async_computation.4 | async-start | bytes 2097152 | tf_op jit(solution)/shard_map/all_to_all | solution.py:340
  130.1 13.7 %collective-permute-start.7 = (f32[8,1152]{1,0:T(8,128)S(1)}, f32[8,1152]{1,0:T(8,128)S(1)}, u32[]{:S(2)}, u32[]{:S(2)}) collective-permute-start(f32[8,1152]{1,0:T(8,128)S(1)} %reduce_sum.37), channel_id=1, source_target_pairs={{9,0},{7,16},{15,32},{10,48},{11,64},{4,80},{1,96},{5,112},{12,128... | collective-permute-start | bytes 110600 | tf_op jit(solution)/shard_map/ppermute | solution.py:295
  146.9 20.4 %all-to-all-start.9 = ((f32[16,8,1152]{2,1,0:T(8,128)}), f32[16,8,1152]{2,1,0:T(8,128)S(1)}, u32[]{:S(2)}, u32[]{:S(2)}) async-start(f32[16,8,1152]{2,1,0:T(8,128)} %get-tuple-element.41), calls=%async_computation.9 | async-start | bytes 1179648 | tf_op jit(solution)/shard_map/all_to_all | solution.py:328
  154.3 13.1 %collective-permute-start.8 = (f32[8,1024]{1,0:T(8,128)S(1)}, f32[8,1024]{1,0:T(8,128)S(1)}, u32[]{:S(2)}, u32[]{:S(2)}) collective-permute-start(f32[8,1024]{1,0:T(8,128)S(1)} %get-tuple-element.40), channel_id=1, source_target_pairs={{0,9},{16,7},{32,15},{48,10},{64,11},{80,4},{96,1},{112,5},{128,12... | collective-permute-start | bytes 98312 | tf_op jit(solution)/shard_map/ppermute | solution.py:291
  168.1 13.4 %all-to-all-start.7 = ((f32[8,8,1024]{2,1,0:T(8,128)}), f32[8,8,1024]{2,1,0:T(8,128)S(1)}, u32[]{:S(2)}, u32[]{:S(2)}) async-start(f32[8,8,1024]{2,1,0:T(8,128)} %broadcast_in_dim.10), calls=%async_computation.7 | async-start | bytes 524288 | tf_op jit(solution)/shard_map/all_to_all | solution.py:330
  175.2 2.6 collective-permute-start.10
  181.5 13.6 %all-to-all-start.10 = ((f32[8,8,1152]{2,1,0:T(8,128)}), f32[8,8,1152]{2,1,0:T(8,128)S(1)}, u32[]{:S(2)}, u32[]{:S(2)}) async-start(f32[8,8,1152]{2,1,0:T(8,128)} %add.29), calls=%async_computation.10 | async-start | bytes 589824 | tf_op jit(solution)/shard_map/all_to_all | solution.py:337
  185.4 3.6 %collective-permute-start.9 = (f32[8,8,1024]{2,1,0:T(8,128)S(1)}, f32[8,8,1024]{2,1,0:T(8,128)S(1)}, u32[]{:S(2)}, u32[]{:S(2)}) collective-permute-start(f32[8,8,1024]{2,1,0:T(8,128)S(1)} %all-to-all-done.7.mine_ref), channel_id=1, source_target_pairs={{0,1},{1,0},{2,3},{3,2},{4,5},{5,4},{6,7},{7,6},{8,9},{9,8},{10,11... | collective-permute-start | bytes 786440 | tf_op jit(solution)/shard_map/ppermute | solution.py:287
  195.2 23.1 %all-to-all-start.8 = ((f32[16,8,2048]{2,1,0:T(8,128)}), f32[16,8,2048]{2,1,0:T(8,128)S(1)}, u32[]{:S(2)}, u32[]{:S(2)}) async-start(f32[16,8,2048]{2,1,0:T(8,128)} %shard_map.103), calls=%async_computation.8 | async-start | bytes 2097152 | tf_op jit(solution)/shard_map/all_to_all | solution.py:340
  202.2 14.0 %collective-permute-start.11 = (f32[8,1152]{1,0:T(8,128)S(1)}, f32[8,1152]{1,0:T(8,128)S(1)}, u32[]{:S(2)}, u32[]{:S(2)}) collective-permute-start(f32[8,1152]{1,0:T(8,128)S(1)} %reduce_sum.38), channel_id=1, source_target_pairs={{9,0},{7,16},{15,32},{10,48},{11,64},{4,80},{1,96},{5,112},{12,128... | collective-permute-start | bytes 110600 | tf_op jit(solution)/shard_map/ppermute | solution.py:295
  219.3 20.0 %all-to-all-start.13 = ((f32[16,8,1152]{2,1,0:T(8,128)}), f32[16,8,1152]{2,1,0:T(8,128)S(1)}, u32[]{:S(2)}, u32[]{:S(2)}) async-start(f32[16,8,1152]{2,1,0:T(8,128)} %get-tuple-element.47), calls=%async_computation.13 | async-start | bytes 1179648 | tf_op jit(solution)/shard_map/all_to_all | solution.py:328
  226.4 12.8 %collective-permute-start.12 = (f32[8,1024]{1,0:T(8,128)S(1)}, f32[8,1024]{1,0:T(8,128)S(1)}, u32[]{:S(2)}, u32[]{:S(2)}) collective-permute-start(f32[8,1024]{1,0:T(8,128)S(1)} %get-tuple-element.46), channel_id=1, source_target_pairs={{0,9},{16,7},{32,15},{48,10},{64,11},{80,4},{96,1},{112,5},{128,12... | collective-permute-start | bytes 98312 | tf_op jit(solution)/shard_map/ppermute | solution.py:291
  240.0 13.1 %all-to-all-start.11 = ((f32[8,8,1024]{2,1,0:T(8,128)}), f32[8,8,1024]{2,1,0:T(8,128)S(1)}, u32[]{:S(2)}, u32[]{:S(2)}) async-start(f32[8,8,1024]{2,1,0:T(8,128)} %broadcast_in_dim.11), calls=%async_computation.11 | async-start | bytes 524288 | tf_op jit(solution)/shard_map/all_to_all | solution.py:330
  247.1 3.1 collective-permute-start.14
  253.1 15.2 %all-to-all-start.14 = ((f32[8,8,1152]{2,1,0:T(8,128)}), f32[8,8,1152]{2,1,0:T(8,128)S(1)}, u32[]{:S(2)}, u32[]{:S(2)}) async-start(f32[8,8,1152]{2,1,0:T(8,128)} %add.30), calls=%async_computation.14 | async-start | bytes 589824 | tf_op jit(solution)/shard_map/all_to_all | solution.py:337
  257.8 3.1 collective-permute-start.13
  268.4 18.0 %all-to-all-start.12 = ((f32[16,8,2048]{2,1,0:T(8,128)}), f32[16,8,2048]{2,1,0:T(8,128)S(1)}, u32[]{:S(2)}, u32[]{:S(2)}) async-start(f32[16,8,2048]{2,1,0:T(8,128)} %shard_map.106), calls=%async_computation.12 | async-start | bytes 2097152 | tf_op jit(solution)/shard_map/all_to_all | solution.py:340
  272.0 11.4 %collective-permute-start.15 = (f32[8,1152]{1,0:T(8,128)S(1)}, f32[8,1152]{1,0:T(8,128)S(1)}, u32[]{:S(2)}, u32[]{:S(2)}) collective-permute-start(f32[8,1152]{1,0:T(8,128)S(1)} %reduce_sum.39), channel_id=1, source_target_pairs={{9,0},{7,16},{15,32},{10,48},{11,64},{4,80},{1,96},{5,112},{12,128... | collective-permute-start | bytes 110600 | tf_op jit(solution)/shard_map/ppermute | solution.py:295
  287.5 26.2 %all-to-all-start.15 = ((f32[16,8,2048]{2,1,0:T(8,128)}), f32[16,8,2048]{2,1,0:T(8,128)S(1)}, u32[]{:S(2)}, u32[]{:S(2)}) async-start(f32[16,8,2048]{2,1,0:T(8,128)} %shard_map.108), calls=%async_computation.15 | async-start | bytes 2097152 | tf_op jit(solution)/shard_map/all_to_all | solution.py:351
